TPU v7x, 32 devices: a whole 2x2x4 slice. The times are simulated.
32 devices in a mesh: seq: 16 (over z, y, core), tp: 2 (over x).
Axes of the slice: x: 2, y: 2, z: 4, core: 2. Of those that a mesh axis runs over, the one named last changes fastest.
Arguments:
- frames_in: bfloat16 [1536, 8192], P('tp', 'seq'), may hold values from -30 to 30
- norm_gain: float32 [1536], P('tp'), may hold values from 0.5 to 2
- value_weight: bfloat16 [1536, 1536], P('tp'), may hold values from -0.15625 to 0.15625
- gate_weight: bfloat16 [1536, 1536], P('tp'), may hold values from -0.15625 to 0.15625
- depth_kernel: float32 [1536, 32], P('tp'), may hold values from -6 to 6
- conv_gain: float32 [1536], P('tp'), may hold values from 0.5 to 2
- out_weight: bfloat16 [1536, 1536], P('tp'), may hold values from -0.15625 to 0.15625
- cotangent: bfloat16 [1536, 8192], P('tp', 'seq'), may hold values from -15 to 15
Outputs:
- block_out: bfloat16 [1536, 8192], P('tp', 'seq')
- input_grad: bfloat16 [1536, 8192], P('tp', 'seq')
- grad_norm_gain: float32 [1536], P('tp')
- grad_value: bfloat16 [1536, 1536], P('tp')
- grad_gate: bfloat16 [1536, 1536], P('tp')
- grad_kernel: float32 [1536, 32], P('tp')
- grad_conv_gain: float32 [1536], P('tp')
- grad_out: bfloat16 [1536, 1536], P('tp')
All inputs are finite; a program needn't handle non-finite values.
Results may differ from a plain program's by a relative error of at most 0.027.
Values may be sent and summed in bfloat16 or wider, within the bound.
No kernel may reach another device: no remote copies, remote signals or barrier semaphores. Data moves between devices by JAX's collectives and lax.ppermute only.
A program may use at most 64 MiB of HBM per device.

v0:
```python
import jax
import jax.numpy as jnp
from jax import lax
from jax.sharding import PartitionSpec as P

EPS = 1e-05


def with_halo(cells, sides, width):
    for axis, dim in sides:
        count = lax.axis_size(axis)
        ends = count - 1
        head = lax.slice_in_dim(cells, 0, width, axis=dim)
        tail = lax.slice_in_dim(cells, cells.shape[dim] - width, cells.shape[dim], axis=dim)
        cells = jnp.concatenate(
            [
                lax.ppermute(tail, axis, [(i, (i + 1) % count) for i in range(ends)]),
                cells,
                lax.ppermute(head, axis, [((i + 1) % count, i) for i in range(ends)]),
            ],
            axis=dim,
        )
    return cells


def widen(values):
    return lax.optimization_barrier(values).astype(jnp.float32)


def row_sums(values):
    return lax.psum(values, "tp")


def split_norm(values, width):
    mean = row_sums(jnp.sum(values, axis=0, keepdims=True)) / width
    centred = values - mean
    spread = row_sums(jnp.sum(centred * centred, axis=0, keepdims=True)) / width
    inverse = lax.rsqrt(spread + EPS)
    return (centred * inverse, inverse)


def split_norm_back(d_hat, hat, inverse, width):
    first, second = row_sums(
        (jnp.sum(d_hat, axis=0, keepdims=True), jnp.sum(d_hat * hat, axis=0, keepdims=True))
    )
    return (d_hat - first / width - hat * (second / width)) * inverse


def spread_channels(values):
    return lax.all_gather(values, "tp", axis=0, tiled=True)


def frame_rims(values, reach):
    return with_halo(values, (("seq", 1),), reach)


def reduce_inputs(term):
    rounded = widen(term.astype(jnp.bfloat16))
    return lax.psum_scatter(
        rounded.astype(jnp.bfloat16), "tp", scatter_dimension=0, tiled=True
    ).astype(jnp.float32)


def contract_rows(left, right):
    return lax.dot_general(
        left, right, (((0,), (0,)), ((), ())), preferred_element_type=jnp.float32
    )


def contract_cols(left, right):
    return lax.dot_general(
        left, right, (((1,), (1,)), ((), ())), preferred_element_type=jnp.float32
    )


def local(
    frames_in, norm_gain, value_weight, gate_weight, depth_kernel, conv_gain, out_weight, cotangent
):
    chans, row_count = frames_in.shape
    parts = lax.axis_size("tp")
    width = chans * parts
    taps = depth_kernel.shape[1]
    reach = taps // 2
    scale = float(row_count * lax.axis_size("seq")) ** (-0.5)
    inputs = frames_in.astype(jnp.float32)
    hat_in, inverse_in = split_norm(inputs, width)
    normed = (hat_in * norm_gain[:, None]).astype(jnp.bfloat16)
    normed_all = spread_channels(normed)
    value = jnp.dot(value_weight, normed_all, preferred_element_type=jnp.float32)
    gate = jnp.dot(gate_weight, normed_all, preferred_element_type=jnp.float32)
    gate_sig = jax.nn.sigmoid(gate)
    glu = (value * gate_sig).astype(jnp.bfloat16)
    glu_wide = widen(frame_rims(glu, reach))
    conv = jnp.zeros((chans, row_count), jnp.float32)
    for tap in range(taps):
        conv = conv + depth_kernel[:, tap : tap + 1] * glu_wide[:, tap : tap + row_count]
    hat_conv, inverse_conv = split_norm(conv, width)
    scaled = hat_conv * conv_gain[:, None]
    swish_sig = jax.nn.sigmoid(scaled)
    act = (scaled * swish_sig).astype(jnp.bfloat16)
    act_all = spread_channels(act)
    block_out = (inputs + jnp.dot(out_weight, act_all, preferred_element_type=jnp.float32)).astype(
        jnp.bfloat16
    )
    grad_out = contract_cols(cotangent, act_all) * scale
    d_act = reduce_inputs(contract_rows(out_weight, cotangent))
    d_scaled = d_act * (swish_sig + scaled * swish_sig * (1.0 - swish_sig))
    grad_conv_gain = jnp.sum(d_scaled * hat_conv, axis=1) * scale
    d_conv = split_norm_back(d_scaled * conv_gain[:, None], hat_conv, inverse_conv, width).astype(
        jnp.bfloat16
    )
    d_conv_f = widen(d_conv)
    d_conv_wide = widen(frame_rims(d_conv, reach))
    d_glu = jnp.zeros((chans, row_count), jnp.float32)
    kernel_cols = []
    for tap in range(taps):
        start = 2 * reach - tap
        d_glu = d_glu + depth_kernel[:, tap : tap + 1] * d_conv_wide[:, start : start + row_count]
        kernel_cols.append(jnp.sum(glu_wide[:, tap : tap + row_count] * d_conv_f, axis=1))
    grad_kernel = jnp.stack(kernel_cols, axis=1) * scale
    d_value = (d_glu * gate_sig).astype(jnp.bfloat16)
    d_gate = (d_glu * value * gate_sig * (1.0 - gate_sig)).astype(jnp.bfloat16)
    grad_value = contract_cols(d_value, normed_all) * scale
    grad_gate = contract_cols(d_gate, normed_all) * scale
    d_normed = reduce_inputs(
        contract_rows(value_weight, d_value) + contract_rows(gate_weight, d_gate)
    )
    grad_norm_gain = jnp.sum(d_normed * hat_in, axis=1) * scale
    input_grad = (
        cotangent.astype(jnp.float32)
        + split_norm_back(d_normed * norm_gain[:, None], hat_in, inverse_in, width)
    ).astype(jnp.bfloat16)
    grad_out, grad_kernel, grad_conv_gain, grad_value, grad_gate, grad_norm_gain = lax.psum(
        (grad_out, grad_kernel, grad_conv_gain, grad_value, grad_gate, grad_norm_gain), "seq"
    )
    return (
        block_out,
        input_grad,
        grad_norm_gain,
        grad_value.astype(jnp.bfloat16),
        grad_gate.astype(jnp.bfloat16),
        grad_kernel,
        grad_conv_gain,
        grad_out.astype(jnp.bfloat16),
    )


def solution(mesh):
    return jax.shard_map(
        local,
        mesh=mesh,
        in_specs=(
            P("tp", "seq"),
            P("tp"),
            P("tp", None),
            P("tp", None),
            P("tp", None),
            P("tp"),
            P("tp", None),
            P("tp", "seq"),
        ),
        out_specs=(
            P("tp", "seq"),
            P("tp", "seq"),
            P("tp"),
            P("tp", None),
            P("tp", None),
            P("tp", None),
            P("tp"),
            P("tp", None),
        ),
        check_vma=False,
    )
```

profile of v0, /device:TPU:0, one launch (start us, length us, event | category | flops | bytes accessed | tf_op | source)
XLA Modules:
  0.0 489.3 jit_solution(3199493002796039852)
XLA Ops:
  9.0 5.8 %psum.98 = f32[1,512]{1,0:T(1,128)S(1)} all-reduce(f32[1,512]{1,0:T(1,128)S(1)} %bitcast.79), channel_id=1, replica_groups=mesh['seq'=16,'tp'=2] {'tp'}, use_global_device_ids=true, to_apply=%region_1.0 | all-reduce | flops 512 | bytes 4096 | tf_op jit(solution)/shard_map/psum | solution.py:31
  15.2 4.9 %psum.99 = f32[1,512]{1,0:T(1,128)S(1)} all-reduce(f32[1,512]{1,0:T(1,128)S(1)} %bitcast.80), channel_id=1, replica_groups=mesh['seq'=16,'tp'=2] {'tp'}, use_global_device_ids=true, to_apply=%region_3.0 | all-reduce | flops 512 | bytes 4096 | tf_op jit(solution)/shard_map/psum | solution.py:31
  21.4 4.4 convolution_convert_fusion
  26.9 23.6 %all-gather.3.cloned.1.call-done = bf16[1536,512]{0,1:T(8,128)(2,1)} async-done(((bf16[768,512]{0,1:T(8,128)(2,1)}), bf16[1536,512]{0,1:T(8,128)(2,1)}) %all-gather.3.cloned.1.call-update) | async-done | bytes 1572880 | tf_op jit(solution)/shard_map/all_gather | solution.py:50
  50.5 3.7 fusion.90
  60.1 2.9 collective-permute-done.1
  63.2 8.9 %fusion.87 = (f32[512]{0:T(512)S(1)}, f32[768,512]{0,1:T(8,128)}) fusion(f32[768,544]{0,1:T(8,128)S(1)} %convert_element_type.70, f32[768]{0:T(1024)S(1)} %get-tuple-element.84, f32[768]{0:T(1024)S(1)} %get-tuple-element.85, f32[768]{0:T(1024)S(1)} %get-tuple-element.55, f32[768]{0:T(1024)S(1)} %get-tuple-element.56, f32[768]{0:T(1024)S(1)} %get-tuple-element.57, ...), kind=kLoop, calls=%fused_computation.221 | loop fusion | flops 25165312 | bytes 52004864 | tf_op jit(solution)/shard_map/reduce_sum | solution.py:35
  72.1 5.1 %psum.100 = f32[1,512]{1,0:T(1,128)S(1)} all-reduce(f32[1,512]{1,0:T(1,128)S(1)} %bitcast.78), channel_id=1, replica_groups=mesh['seq'=16,'tp'=2] {'tp'}, use_global_device_ids=true, to_apply=%region_5.0 | all-reduce | flops 512 | bytes 4096 | tf_op jit(solution)/shard_map/psum | solution.py:31
  78.9 4.9 %psum.101 = f32[1,512]{1,0:T(1,128)S(1)} all-reduce(f32[1,512]{1,0:T(1,128)S(1)} %bitcast.81), channel_id=1, replica_groups=mesh['seq'=16,'tp'=2] {'tp'}, use_global_device_ids=true, to_apply=%region_7.0 | all-reduce | flops 512 | bytes 4096 | tf_op jit(solution)/shard_map/psum | solution.py:31
  83.9 3.8 multiply_reduce_fusion
  87.8 4.9 %all-reduce.2 = (f32[1,512]{1,0:T(1,128)S(1)}, f32[1,512]{1,0:T(1,128)S(1)}) all-reduce(f32[1,512]{1,0:T(1,128)S(1)} %bitcast.73, f32[1,512]{1,0:T(1,128)S(1)} %bitcast.74), channel_id=1, replica_groups=mesh['seq'=16,'tp'=2] {'tp'}, use_global_device_ids=true, to_apply=%region_12.0 | all-reduce | flops 1024 | bytes 8192 | tf_op jit(solution)/shard_map/psum | solution.py:31
  92.7 3.6 multiply_convert_fusion
  100.1 4.1 collective-permute-done.3
  107.0 6.6 %fusion.84 = (bf16[768,512]{0,1:T(8,128)(2,1)S(1)}, f32[768,512]{0,1:T(8,128)S(1)}) fusion(f32[512,768]{1,0:T(8,128)S(1)} %copy-done.7, f32[512,768]{1,0:T(8,128)S(1)} %copy-done.12, f32[768,544]{0,1:T(8,128)S(1)} %convert_element_type.77, f32[768]{0:T(1024)S(1)} %get-tuple-element.84, f32[768]{0:T(1024)S(1)} %get-tuple-element.85, ...), kind=kLoop, calls=%fused_computation.162 | loop fusion | flops 26738688 | bytes 55934976 | tf_op jit(solution)/shard_map/convert_element_type | solution.py:122
  121.9 14.7 %fusion.49 = (f32[768]{0:T(1024)S(1)}, f32[768]{0:T(1024)S(1)}, f32[768]{0:T(1024)S(1)}, f32[768]{0:T(1024)S(1)}, f32[768]{0:T(1024)S(1)}, /*index=5*/f32[768]{0...) fusion(bf16[768,512]{0,1:T(8,128)(2,1)} %copy-done.3, ...), kind=kLoop, calls=%fused_computation.91 | loop fusion | flops 14535168 | bytes 29153280 | tf_op jit(solution)/shard_map/reduce_sum | solution.py:119
  136.6 2.8 fusion.48
  140.7 5.4 %convolution_multiply_fusion = f32[768,1536]{1,0:T(8,128)} fusion(bf16[768,512]{0,1:T(8,128)(2,1)} %copy-done.10, bf16[1536,512]{0,1:T(8,128)(2,1)} %all-gather.3.cloned.1.call-done), kind=kOutput, calls=%fused_computation.33 | convolution fusion | flops 1209139200 | bytes 7077888 | tf_op jit(solution)/shard_map/dot_general | solution.py:71
  146.1 3.6 convolution_multiply_fusion.1
  149.6 4.4 fusion.17
  156.4 5.3 %multiply_bitcast_fusion = f32[768,1536]{0,1:T(8,128)} fusion(bf16[1536,512]{0,1:T(8,128)(2,1)} %all-gather.5.cloned.1.call-done, bf16[768,512]{1,0:T(8,128)(2,1)} %param.15), kind=kOutput, calls=%fused_computation.32 | convolution fusion | flops 1209139200 | bytes 7077888 | tf_op jit(solution)/shard_map/dot_general | solution.py:71
  163.7 4.9 %all-reduce.1 = (f32[1,512]{1,0:T(1,128)S(1)}, f32[1,512]{1,0:T(1,128)S(1)}) all-reduce(f32[1,512]{1,0:T(1,128)S(1)} %bitcast.76, f32[1,512]{1,0:T(1,128)S(1)} %bitcast.77), channel_id=1, replica_groups=mesh['seq'=16,'tp'=2] {'tp'}, use_global_device_ids=true, to_apply=%region_17.0 | all-reduce | flops 1024 | bytes 8192 | tf_op jit(solution)/shard_map/psum | solution.py:31
  168.6 2.9 fusion.13
  173.8 303.2 %all-reduce.7 = (f32[768]{0:T(1024)}, bf16[768,1536]{1,0:T(8,128)(2,1)}, bf16[768,1536]{1,0:T(8,128)(2,1)}, f32[768]{0:T(1024)}, bf16[768,1536]{0,1:T(8,128)(2,1)}) all-reduce(f32[768]{0:T(1024)S(1)} %broadcast_multiply_fusion.2, f32[768,1536]{1,0:T(8,128)} %convolution_multiply_fusion.1, ...), channel_id=1, replica_groups=mesh['seq'=16,'tp'=2] {'seq'}, use_global_device_ids=true, to_apply=%region_19.0 | all-reduce | flops 3540480 | bytes 21245952 | tf_op jit(solution)/shard_map/psum | solution.py:133
  477.0 4.3 copy.21
  (119 shorter events, 36.1 us)
Async XLA Ops:
  7.2 47.0 %copy-start = (bf16[768,1536]{1,0:T(8,128)(2,1)S(1)}, bf16[768,1536]{1,0:T(8,128)(2,1)}, u32[]{:S(2)}) copy-start(bf16[768,1536]{1,0:T(8,128)(2,1)} %param.11) | copy-start | bytes 7077892
  7.2 13.0 %copy-start.14 = (f32[768]{0:T(1024)S(1)}, f32[768]{0:T(1024)}, u32[]{:S(2)}) copy-start(f32[768]{0:T(1024)} %param.9) | copy-start | bytes 9220
  7.2 43.3 %all-gather.3.cloned.1.call-start = ((), (), s32[]{:S(2)}) async-start(), calls=%async_computation.2 | async-start | bytes 2359296 | tf_op jit(solution)/shard_map/all_gather | solution.py:50
  21.4 62.6 %reduce-scatter.3.cloned.1.call-start = ((), (), s32[]{:S(2)}) async-start(), calls=%async_computation.4 | async-start | bytes 2359296 | tf_op jit(solution)/shard_map/reduce_scatter | solution.py:59
  25.9 123.8 %all-gather.5.cloned.1.call-start = ((), (), s32[]{:S(2)}) async-start(), calls=%async_computation.3 | async-start | bytes 2359296 | tf_op jit(solution)/shard_map/all_gather | solution.py:50
  50.5 3.7 copy-start.5
  54.2 2.7 copy-start.11
  57.0 3.2 collective-permute-start
  58.7 4.3 collective-permute-start.1
  63.2 8.9 %copy-start.1 = (f32[768,544]{0,1:T(8,128)}, f32[768,544]{0,1:T(8,128)S(1)}, u32[]{:S(2)}) copy-start(f32[768,544]{0,1:T(8,128)S(1)} %convert_element_type.70) | copy-start | bytes 5013508
  72.1 11.8 %copy-start.15 = (f32[768]{0:T(1024)S(1)}, f32[768]{0:T(1024)}, u32[]{:S(2)}) copy-start(f32[768]{0:T(1024)} %param.13) | copy-start | bytes 9220
  97.1 2.9 collective-permute-start.2
  98.5 5.7 %collective-permute-start.3 = (bf16[768,16]{0,1:T(8,128)(2,1)S(1)}, bf16[768,16]{0,1:T(8,128)(2,1)S(1)}, u32[]{:S(2)}, u32[]{:S(2)}) collective-permute-start(bf16[768,16]{0,1:T(8,128)(2,1)S(1)} %get-tuple-element.103), channel_id=1, source_target_pairs={{2,0},{4,2},{6,4},{8,6},{10,8},{12,10},{14,12},{16,14},{18,16},{20... | collective-permute-start | bytes 73736 | tf_op jit(solution)/shard_map/ppermute | solution.py:19
  99.8 61.9 %reduce-scatter.5.cloned.1.call-start = ((), (), s32[]{:S(2)}) async-start(), calls=%async_computation.5 | async-start | bytes 2359296 | tf_op jit(solution)/shard_map/reduce_scatter | solution.py:59
  104.2 1.6 copy-start.12
  105.5 1.5 copy-start.7
  113.6 3.4 copy-start.10
  113.6 2.0 copy-start.16
  115.6 1.4 copy-start.8
  119.5 361.7 %all-reduce.6.cloned.1.call-start = ((), (), s32[]{:S(2)}) async-start(), calls=%async_computation.6 | async-start | bytes 196608 | tf_op jit(solution)/shard_map/psum | solution.py:133
  121.9 14.7 %copy-start.2 = (f32[768,544]{0,1:T(8,128)S(1)}, f32[768,544]{0,1:T(8,128)}, u32[]{:S(2)}) copy-start(f32[768,544]{0,1:T(8,128)} %copy-done.1) | copy-start | bytes 5013508
  121.9 14.7 %copy-start.4 = (bf16[768,512]{0,1:T(8,128)(2,1)S(1)}, bf16[768,512]{0,1:T(8,128)(2,1)}, u32[]{:S(2)}) copy-start(bf16[768,512]{0,1:T(8,128)(2,1)} %copy-done.3) | copy-start | bytes 2359300
  140.7 5.4 %copy-start.6 = (bf16[1536,512]{0,1:T(8,128)(2,1)S(1)}, bf16[1536,512]{0,1:T(8,128)(2,1)}, u32[]{:S(2)}) copy-start(bf16[1536,512]{0,1:T(8,128)(2,1)} %all-gather.3.cloned.1.call-done) | copy-start | bytes 4718596
  140.7 5.4 %copy-start.9 = (bf16[768,512]{0,1:T(8,128)(2,1)S(1)}, bf16[768,512]{0,1:T(8,128)(2,1)}, u32[]{:S(2)}) copy-start(bf16[768,512]{0,1:T(8,128)(2,1)} %copy-done.8) | copy-start | bytes 2359300
  (2 other events, 1.8 us)
Sparse Core Ops, SparseCore 0:
  21.5 29.0 all-gather.2
  52.8 26.1 reduce-scatter.2
  99.9 31.9 all-gather.4
  134.7 26.0 reduce-scatter.4
  164.7 98.4 all-reduce.5
where the time goes:
time: 494 us; the launch traced here: 489 us
  blocking collectives  334 us (68%)
  other arithmetic  51.1 us (10%)
  matrix products  33.5 us (7%)
  waiting for transfers between devices  30.8 us (6%)
  local copies, waits for them, and re-layouts  19.7 us (4%)
  between operations  14.3 us (3%)
  starting transfers between devices  6.04 us (1%)
    psum x1, blocking collectives, local(): lax.psum((grad_out, grad_kernel, grad_conv_gain, grad_value, grad_gate, g...  303 us
    psum x6, blocking collectives, row_sums(): return lax.psum(values, 'tp')  30.7 us
    all_gather x2, waiting for transfers between devices, spread_channels(): return lax.all_gather(values, 'tp', axis=0, tiled=True)  23.6 us
    unnamed x40, local copies, waits for them, and re-layouts  19.1 us
    reduce_sum x2, other arithmetic, local(): jnp.sum(glu_wide[:, tap:tap + row_count] * d_conv_f, axis=1)  17.5 us
    dot_general x3, matrix products, contract_cols(): lax.dot_general(left, right, (((1,), (1,)), ((), ())), preferred_element_...  14.3 us
  transfers between devices with their start and end apart: 9, of which 3 were waited for; matrix products, arithmetic and copies ran while one was open for 18% of the time, Pallas kernels for 0%

commit v1 on v0

v1 whole, which is shorter than its diff:
```python
import jax
import jax.numpy as jnp
from jax import lax
from jax.sharding import PartitionSpec as P

EPS = 1e-05
F32 = jnp.float32
BF16 = jnp.bfloat16


def ring_of(count):
    chips = count // 2
    if chips % 2 == 0:
        cols = chips // 2
        order = [2 * col for col in range(cols)] + [2 * col + 1 for col in reversed(range(cols))]
    else:
        order = list(range(chips))
    place = [0] * count
    ahead, behind = [], []
    for spot, chip in enumerate(order):
        after = order[(spot + 1) % chips]
        for core in range(2):
            place[2 * chip + core] = spot
            ahead.append((2 * chip + core, 2 * after + core))
            behind.append((2 * after + core, 2 * chip + core))
    return chips, place, ahead, behind


def pairs_of(count, step):
    return [(i, i ^ step) for i in range(count)]


def add(left, right):
    return (left.astype(F32) + right.astype(F32)).astype(BF16)


def ring_sum(sets):
    count = lax.axis_size("seq")
    chips, place, ahead, behind = ring_of(count)
    spot = jnp.asarray(place, jnp.int32)[lax.axis_index("seq")]
    reach = chips // 2

    def part(cells, step):
        return lax.dynamic_index_in_dim(cells, (spot + step + chips) % chips, 0, keepdims=False)

    def up(cells):
        return lax.ppermute(cells, "seq", ahead)

    def down(cells):
        return lax.ppermute(cells, "seq", behind)

    half = sets[0].shape[1] // 2
    flows = [(up(part(x, reach)[half:]), down(part(x, -reach)[:half])) for x in sets]
    for hop in range(reach - 1, 0, -1):
        later = []
        for x, (u, d) in zip(sets, flows):
            own_u, own_d = part(x, hop), part(x, -hop)
            if hop == reach - 1:
                u = jnp.concatenate([own_u[:half], add(own_u[half:], u)])
                d = jnp.concatenate([add(own_d[:half], d), own_d[half:]])
            else:
                u, d = add(own_u, u), add(own_d, d)
            later.append((up(u), down(d)))
        flows = later
    owns = [
        (part(x, 0).astype(F32) + u.astype(F32) + d.astype(F32)).astype(BF16)
        for x, (u, d) in zip(sets, flows)
    ]
    outs = []
    for x, own in zip(sets, owns):
        outs.append(lax.dynamic_update_index_in_dim(jnp.zeros_like(x), own, spot, 0))
    flows = [(own, own) for own in owns]
    for hop in range(1, reach):
        flows = [(up(u), down(d)) for u, d in flows]
        for i, (u, d) in enumerate(flows):
            out = lax.dynamic_update_index_in_dim(outs[i], u, (spot - hop + chips) % chips, 0)
            outs[i] = lax.dynamic_update_index_in_dim(out, d, (spot + hop) % chips, 0)
    for i, (u, d) in enumerate(flows):
        far = jnp.concatenate([down(d[:half]), up(u[half:])])
        outs[i] = lax.dynamic_update_index_in_dim(outs[i], far, (spot + reach) % chips, 0)
    return outs


def weight_sums(grads):
    count = lax.axis_size("seq")
    rows, cols = grads[0].shape
    chips = count // 2
    if count % 4 or rows % (2 * chips) or rows // (2 * chips) < 2:
        return [lax.psum(g.astype(BF16), "seq") for g in grads]
    core = lax.axis_index("seq") % 2
    swap = pairs_of(count, 1)
    half = rows // 2
    sets = []
    for g in grads:
        g = g.astype(BF16)
        theirs = lax.dynamic_slice_in_dim(g, (1 - core) * half, half, 0)
        mine = lax.dynamic_slice_in_dim(g, core * half, half, 0)
        mine = add(mine, lax.ppermute(theirs, "seq", swap))
        sets.append(mine.reshape(chips, half // chips, cols))
    outs = []
    for mine in ring_sum(sets):
        mine = mine.reshape(half, cols)
        theirs = lax.ppermute(mine, "seq", swap)
        outs.append(
            jnp.where(
                core == 0,
                jnp.concatenate([mine, theirs]),
                jnp.concatenate([theirs, mine]),
            )
        )
    return outs


def small_sum(values):
    count = lax.axis_size("seq")
    if count & (count - 1):
        return lax.psum(values, "seq")
    step = 1
    while step < count:
        values = values + lax.ppermute(values, "seq", pairs_of(count, step))
        step *= 2
    return values


def other(values):
    return lax.ppermute(values, "tp", [(0, 1), (1, 0)])


def tp_sum(values):
    if lax.axis_size("tp") == 2:
        return values + other(values)
    return lax.psum(values, "tp")


def tp_gather(values):
    if lax.axis_size("tp") == 2:
        theirs = other(values)
        first = lax.axis_index("tp") == 0
        return jnp.where(
            first, jnp.concatenate([values, theirs]), jnp.concatenate([theirs, values])
        )
    return lax.all_gather(values, "tp", axis=0, tiled=True)


def tp_scatter(term):
    term = term.astype(BF16)
    if lax.axis_size("tp") == 2:
        rows = term.shape[0] // 2
        me = lax.axis_index("tp")
        theirs = lax.dynamic_slice_in_dim(term, (1 - me) * rows, rows, 0)
        mine = lax.dynamic_slice_in_dim(term, me * rows, rows, 0)
        return mine.astype(F32) + other(theirs).astype(F32)
    return lax.psum_scatter(term, "tp", scatter_dimension=0, tiled=True).astype(F32)


def halo(cells, reach):
    count = lax.axis_size("seq")
    size = cells.shape[1]
    right = [(i, i + 1) for i in range(count - 1)]
    left = [(i + 1, i) for i in range(count - 1)]
    before = lax.ppermute(cells[:, size - reach :], "seq", right)
    after = lax.ppermute(cells[:, :reach], "seq", left)
    return jnp.concatenate([before, cells, after], axis=1)


def norm_back(d_hat, hat, inverse, width):
    sums = jnp.concatenate(
        [jnp.sum(d_hat, axis=0, keepdims=True), jnp.sum(d_hat * hat, axis=0, keepdims=True)]
    )
    sums = tp_sum(sums) / width
    return (d_hat - sums[:1] - hat * sums[1:]) * inverse


def contract_rows(left, right):
    return lax.dot_general(left, right, (((0,), (0,)), ((), ())), preferred_element_type=F32)


def contract_cols(left, right):
    return lax.dot_general(left, right, (((1,), (1,)), ((), ())), preferred_element_type=F32)


def local(
    frames_in, norm_gain, value_weight, gate_weight, depth_kernel, conv_gain, out_weight, cotangent
):
    chans, row_count = frames_in.shape
    parts = lax.axis_size("tp")
    me = lax.axis_index("tp")
    width = chans * parts
    taps = depth_kernel.shape[1]
    reach = taps // 2
    scale = float(row_count * lax.axis_size("seq")) ** (-0.5)

    frames_all = tp_gather(frames_in)
    gain_all = lax.all_gather(norm_gain, "tp", axis=0, tiled=True)
    d_act = tp_scatter(contract_rows(out_weight, cotangent))

    wide = frames_all.astype(F32)
    centred = wide - jnp.mean(wide, axis=0, keepdims=True)
    inverse_in = lax.rsqrt(jnp.mean(centred * centred, axis=0, keepdims=True) + EPS)
    hat_all = centred * inverse_in
    normed_all = (hat_all * gain_all[:, None]).astype(BF16)
    value = jnp.dot(value_weight, normed_all, preferred_element_type=F32)
    gate = jnp.dot(gate_weight, normed_all, preferred_element_type=F32)
    gate_sig = jax.nn.sigmoid(gate)
    glu = (value * gate_sig).astype(BF16)
    glu_wide = halo(glu, reach).astype(F32)
    conv = jnp.zeros((chans, row_count), F32)
    for tap in range(taps):
        conv = conv + depth_kernel[:, tap : tap + 1] * glu_wide[:, tap : tap + row_count]

    mean = jnp.mean(conv, axis=0, keepdims=True)
    spread = jnp.sum((conv - mean) ** 2, axis=0, keepdims=True)
    if parts == 2:
        there = other(jnp.concatenate([mean, spread]))
        gap = mean - there[:1]
        mean = (mean + there[:1]) * 0.5
        spread = (spread + there[1:] + gap * gap * (chans * 0.5)) / width
    else:
        whole = lax.pmean(mean, "tp")
        spread = lax.psum(spread + chans * (mean - whole) ** 2, "tp") / width
        mean = whole
    inverse_conv = lax.rsqrt(spread + EPS)
    hat_conv = (conv - mean) * inverse_conv
    scaled = hat_conv * conv_gain[:, None]
    swish_sig = jax.nn.sigmoid(scaled)
    act = (scaled * swish_sig).astype(BF16)
    act_all = tp_gather(act)
    block_out = (
        frames_in.astype(F32) + jnp.dot(out_weight, act_all, preferred_element_type=F32)
    ).astype(BF16)
    grad_out = contract_cols(cotangent, act_all) * scale

    d_scaled = d_act * (swish_sig + scaled * swish_sig * (1.0 - swish_sig))
    grad_conv_gain = jnp.sum(d_scaled * hat_conv, axis=1) * scale
    d_conv = norm_back(d_scaled * conv_gain[:, None], hat_conv, inverse_conv, width).astype(BF16)
    d_conv_f = d_conv.astype(F32)
    d_conv_wide = halo(d_conv, reach).astype(F32)
    d_glu = jnp.zeros((chans, row_count), F32)
    kernel_cols = []
    for tap in range(taps):
        start = 2 * reach - tap
        d_glu = d_glu + depth_kernel[:, tap : tap + 1] * d_conv_wide[:, start : start + row_count]
        kernel_cols.append(jnp.sum(glu_wide[:, tap : tap + row_count] * d_conv_f, axis=1))
    grad_kernel = jnp.stack(kernel_cols, axis=0) * scale
    d_value = (d_glu * gate_sig).astype(BF16)
    d_gate = (d_glu * value * gate_sig * (1.0 - gate_sig)).astype(BF16)
    grad_value = contract_cols(d_value, normed_all) * scale
    grad_gate = contract_cols(d_gate, normed_all) * scale
    d_normed = tp_scatter(
        contract_rows(value_weight, d_value) + contract_rows(gate_weight, d_gate)
    )
    hat_in = lax.dynamic_slice_in_dim(hat_all, me * chans, chans, 0)
    grad_norm_gain = jnp.sum(d_normed * hat_in, axis=1) * scale
    input_grad = (
        cotangent.astype(F32) + norm_back(d_normed * norm_gain[:, None], hat_in, inverse_in, width)
    ).astype(BF16)
    small = small_sum(
        jnp.concatenate([grad_kernel, grad_conv_gain[None], grad_norm_gain[None]], axis=0)
    )
    grad_out, grad_value, grad_gate = weight_sums([grad_out, grad_value, grad_gate])
    return (
        block_out,
        input_grad,
        small[taps + 1],
        grad_value,
        grad_gate,
        small[:taps].T,
        small[taps],
        grad_out,
    )


def solution(mesh):
    return jax.shard_map(
        local,
        mesh=mesh,
        in_specs=(
            P("tp", "seq"),
            P("tp"),
            P("tp", None),
            P("tp", None),
            P("tp", None),
            P("tp"),
            P("tp", None),
            P("tp", "seq"),
        ),
        out_specs=(
            P("tp", "seq"),
            P("tp", "seq"),
            P("tp"),
            P("tp", None),
            P("tp", None),
            P("tp", None),
            P("tp"),
            P("tp", None),
        ),
        check_vma=False,
    )
```

time: 494 us -> 317 us (0.64)
  blocking collectives: 334 us -> 29.2 us
  starting transfers between devices: 6.04 us -> 78.5 us
  waiting for transfers between devices: 30.8 us -> 69.4 us
  local copies, waits for them, and re-layouts: 19.7 us -> 45.5 us
  matrix products: 33.5 us -> 20.7 us
  other arithmetic: 51.1 us -> 62.1 us
    psum x7 -> x0, blocking collectives: 334 us -> none  [the longest x1 303 us: local(): lax.psum((grad_out, grad_kernel, grad_conv_gain, grad_value, grad_gate, g...]
    ppermute x4 -> x69, starting transfers between devices: 5.65 us -> 78.5 us  [the longest x24 27.4 us: up(): return lax.ppermute(cells, 'seq', ahead)]
    ppermute x4 -> x69, waiting for transfers between devices: 7.06 us -> 69.4 us  [the longest x24 24.4 us: up(): return lax.ppermute(cells, 'seq', ahead)]
    all_gather x0 -> x1, blocking collectives: none -> 29.2 us  [local(): gain_all = lax.all_gather(norm_gain, 'tp', axis=0, tiled=True)]
    all_gather x2 -> x0, waiting for transfers between devices: 23.6 us -> none  [spread_channels(): return lax.all_gather(values, 'tp', axis=0, tiled=True)]
    dynamic_update_slice x0 -> x18, local copies, waits for them, and re-layouts: none -> 12.1 us  [the longest x9 6.05 us: ring_sum(): outs[i] = lax.dynamic_update_index_in_dim(out, d, (spot + hop) % chips, 0)]
    select_n x0 -> x3, other arithmetic: none -> 11.1 us  [weight_sums(): jnp.where(core == 0, jnp.concatenate([mine, theirs]), jnp.concatenate([th...]
    another operation x33 -> x36, local copies, waits for them, and re-layouts: 0.33 us -> 10.3 us  [the longest x33 6.97 us: local(): grad_kernel = jnp.stack(kernel_cols, axis=0) * scale]
  transfers between devices with their start and end apart: 9 -> 69, of which waited for: 3 -> 28; matrix products, arithmetic and copies ran while one was open for 18% -> 35% of each run, Pallas kernels for 0% -> 0%
where the time goes in v1:
time: 317 us; the launch traced here: 316 us
  starting transfers between devices  78.5 us (25%)
  waiting for transfers between devices  69.4 us (22%)
  other arithmetic  62.1 us (20%)
  local copies, waits for them, and re-layouts  45.5 us (14%)
  blocking collectives  29.2 us (9%)
  matrix products  20.7 us (7%)
  between operations  10.9 us (3%)
    all_gather x1, blocking collectives, local(): gain_all = lax.all_gather(norm_gain, 'tp', axis=0, tiled=True)  29.2 us
    ppermute x24, starting transfers between devices, up(): return lax.ppermute(cells, 'seq', ahead)  27.4 us
    ppermute x24, starting transfers between devices, down(): return lax.ppermute(cells, 'seq', behind)  25.8 us
    ppermute x24, waiting for transfers between devices, up(): return lax.ppermute(cells, 'seq', ahead)  24.4 us
    ppermute x7, waiting for transfers between devices, other(): return lax.ppermute(values, 'tp', [(0, 1), (1, 0)])  22.4 us
    ppermute x24, waiting for transfers between devices, down(): return lax.ppermute(cells, 'seq', behind)  16.3 us
    unnamed x66, local copies, waits for them, and re-layouts  15.9 us
    select_n x3, other arithmetic, weight_sums(): jnp.where(core == 0, jnp.concatenate([mine, theirs]), jnp.concatenate([th...  11.1 us
  transfers between devices with their start and end apart: 69, of which 28 were waited for; matrix products, arithmetic and copies ran while one was open for 35% of the time, Pallas kernels for 0%

profile of v1, /device:TPU:0, one launch (start us, length us, event | category | flops | bytes accessed | tf_op | source)
XLA Modules:
  0.0 316.3 jit_solution(2036407194559973012)
XLA Ops:
  2.2 3.0 collective-permute-start
  5.2 3.3 %convolution_convert_fusion = bf16[1536,512]{0,1:T(8,128)(2,1)S(1)} fusion(bf16[768,1536]{1,0:T(8,128)(2,1)} %param.15, bf16[768,512]{1,0:T(8,128)(2,1)} %param.16), kind=kOutput, calls=%fused_computation.43 | convolution fusion | flops 1208745984 | bytes 4718592 | tf_op jit(solution)/shard_map/dot_general | solution.py:175
  10.6 29.2 %all-gather = f32[2,1,768]{2,1,0:T(1,128)S(1)} all-gather(f32[1,1,768]{2,1,0:T(1,128)S(1)} %reshape.164), channel_id=1, replica_groups=mesh['seq'=16,'tp'=2] {'tp'}, dimensions={0}, use_global_device_ids=true | all-gather | bytes 9216 | tf_op jit(solution)/shard_map/all_gather | solution.py:194
  44.1 3.4 %multiply_convert_fusion.3 = (bf16[1536,512]{0,1:T(8,128)(2,1)S(1)}, f32[1536,512]{0,1:T(8,128)}) fusion(f32[1536]{0:T(1024)S(1)} %reshape.165, f32[512]{0:T(512)S(1)} %add_rsqrt_fusion.1, f32[512]{0:T(512)S(1)} %broadcast_multiply_fusion.4, bf16[768,512]{0,1:T(8,128)(2,1)S(1)} %copy.24, bf16[768,512]{0,1:T(8,128)(2,1)} %collective-permute-done, pred[]{:T(512)S(6)} %eq.59), kind=kLoop, calls=%fused_computation.41 | loop fusion | flops 11010048 | bytes 6301697 | tf_op jit(solution)/shard_map/convert_element_type | solution.py:201
  53.9 3.2 %collective-permute-start.1 = (bf16[768,16]{0,1:T(8,128)(2,1)S(1)}, bf16[768,16]{0,1:T(8,128)(2,1)S(1)}, u32[]{:S(2)}, u32[]{:S(2)}) collective-permute-start(bf16[768,16]{0,1:T(8,128)(2,1)S(1)} %get-tuple-element.137), channel_id=1, source_target_pairs={{0,2},{2,4},{4,6},{6,8},{8,10},{10,12},{12,14},{14,16},{16,18},{18... | collective-permute-start | bytes 73736 | tf_op jit(solution)/shard_map/ppermute | solution.py:161
  68.1 8.2 %fusion.111 = (f32[512]{0:T(512)S(1)}, f32[768,512]{0,1:T(8,128)S(1)}) fusion(f32[768,544]{0,1:T(8,128)S(1)} %maximum_convert_fusion, f32[768]{0:T(1024)S(1)} %get-tuple-element.94, f32[768]{0:T(1024)S(1)} %get-tuple-element.95, f32[768]{0:T(1024)S(1)} %get-tuple-element.65, f32[768]{0:T(1024)S(1)} %get-tuple-element.66, f32[768]{0:T(1024)S(1)} %get-tuple-element.67, ...), kind=kLoop, calls=%fused_computation.334 | loop fusion | flops 25165312 | bytes 52004864 | tf_op jit(solution)/shard_map/reduce_sum | solution.py:211
  82.3 4.1 %multiply_reduce_fusion.1 = (f32[768]{0:T(1024)S(1)}, f32[512]{0:T(512)S(1)}, f32[512]{0:T(512)S(1)}, f32[768,512]{0,1:T(8,128)S(1)}, bf16[768,512]{0,1:T(8,128)(2,1)}) fusion(f32[768,512]{0,1:T(8,128)} %copy-done.3, f32[512]{0:T(512)S(1)} %bitcast.259, f32[512]{0:T(512)S(1)} %bitcast.257, f32[768]{0:T(1024)S(1)} %copy-done.25, ...), kind=kLoop, calls=%fused_computation.161 | loop fusion | flops 8255744 | bytes 5519364 | tf_op jit(solution)/shard_map/reduce_sum | solution.py:234
  88.6 18.6 %collective-permute-done.6 = f32[2,512]{1,0:T(2,128)S(1)} collective-permute-done((f32[2,512]{1,0:T(2,128)S(1)}, f32[2,512]{1,0:T(2,128)S(1)}, u32[]{:S(2)}, u32[]{:S(2)}) %collective-permute-start.6) | collective-permute-done | bytes 4128 | tf_op jit(solution)/shard_map/ppermute | solution.py:126
  107.2 4.7 %fusion.36 = (f32[768]{0:T(1024)S(1)}, f32[768]{0:T(1024)S(1)}, f32[768]{0:T(1024)S(1)}, f32[768]{0:T(1024)S(1)}, f32[768]{0:T(1024)S(1)}, /*index=5*/f32[768]{0...) fusion(f32[768,544]{0,1:T(8,128)S(1)} %copy-done.2, ...), kind=kLoop, calls=%fused_computation.82 | loop fusion | flops 17680896 | bytes 32310272 | tf_op jit(solution)/shard_map/reduce_sum | solution.py:243
  116.7 3.3 %collective-permute-start.7 = (bf16[768,16]{0,1:T(8,128)(2,1)S(1)}, bf16[768,16]{0,1:T(8,128)(2,1)S(1)}, u32[]{:S(2)}, u32[]{:S(2)}) collective-permute-start(bf16[768,16]{0,1:T(8,128)(2,1)S(1)} %get-tuple-element.135), channel_id=1, source_target_pairs={{0,2},{2,4},{4,6},{6,8},{8,10},{10,12},{12,14},{14,16},{16,18},{18... | collective-permute-start | bytes 73736 | tf_op jit(solution)/shard_map/ppermute | solution.py:161
  128.8 7.6 %fusion.72 = (bf16[768,512]{0,1:T(8,128)(2,1)S(1)}, f32[768,512]{0,1:T(8,128)S(1)}) fusion(f32[512,768]{1,0:T(8,128)S(1)} %copy-done.7, f32[512,768]{1,0:T(8,128)} %copy-done.18, f32[768,544]{0,1:T(8,128)S(1)} %maximum_convert_fusion.1, f32[768]{0:T(1024)S(1)} %get-tuple-element.94, f32[768]{0:T(1024)S(1)} %get-tuple-element.95, ...), kind=kLoop, calls=%fused_computation.158 | loop fusion | flops 26738688 | bytes 55934976 | tf_op jit(solution)/shard_map/convert_element_type | solution.py:246
  150.8 4.2 %fusion.68 = bf16[768,512]{0,1:T(8,128)(2,1)} fusion(bf16[768,512]{0,1:T(8,128)(2,1)S(1)} %copy.24, bf16[768,1536]{1,0:T(8,128)(2,1)S(1)} %copy-done.28, bf16[768,512]{0,1:T(8,128)(2,1)} %collective-permute-done.4, bf16[768,512]{0,1:T(8,128)(2,1)} %get-tuple-element.110, pred[]{:T(512)S(6)} %eq.59), kind=kOutput, calls=%fused_computation.150 | convolution fusion | flops 1216217088 | bytes 5505025 | tf_op jit(solution)/shard_map/dot_general | solution.py:229
  157.4 3.4 %multiply_convert_fusion = bf16[1536,768]{0,1:T(8,128)(2,1)S(1)} fusion(bf16[768,512]{1,0:T(8,128)(2,1)S(1)} %copy-done.20, bf16[768,512]{0,1:T(8,128)(2,1)} %collective-permute-done.4, bf16[768,512]{0,1:T(8,128)(2,1)} %get-tuple-element.110, pred[]{:T(512)S(6)} %eq.59), kind=kOutput, calls=%fused_computation.32 | convolution fusion | flops 1217396736 | bytes 4718593 | tf_op jit(solution)/shard_map/dot_general | solution.py:179
  169.6 3.0 collective-permute-done.12
  177.8 3.1 collective-permute-start.14
  195.6 4.1 %collective-permute-done.35 = bf16[48,1536]{1,0:T(8,128)(2,1)S(1)} collective-permute-done((bf16[48,1536]{1,0:T(8,128)(2,1)S(1)}, bf16[48,1536]{1,0:T(8,128)(2,1)S(1)}, u32[]{:S(2)}, u32[]{:S(2)}) %collective-permute-start.35) | collective-permute-done | bytes 147488 | tf_op jit(solution)/shard_map/ppermute | solution.py:47
  201.1 4.9 %collective-permute-done.18 = bf16[48,1536]{1,0:T(8,128)(2,1)S(1)} collective-permute-done((bf16[48,1536]{1,0:T(8,128)(2,1)S(1)}, bf16[48,1536]{1,0:T(8,128)(2,1)S(1)}, u32[]{:S(2)}, u32[]{:S(2)}) %collective-permute-start.18) | collective-permute-done | bytes 147488 | tf_op jit(solution)/shard_map/ppermute | solution.py:47
  209.1 3.6 %collective-permute-done.22 = bf16[48,1536]{1,0:T(8,128)(2,1)S(1)} collective-permute-done((bf16[48,1536]{1,0:T(8,128)(2,1)S(1)}, bf16[48,1536]{1,0:T(8,128)(2,1)S(1)}, u32[]{:S(2)}, u32[]{:S(2)}) %collective-permute-start.22) | collective-permute-done | bytes 147488 | tf_op jit(solution)/shard_map/ppermute | solution.py:50
  216.3 3.5 %collective-permute-done.23 = bf16[48,1536]{1,0:T(8,128)(2,1)S(1)} collective-permute-done((bf16[48,1536]{1,0:T(8,128)(2,1)S(1)}, bf16[48,1536]{1,0:T(8,128)(2,1)S(1)}, u32[]{:S(2)}, u32[]{:S(2)}) %collective-permute-start.23) | collective-permute-done | bytes 147488 | tf_op jit(solution)/shard_map/ppermute | solution.py:50
  240.5 3.6 %collective-permute-done.44 = bf16[48,1536]{1,0:T(8,128)(2,1)S(1)} collective-permute-done((bf16[48,1536]{1,0:T(8,128)(2,1)S(1)}, bf16[48,1536]{1,0:T(8,128)(2,1)S(1)}, u32[]{:S(2)}, u32[]{:S(2)}) %collective-permute-start.44) | collective-permute-done | bytes 147488 | tf_op jit(solution)/shard_map/ppermute | solution.py:47
  263.3 4.1 %collective-permute-done.58 = bf16[48,1536]{1,0:T(8,128)(2,1)S(1)} collective-permute-done((bf16[48,1536]{1,0:T(8,128)(2,1)S(1)}, bf16[48,1536]{1,0:T(8,128)(2,1)S(1)}, u32[]{:S(2)}, u32[]{:S(2)}) %collective-permute-start.58) | collective-permute-done | bytes 147488 | tf_op jit(solution)/shard_map/ppermute | solution.py:50
  305.2 3.6 %maximum_select_fusion = bf16[768,1536]{1,0:T(8,128)(2,1)} fusion(bf16[384,1536]{1,0:T(8,128)(2,1)} %collective-permute-done.32, bf16[384,1536]{1,0:T(8,128)(2,1)} %bitcast.38, pred[]{:T(512)S(6)} %eq.60), kind=kLoop, calls=%fused_computation.44 | loop fusion | flops 10616832 | bytes 4718593 | tf_op jit(solution)/shard_map/jit(_where)/select_n | solution.py:105
  308.8 3.7 %maximum_select_fusion.1 = bf16[768,1536]{1,0:T(8,128)(2,1)} fusion(bf16[384,1536]{1,0:T(8,128)(2,1)} %collective-permute-done.50, bf16[384,1536]{1,0:T(8,128)(2,1)} %bitcast.59, pred[]{:T(512)S(6)} %eq.60), kind=kLoop, calls=%fused_computation.45 | loop fusion | flops 10616832 | bytes 4718593 | tf_op jit(solution)/shard_map/jit(_where)/select_n | solution.py:105
  312.5 3.8 %maximum_select_fusion.2 = bf16[768,1536]{1,0:T(8,128)(2,1)} fusion(bf16[384,1536]{1,0:T(8,128)(2,1)} %collective-permute-done.68, bf16[384,1536]{1,0:T(8,128)(2,1)} %bitcast.83, pred[]{:T(512)S(6)} %eq.60), kind=kLoop, calls=%fused_computation.46 | loop fusion | flops 10616832 | bytes 4718593 | tf_op jit(solution)/shard_map/jit(_where)/select_n | solution.py:105
  (331 shorter events, 168.3 us)
Async XLA Ops:
  2.2 37.8 %collective-permute-start = (bf16[768,512]{0,1:T(8,128)(2,1)S(1)}, bf16[768,512]{0,1:T(8,128)(2,1)}, u32[]{:S(2)}, u32[]{:S(2)}) collective-permute-start(bf16[768,512]{0,1:T(8,128)(2,1)S(1)} %copy.24), channel_id=1, source_target_pairs={{0,1},{1,0},{2,3},{3,2},{4,5},{5,4},{6,7},{7,6},{8,9},{9,8},{10,11... | collective-permute-start | bytes 2359304 | tf_op jit(solution)/shard_map/ppermute | solution.py:126
  10.6 71.7 %collective-permute-start.5 = (bf16[768,512]{0,1:T(8,128)(2,1)}, bf16[768,512]{0,1:T(8,128)(2,1)}, u32[]{:S(2)}, u32[]{:S(2)}) collective-permute-start(bf16[768,512]{0,1:T(8,128)(2,1)} %constant_dynamic-slice_fusion.2), channel_id=1, source_target_pairs={{0,1},{1,0},{2,3},{3,2},{4,5},{5,4},{6,7},{7,6},{8,9},{9,8},{10,11... | collective-permute-start | bytes 2359304 | tf_op jit(solution)/shard_map/ppermute | solution.py:126
  52.6 14.2 %collective-permute-start.2 = (bf16[768,16]{0,1:T(8,128)(2,1)S(1)}, bf16[768,16]{0,1:T(8,128)(2,1)S(1)}, u32[]{:S(2)}, u32[]{:S(2)}) collective-permute-start(bf16[768,16]{0,1:T(8,128)(2,1)S(1)} %get-tuple-element.138), channel_id=1, source_target_pairs={{2,0},{4,2},{6,4},{8,6},{10,8},{12,10},{14,12},{16,14},{18,16},{20... | collective-permute-start | bytes 73736 | tf_op jit(solution)/shard_map/ppermute | solution.py:162
  53.9 12.9 %collective-permute-start.1 = (bf16[768,16]{0,1:T(8,128)(2,1)S(1)}, bf16[768,16]{0,1:T(8,128)(2,1)S(1)}, u32[]{:S(2)}, u32[]{:S(2)}) collective-permute-start(bf16[768,16]{0,1:T(8,128)(2,1)S(1)} %get-tuple-element.137), channel_id=1, source_target_pairs={{0,2},{2,4},{4,6},{6,8},{8,10},{10,12},{12,14},{14,16},{16,18},{18... | collective-permute-start | bytes 73736 | tf_op jit(solution)/shard_map/ppermute | solution.py:161
  86.5 63.4 %collective-permute-start.4 = (bf16[768,512]{0,1:T(8,128)(2,1)}, bf16[768,512]{0,1:T(8,128)(2,1)}, u32[]{:S(2)}, u32[]{:S(2)}) collective-permute-start(bf16[768,512]{0,1:T(8,128)(2,1)} %get-tuple-element.110), channel_id=1, source_target_pairs={{0,1},{1,0},{2,3},{3,2},{4,5},{5,4},{6,7},{7,6},{8,9},{9,8},{10,11... | collective-permute-start | bytes 2359304 | tf_op jit(solution)/shard_map/ppermute | solution.py:126
  87.4 19.8 %collective-permute-start.6 = (f32[2,512]{1,0:T(2,128)S(1)}, f32[2,512]{1,0:T(2,128)S(1)}, u32[]{:S(2)}, u32[]{:S(2)}) collective-permute-start(f32[2,512]{1,0:T(2,128)S(1)} %pad_maximum_fusion.8), channel_id=1, source_target_pairs={{0,1},{1,0},{2,3},{3,2},{4,5},{5,4},{6,7},{7,6},{8,9},{9,8},{10,11... | collective-permute-start | bytes 12296 | tf_op jit(solution)/shard_map/ppermute | solution.py:126
  115.4 11.7 %collective-permute-start.8 = (bf16[768,16]{0,1:T(8,128)(2,1)}, bf16[768,16]{0,1:T(8,128)(2,1)S(1)}, u32[]{:S(2)}, u32[]{:S(2)}) collective-permute-start(bf16[768,16]{0,1:T(8,128)(2,1)} %get-tuple-element.136), channel_id=1, source_target_pairs={{2,0},{4,2},{6,4},{8,6},{10,8},{12,10},{14,12},{16,14},{18,16},{20... | collective-permute-start | bytes 73736 | tf_op jit(solution)/shard_map/ppermute | solution.py:162
  116.7 10.5 %collective-permute-start.7 = (bf16[768,16]{0,1:T(8,128)(2,1)S(1)}, bf16[768,16]{0,1:T(8,128)(2,1)S(1)}, u32[]{:S(2)}, u32[]{:S(2)}) collective-permute-start(bf16[768,16]{0,1:T(8,128)(2,1)S(1)} %get-tuple-element.135), channel_id=1, source_target_pairs={{0,2},{2,4},{4,6},{6,8},{8,10},{10,12},{12,14},{14,16},{16,18},{18... | collective-permute-start | bytes 73736 | tf_op jit(solution)/shard_map/ppermute | solution.py:161
  143.3 20.4 %collective-permute-start.9 = (bf16[768,512]{0,1:T(8,128)(2,1)}, bf16[768,512]{0,1:T(8,128)(2,1)}, u32[]{:S(2)}, u32[]{:S(2)}) collective-permute-start(bf16[768,512]{0,1:T(8,128)(2,1)} %dynamic-slice_bitcast_fusion.1), channel_id=1, source_target_pairs={{0,1},{1,0},{2,3},{3,2},{4,5},{5,4},{6,7},{7,6},{8,9},{9,8},{10,11... | collective-permute-start | bytes 2359304 | tf_op jit(solution)/shard_map/ppermute | solution.py:126
  144.9 35.9 %collective-permute-start.15 = (bf16[384,1536]{1,0:T(8,128)(2,1)}, bf16[384,1536]{1,0:T(8,128)(2,1)}, u32[]{:S(2)}, u32[]{:S(2)}) collective-permute-start(bf16[384,1536]{1,0:T(8,128)(2,1)} %constant_dynamic-slice_fusion.1), channel_id=1, source_target_pairs={{0,2},{2,0},{4,6},{6,4},{8,10},{10,8},{12,14},{14,12},{16,18},{18,... | collective-permute-start | bytes 3538952 | tf_op jit(solution)/shard_map/ppermute | solution.py:98
  149.8 34.7 %collective-permute-start.33 = (bf16[384,1536]{1,0:T(8,128)(2,1)}, bf16[384,1536]{1,0:T(8,128)(2,1)}, u32[]{:S(2)}, u32[]{:S(2)}) collective-permute-start(bf16[384,1536]{1,0:T(8,128)(2,1)} %constant_dynamic-slice_fusion), channel_id=1, source_target_pairs={{0,2},{2,0},{4,6},{6,4},{8,10},{10,8},{12,14},{14,12},{16,18},{18,... | collective-permute-start | bytes 3538952 | tf_op jit(solution)/shard_map/ppermute | solution.py:98
  160.9 66.0 %collective-permute-start.51 = (bf16[384,1536]{1,0:T(8,128)(2,1)S(1)}, bf16[384,1536]{1,0:T(8,128)(2,1)S(1)}, u32[]{:S(2)}, u32[]{:S(2)}) collective-permute-start(bf16[384,1536]{1,0:T(8,128)(2,1)S(1)} %dynamic-slice_bitcast_fusion), channel_id=1, source_target_pairs={{0,2},{2,0},{4,6},{6,4},{8,10},{10,8},{12,14},{14,12},{16,18},{18,... | collective-permute-start | bytes 3538952 | tf_op jit(solution)/shard_map/ppermute | solution.py:98
  177.8 126.2 %collective-permute-start.14 = (f32[34,768]{1,0:T(8,128)S(1)}, f32[34,768]{1,0:T(8,128)S(1)}, u32[]{:S(2)}, u32[]{:S(2)}) collective-permute-start(f32[34,768]{1,0:T(8,128)S(1)} %add.708), channel_id=1, source_target_pairs={{0,16},{2,18},{4,20},{6,22},{8,24},{10,26},{12,28},{14,30},{16,0},... | collective-permute-start | bytes 313352 | tf_op jit(solution)/shard_map/ppermute | solution.py:120
  190.6 10.5 %collective-permute-start.21 = (bf16[48,1536]{1,0:T(8,128)(2,1)S(1)}, bf16[48,1536]{1,0:T(8,128)(2,1)S(1)}, u32[]{:S(2)}, u32[]{:S(2)}) collective-permute-start(bf16[48,1536]{1,0:T(8,128)(2,1)S(1)} %pad_maximum_fusion.1), channel_id=1, source_target_pairs={{8,0},{10,2},{16,8},{18,10},{24,16},{26,18},{28,24},{30,26},{20,28... | collective-permute-start | bytes 442376 | tf_op jit(solution)/shard_map/ppermute | solution.py:50
  194.7 11.8 %collective-permute-start.39 = (bf16[48,1536]{1,0:T(8,128)(2,1)S(1)}, bf16[48,1536]{1,0:T(8,128)(2,1)S(1)}, u32[]{:S(2)}, u32[]{:S(2)}) collective-permute-start(bf16[48,1536]{1,0:T(8,128)(2,1)S(1)} %pad_maximum_fusion.3), channel_id=1, source_target_pairs={{8,0},{10,2},{16,8},{18,10},{24,16},{26,18},{28,24},{30,26},{20,28... | collective-permute-start | bytes 442376 | tf_op jit(solution)/shard_map/ppermute | solution.py:50
  222.5 11.6 %collective-permute-start.25 = (bf16[48,1536]{1,0:T(8,128)(2,1)S(1)}, bf16[48,1536]{1,0:T(8,128)(2,1)S(1)}, u32[]{:S(2)}, u32[]{:S(2)}) collective-permute-start(bf16[48,1536]{1,0:T(8,128)(2,1)S(1)} %get-tuple-element.101), channel_id=1, source_target_pairs={{8,0},{10,2},{16,8},{18,10},{24,16},{26,18},{28,24},{30,26},{20,28... | collective-permute-start | bytes 442376 | tf_op jit(solution)/shard_map/ppermute | solution.py:50
  244.2 14.2 %collective-permute-start.57 = (bf16[48,1536]{1,0:T(8,128)(2,1)S(1)}, bf16[48,1536]{1,0:T(8,128)(2,1)S(1)}, u32[]{:S(2)}, u32[]{:S(2)}) collective-permute-start(bf16[48,1536]{1,0:T(8,128)(2,1)S(1)} %pad_maximum_fusion.5), channel_id=1, source_target_pairs={{8,0},{10,2},{16,8},{18,10},{24,16},{26,18},{28,24},{30,26},{20,28... | collective-permute-start | bytes 442376 | tf_op jit(solution)/shard_map/ppermute | solution.py:50
  250.3 11.8 %collective-permute-start.47 = (bf16[48,1536]{1,0:T(8,128)(2,1)S(1)}, bf16[48,1536]{1,0:T(8,128)(2,1)S(1)}, u32[]{:S(2)}, u32[]{:S(2)}) collective-permute-start(bf16[48,1536]{1,0:T(8,128)(2,1)S(1)} %collective-permute-done.45), channel_id=1, source_target_pairs={{8,0},{10,2},{16,8},{18,10},{24,16},{26,18},{28,24},{30,26},{20,28... | collective-permute-start | bytes 442376 | tf_op jit(solution)/shard_map/ppermute | solution.py:50
  257.6 10.2 %collective-permute-start.31 = (bf16[24,1536]{1,0:T(8,128)(2,1)S(1)}, bf16[24,1536]{1,0:T(8,128)(2,1)S(1)}, u32[]{:S(2)}, u32[]{:S(2)}) collective-permute-start(bf16[24,1536]{1,0:T(8,128)(2,1)S(1)} %slice.727), channel_id=1, source_target_pairs={{0,8},{2,10},{8,16},{10,18},{16,24},{18,26},{24,28},{26,30},{28,20... | collective-permute-start | bytes 221192 | tf_op jit(solution)/shard_map/ppermute | solution.py:47
  258.4 11.1 %collective-permute-start.30 = (bf16[24,1536]{1,0:T(8,128)(2,1)S(1)}, bf16[24,1536]{1,0:T(8,128)(2,1)S(1)}, u32[]{:S(2)}, u32[]{:S(2)}) collective-permute-start(bf16[24,1536]{1,0:T(8,128)(2,1)S(1)} %slice.726), channel_id=1, source_target_pairs={{8,0},{10,2},{16,8},{18,10},{24,16},{26,18},{28,24},{30,26},{20,28... | collective-permute-start | bytes 221192 | tf_op jit(solution)/shard_map/ppermute | solution.py:50
  260.4 16.2 %collective-permute-start.49 = (bf16[24,1536]{1,0:T(8,128)(2,1)S(1)}, bf16[24,1536]{1,0:T(8,128)(2,1)S(1)}, u32[]{:S(2)}, u32[]{:S(2)}) collective-permute-start(bf16[24,1536]{1,0:T(8,128)(2,1)S(1)} %slice.729), channel_id=1, source_target_pairs={{0,8},{2,10},{8,16},{10,18},{16,24},{18,26},{24,28},{26,30},{28,20... | collective-permute-start | bytes 221192 | tf_op jit(solution)/shard_map/ppermute | solution.py:47
  273.0 32.3 %collective-permute-start.32 = (bf16[384,1536]{1,0:T(8,128)(2,1)}, bf16[384,1536]{1,0:T(8,128)(2,1)}, u32[]{:S(2)}, u32[]{:S(2)}) collective-permute-start(bf16[384,1536]{1,0:T(8,128)(2,1)} %bitcast.38), channel_id=1, source_target_pairs={{0,2},{2,0},{4,6},{6,4},{8,10},{10,8},{12,14},{14,12},{16,18},{18,... | collective-permute-start | bytes 3538952 | tf_op jit(solution)/shard_map/ppermute | solution.py:103
  277.3 31.6 %collective-permute-start.50 = (bf16[384,1536]{1,0:T(8,128)(2,1)}, bf16[384,1536]{1,0:T(8,128)(2,1)}, u32[]{:S(2)}, u32[]{:S(2)}) collective-permute-start(bf16[384,1536]{1,0:T(8,128)(2,1)} %bitcast.59), channel_id=1, source_target_pairs={{0,2},{2,0},{4,6},{6,4},{8,10},{10,8},{12,14},{14,12},{16,18},{18,... | collective-permute-start | bytes 3538952 | tf_op jit(solution)/shard_map/ppermute | solution.py:103
  299.0 13.5 %collective-permute-start.68 = (bf16[384,1536]{1,0:T(8,128)(2,1)}, bf16[384,1536]{1,0:T(8,128)(2,1)}, u32[]{:S(2)}, u32[]{:S(2)}) collective-permute-start(bf16[384,1536]{1,0:T(8,128)(2,1)} %bitcast.83), channel_id=1, source_target_pairs={{0,2},{2,0},{4,6},{6,4},{8,10},{10,8},{12,14},{14,12},{16,18},{18,... | collective-permute-start | bytes 3538952 | tf_op jit(solution)/shard_map/ppermute | solution.py:103
  (75 other events, 546.9 us)

commit v2 on v1

--- a/solution.py
+++ b/solution.py
@@ -1,11 +1,596 @@
+import functools
+
 import jax
 import jax.numpy as jnp
 from jax import lax
+from jax.experimental import pallas as pl
+from jax.experimental.pallas import tpu as pltpu
 from jax.sharding import PartitionSpec as P
 
 EPS = 1e-05
 F32 = jnp.float32
 BF16 = jnp.bfloat16
+LANES = 128
+
+
+def dot(left, right, contract):
+    return lax.dot_general(left, right, (contract, ((), ())), preferred_element_type=F32)
+
+
+NT = ((1,), (1,))
+NN = ((1,), (0,))
+TN = ((0,), (0,))
+
+
+def call(body, name, places, grid, ins, outs, args, scratch=(), flops=0):
+    size = sum(a.size * a.dtype.itemsize for a in args)
+    size += sum(s.size * s.dtype.itemsize for s, _ in outs)
+    return pl.pallas_call(
+        body,
+        out_shape=[s for s, _ in outs],
+        grid_spec=pltpu.PrefetchScalarGridSpec(
+            num_scalar_prefetch=1,
+            grid=grid,
+            in_specs=ins,
+            out_specs=[b for _, b in outs],
+            scratch_shapes=list(scratch),
+        ),
+        compiler_params=pltpu.CompilerParams(vmem_limit_bytes=48 * 2**20),
+        cost_estimate=pl.CostEstimate(flops=flops, bytes_accessed=size, transcendentals=0),
+        name=name,
+    )(places, *args)
+
+
+def shape(dims, kind):
+    return jax.ShapeDtypeStruct(dims, kind)
+
+
+def whole(dims):
+    return pl.BlockSpec(dims, lambda i, p: (0,) * len(dims))
+
+
+def lanes(rows, width):
+    return pl.BlockSpec((rows, width), lambda i, p: (0, i))
+
+
+def rows_of(height, cols):
+    return pl.BlockSpec((height, cols), lambda i, p: (i, 0))
+
+
+def d_act_terms(places, cotangent, weight):
+    chans, frames = cotangent.shape
+
+    def body(p, cot, w, theirs, mine, turned):
+        @pl.when(pl.program_id(0) == 0)
+        def _():
+            turned[...] = cot[...].T
+            theirs[...] = dot(turned[...], w[...], NN).astype(BF16)
+
+        @pl.when(pl.program_id(0) == 1)
+        def _():
+            mine[...] = dot(turned[...], w[...], NN).astype(BF16)
+
+    out = (shape((frames, chans), BF16), whole((frames, chans)))
+    return call(
+        body,
+        "d_act_terms",
+        places,
+        (2,),
+        [
+            whole((chans, frames)),
+            pl.BlockSpec((chans, chans), lambda i, p: (0, jnp.where(i == 0, 1 - p[0], p[0]))),
+        ],
+        [out, out],
+        [cotangent, weight],
+        [pltpu.VMEM((frames, chans), BF16)],
+        4 * chans * chans * frames,
+    )
+
+
+def glu_forward(places, mine, theirs, gain_mine, gain_theirs, value_weight, gate_weight):
+    chans, frames = mine.shape
+    width = 2 * chans
+    step = 256
+
+    def body(p, xm, xt, gm, gt, wv, wg, normed, hat, inv, glu, sig, slope, edge):
+        @pl.when(pl.program_id(0) == 0)
+        def _():
+            low = pl.multiple_of(p[0] * chans, LANES)
+            high = pl.multiple_of((1 - p[0]) * chans, LANES)
+            for at in range(0, frames, LANES):
+                some = pl.ds(at, LANES)
+                a = xm[:, some].T.astype(F32)
+                b = xt[:, some].T.astype(F32)
+                total = jnp.sum(a, axis=1, keepdims=True) + jnp.sum(b, axis=1, keepdims=True)
+                mean = total / width
+                a = a - mean
+                b = b - mean
+                spread = jnp.sum(a * a, axis=1, keepdims=True)
+                spread = spread + jnp.sum(b * b, axis=1, keepdims=True)
+                scale = lax.rsqrt(spread / width + EPS)
+                a = a * scale
+                b = b * scale
+                hat[some, :] = a
+                inv[some, :] = jnp.broadcast_to(scale, (LANES, LANES))
+                normed[some, pl.ds(low, chans)] = (a * gm[...]).astype(BF16)
+                normed[some, pl.ds(high, chans)] = (b * gt[...]).astype(BF16)
+
+        value = dot(normed[...], wv[...], NT)
+        gate = dot(normed[...], wg[...], NT)
+        s = jax.nn.sigmoid(gate)
+        g = (value * s).astype(BF16)
+        glu[...] = g
+        edge[0] = g[:16]
+        edge[1] = g[frames - 16 :]
+        sig[...] = s
+        slope[...] = value * s * (1.0 - s)
+
+    block = lanes(frames, step)
+    return call(
+        body,
+        "glu_forward",
+        places,
+        (chans // step,),
+        [whole((chans, frames))] * 2
+        + [whole((1, chans))] * 2
+        + [rows_of(step, width)] * 2,
+        [
+            (shape((frames, width), BF16), whole((frames, width))),
+            (shape((frames, chans), F32), whole((frames, chans))),
+            (shape((frames, LANES), F32), whole((frames, LANES))),
+            (shape((frames, chans), BF16), block),
+            (shape((frames, chans), F32), block),
+            (shape((frames, chans), F32), block),
+            (shape((2, 16, chans), BF16), pl.BlockSpec((2, 16, step), lambda i, p: (0, 0, i))),
+        ],
+        [mine, theirs, gain_mine, gain_theirs, value_weight, gate_weight],
+        (),
+        4 * chans * width * frames,
+    )
+
+
+def fill(wide, before, own, after):
+    frames = own.shape[0]
+    wide[:16, :] = before[...].astype(F32)
+    wide[16 : 16 + frames, :] = own[...].astype(F32)
+    wide[16 + frames :, :] = after[...].astype(F32)
+
+
+def to_rows(first, second):
+    size = first.shape[0]
+    lane = lax.broadcasted_iota(jnp.int32, (size, LANES), 1)
+    both = jnp.where(lane == 0, first, jnp.where(lane == 1, second, 0.0))
+    return both.T[:8]
+
+
+def to_cols(rows):
+    turned = jnp.concatenate([rows] * (LANES // 8)).T
+    return turned[:, 0:1], turned[:, 1:2]
+
+
+STEP = 64
+
+
+def conv_forward(places, before, glu, after, taps):
+    frames, chans = glu.shape
+    blocks = chans // LANES
+
+    def body(p, b, g, a, w, conv, stats, wide):
+        at = pl.program_id(0)
+        fill(wide, b, g, a)
+
+        def chunk(i, carry):
+            start = pl.multiple_of(i * STEP, STEP)
+            total = jnp.zeros((STEP, LANES), F32)
+            for r in range(8):
+                x = wide[pl.ds(start + r, STEP + 24), :]
+                for q in range(4):
+                    tap = 8 * q + r
+                    total = total + w[tap : tap + 1, :] * x[8 * q : 8 * q + STEP]
+            conv[pl.ds(start, STEP), pl.ds(pl.multiple_of(at * LANES, LANES), LANES)] = total
+            return carry
+
+        lax.fori_loop(0, frames // STEP, chunk, 0)
+
+        @pl.when(at == blocks - 1)
+        def _():
+            for low in range(0, frames, LANES):
+                x = conv[low : low + LANES, :]
+                mean = jnp.sum(x, axis=1, keepdims=True) / chans
+                x = x - mean
+                stats[:, low : low + LANES] = to_rows(mean, jnp.sum(x * x, axis=1, keepdims=True))
+
+    return call(
+        body,
+        "conv_forward",
+        places,
+        (blocks,),
+        [lanes(16, LANES), lanes(frames, LANES), lanes(16, LANES), lanes(32, LANES)],
+        [
+            (shape((frames, chans), F32), whole((frames, chans))),
+            (shape((8, frames), F32), whole((8, frames))),
+        ],
+        [before, glu, after, taps],
+        [pltpu.VMEM((frames + 32, LANES), F32)],
+        64 * frames * chans,
+    )
+
+
+def merge(mine, theirs, chans):
+    mean, spread = to_cols(mine)
+    there, more = to_cols(theirs)
+    gap = mean - there
+    whole_spread = spread + more + gap * gap * (chans * 0.5)
+    return (mean + there) * 0.5, lax.rsqrt(whole_spread / (2 * chans) + EPS)
+
+
+def act_step(places, conv, mine, theirs, term, recv, gain):
+    frames, chans = conv.shape
+    height = LANES
+
+    def body(p, x, sm, st, tm, tr, g, act, hat, e, sums, gain_grad):
+        mean, inverse = merge(sm[...], st[...], chans)
+        h = (x[...] - mean) * inverse
+        hat[...] = h
+        scaled = h * g[...]
+        s = jax.nn.sigmoid(scaled)
+        soft = scaled * s
+        act[...] = soft.astype(BF16)
+        d = tm[...].astype(F32) + tr[...].astype(F32)
+        d = d * (s + soft * (1.0 - s))
+
+        @pl.when(pl.program_id(0) == 0)
+        def _():
+            gain_grad[...] = jnp.zeros_like(gain_grad)
+
+        gain_grad[...] += jnp.sum(d * h, axis=0, keepdims=True)
+        d = d * g[...]
+        e[...] = d
+        sums[...] = to_rows(
+            jnp.sum(d, axis=1, keepdims=True), jnp.sum(d * h, axis=1, keepdims=True)
+        )
+
+    some = rows_of(height, chans)
+    line = lanes(8, height)
+    return call(
+        body,
+        "act_step",
+        places,
+        (frames // height,),
+        [some, line, line, some, some, whole((1, chans))],
+        [
+            (shape((frames, chans), BF16), some),
+            (shape((frames, chans), F32), some),
+            (shape((frames, chans), F32), some),
+            (shape((8, frames), F32), line),
+            (shape((1, chans), F32), whole((1, chans))),
+        ],
+        [conv, mine, theirs, term, recv, gain],
+        (),
+        30 * frames * chans,
+    )
+
+
+def d_conv_step(places, e, hat, mine, theirs, sums_mine, sums_theirs):
+    frames, chans = e.shape
+    height = LANES
+    steps = frames // height
+
+    def body(p, d, h, sm, st, um, ut, out, head, tail):
+        _, inverse = merge(sm[...], st[...], chans)
+        first, second = to_cols(um[...] + ut[...])
+        width = 2 * chans
+        got = (d[...] - first / width - h[...] * (second / width)) * inverse
+        got = got.astype(BF16)
+        out[...] = got
+
+        @pl.when(pl.program_id(0) == 0)
+        def _():
+            head[...] = got[:16]
+
+        @pl.when(pl.program_id(0) == steps - 1)
+        def _():
+            tail[...] = got[height - 16 :]
+
+    some = rows_of(height, chans)
+    line = lanes(8, height)
+    rim = (shape((16, chans), BF16), whole((16, chans)))
+    return call(
+        body,
+        "d_conv_step",
+        places,
+        (steps,),
+        [some, some, line, line, line, line],
+        [(shape((frames, chans), BF16), some), rim, rim],
+        [e, hat, mine, theirs, sums_mine, sums_theirs],
+        (),
+        10 * frames * chans,
+    )
+
+
+def d_glu_step(places, before, d_conv, after, taps, sig, slope, own):
+    frames, chans = d_conv.shape
+    blocks = chans // LANES // 2
+
+    def body(p, b, d, a, w, s, h, d_value, d_gate, wide):
+        fill(wide, b, d, a)
+
+        def chunk(i, carry):
+            start = pl.multiple_of(i * STEP, STEP)
+            total = jnp.zeros((STEP, LANES), F32)
+            for r in range(8):
+                x = wide[pl.ds(start + r + 1, STEP + 24), :]
+                for q in range(4):
+                    tap = 31 - (8 * q + r)
+                    total = total + w[tap : tap + 1, :] * x[8 * q : 8 * q + STEP]
+            some = pl.ds(start, STEP)
+            d_value[some, :] = (total * s[some, :]).astype(BF16)
+            d_gate[some, :] = (total * h[some, :]).astype(BF16)
+            return carry
+
+        lax.fori_loop(0, frames // STEP, chunk, 0)
+
+    def pick(height):
+        if own:
+            return pl.BlockSpec((height, LANES), lambda i, p: (0, i + blocks * p[1]))
+        return pl.BlockSpec((height, LANES), lambda i, p: (0, i + blocks * (1 - p[1])))
+
+    out = (shape((frames, chans // 2), BF16), lanes(frames, LANES))
+    return call(
+        body,
+        "d_glu_own" if own else "d_glu_other",
+        places,
+        (blocks,),
+        [pick(16), pick(frames), pick(16), pick(32), pick(frames), pick(frames)],
+        [out, out],
+        [before, d_conv, after, taps, sig, slope],
+        [pltpu.VMEM((frames + 32, LANES), F32)],
+        32 * frames * chans,
+    )
+
+
+def taps_grad(places, before, glu, after, d_conv, scale):
+    frames, chans = glu.shape
+    part = 32
+
+    def body(p, b, g, a, d, out, wide, sums):
+        fill(wide, b, g, a)
+        sums[...] = jnp.zeros_like(sums)
+
+        def chunk(i, carry):
+            start = pl.multiple_of(i * part, part)
+            mine = d[pl.ds(start, part), :].astype(F32)
+            for r in range(8):
+                x = wide[pl.ds(start + r, part + 24), :]
+                for q in range(4):
+                    both = mine * x[8 * q : 8 * q + part]
+                    sums[8 * q + r] += jnp.sum(both.reshape(part // 8, 8, LANES), axis=0)
+            return carry
+
+        lax.fori_loop(0, frames // part, chunk, 0)
+        out[...] = jnp.sum(sums[...], axis=1) * scale
+
+    return call(
+        body,
+        "taps_grad",
+        places,
+        (chans // LANES,),
+        [lanes(16, LANES), lanes(frames, LANES), lanes(16, LANES), lanes(frames, LANES)],
+        [(shape((32, chans), F32), lanes(32, LANES))],
+        [before, glu, after, d_conv],
+        [pltpu.VMEM((frames + 32, LANES), F32), pltpu.VMEM((32, 8, LANES), F32)],
+        64 * frames * chans,
+    )[0]
+
+
+def pair_grads(places, mine, theirs, normed, normed_theirs, scale):
+    frames, half = mine.shape
+    width = normed.shape[1]
+    step = 512
+
+    def body(p, m, t, n, nt, out, turned):
+        @pl.when(pl.program_id(0) == 0)
+        def _():
+            turned[:, :frames] = m[...].T
+            turned[:, frames:] = t[...].T
+
+        total = dot(turned[:, :frames], n[...], NN) + dot(turned[:, frames:], nt[...], NN)
+        out[...] = (total * scale).astype(BF16)
+
+    return call(
+        body,
+        "pair_grads",
+        places,
+        (width // step,),
+        [whole((frames, half))] * 2 + [lanes(frames, step)] * 2,
+        [(shape((half, width), BF16), lanes(half, step))],
+        [mine, theirs, normed, normed_theirs],
+        [pltpu.VMEM((half, 2 * frames), BF16)],
+        4 * half * width * frames,
+    )[0]
+
+
+def out_grads(places, cot, cot_theirs, acts, scale):
+    chans, frames = cot.shape
+    half = chans // 2
+
+    def body(p, c, ct, a, b, a_theirs, b_theirs, out):
+        @pl.when(pl.program_id(0) == 0)
+        def _():
+            total = dot(c[...], a[...], NN) + dot(ct[...], a_theirs[...], NN)
+            out[...] = (total * scale).astype(BF16)
+
+        @pl.when(pl.program_id(0) == 1)
+        def _():
+            total = dot(c[...], b[...], NN) + dot(ct[...], b_theirs[...], NN)
+            out[...] = (total * scale).astype(BF16)
+
+    return call(
+        body,
+        "out_grads",
+        places,
+        (2,),
+        [pl.BlockSpec((half, frames), lambda i, p: (p[1], 0)), whole((half, frames))]
+        + [whole((frames, chans))] * 4,
+        [
+            (
+                shape((half, 2 * chans), BF16),
+                pl.BlockSpec((half, chans), lambda i, p: (0, jnp.where(i == 0, p[0], 1 - p[0]))),
+            )
+        ],
+        [cot, cot_theirs, *acts],
+        (),
+        8 * half * chans * frames,
+    )[0]
+
+
+def d_normed_terms(places, values, gates, value_weight, gate_weight):
+    frames, half = values[0].shape
+    chans = 2 * half
+
+    def body(p, vo, vt, go, gt, wv, wg, theirs, mine):
+        own = pl.ds(pl.multiple_of(p[1] * half, LANES), half)
+        other = pl.ds(pl.multiple_of((1 - p[1]) * half, LANES), half)
+        total = dot(vo[...], wv[own, :], NN) + dot(vt[...], wv[other, :], NN)
+        total = total + dot(go[...], wg[own, :], NN) + dot(gt[...], wg[other, :], NN)
+
+        @pl.when(pl.program_id(0) == 0)
+        def _():
+            theirs[...] = total.astype(BF16)
+
+        @pl.when(pl.program_id(0) == 1)
+        def _():
+            mine[...] = total.astype(BF16)
+
+    out = (shape((frames, chans), BF16), whole((frames, chans)))
+    weight = pl.BlockSpec((chans, chans), lambda i, p: (0, jnp.where(i == 0, 1 - p[0], p[0])))
+    return call(
+        body,
+        "d_normed_terms",
+        places,
+        (2,),
+        [whole((frames, half))] * 4 + [weight] * 2,
+        [out, out],
+        [*values, *gates, value_weight, gate_weight],
+        (),
+        8 * chans * chans * frames,
+    )
+
+
+def norm_sums(places, term, recv, hat, gain):
+    frames, chans = hat.shape
+    height = LANES
+
+    def body(p, tm, tr, h, g, sums, gain_grad):
+        d = tm[...].astype(F32) + tr[...].astype(F32)
+
+        @pl.when(pl.program_id(0) == 0)
+        def _():
+            gain_grad[...] = jnp.zeros_like(gain_grad)
+
+        gain_grad[...] += jnp.sum(d * h[...], axis=0, keepdims=True)
+        d = d * g[...]
+        sums[...] = to_rows(
+            jnp.sum(d, axis=1, keepdims=True), jnp.sum(d * h[...], axis=1, keepdims=True)
+        )
+
+    some = rows_of(height, chans)
+    return call(
+        body,
+        "norm_sums",
+        places,
+        (frames // height,),
+        [some, some, some, whole((1, chans))],
+        [
+            (shape((8, frames), F32), lanes(8, height)),
+            (shape((1, chans), F32), whole((1, chans))),
+        ],
+        [term, recv, hat, gain],
+        (),
+        10 * frames * chans,
+    )
+
+
+def input_step(places, term, recv, hat, gain, inv, mine, theirs, cot):
+    frames, chans = hat.shape
+    height = LANES
+    width = 2 * chans
+
+    def body(p, tm, tr, h, g, i, um, ut, c, out):
+        d = (tm[...].astype(F32) + tr[...].astype(F32)) * g[...]
+        first, second = to_cols(um[...] + ut[...])
+        got = (d - first / width - h[...] * (second / width)) * i[:, 0:1]
+        out[...] = (c[...].astype(F32) + got.T).astype(BF16)
+
+    some = rows_of(height, chans)
+    line = lanes(8, height)
+    return call(
+        body,
+        "input_step",
+        places,
+        (frames // height,),
+        [some, some, some, whole((1, chans)), rows_of(height, LANES), line, line, lanes(chans, height)],
+        [(shape((chans, frames), BF16), lanes(chans, height))],
+        [term, recv, hat, gain, inv, mine, theirs, cot],
+        (),
+        10 * frames * chans,
+    )[0]
+
+
+def out_step(places, frames_in, weight, act, act_theirs):
+    chans, frames = frames_in.shape
+    step = 256
+
+    def body(p, x, w, a, b, out):
+        own = pl.ds(pl.multiple_of(p[0] * chans, LANES), chans)
+        other = pl.ds(pl.multiple_of((1 - p[0]) * chans, LANES), chans)
+        total = dot(w[:, own], a[...], NT) + dot(w[:, other], b[...], NT)
+        out[...] = (x[...].astype(F32) + total).astype(BF16)
+
+    return call(
+        body,
+        "out_step",
+        places,
+        (chans // step,),
+        [rows_of(step, frames), rows_of(step, 2 * chans)] + [whole((frames, chans))] * 2,
+        [(shape((chans, frames), BF16), rows_of(step, frames))],
+        [frames_in, weight, act, act_theirs],
+        (),
+        4 * chans * chans * frames,
+    )[0]
+
+
+def join_halves(places, mine, theirs):
+    half, cols = mine.shape
+    parts = 2
+    step = half // parts
+
+    def body(p, m, t, out):
+        lower = pl.program_id(0) < parts
+
+        @pl.when(lower == (p[1] == 0))
+        def _():
+            out[...] = m[...]
+
+        @pl.when(lower != (p[1] == 0))
+        def _():
+            out[...] = t[...]
+
+    def hold(first, i):
+        return jnp.where(first, jnp.minimum(i, parts - 1), jnp.maximum(i - parts, 0))
+
+    return call(
+        body,
+        "join_halves",
+        places,
+        (2 * parts,),
+        [
+            pl.BlockSpec((step, cols), lambda i, p: (hold(p[1] == 0, i), 0)),
+            pl.BlockSpec((step, cols), lambda i, p: (hold(p[1] == 1, i), 0)),
+        ],
+        [(shape((2 * half, cols), BF16), rows_of(step, cols))],
+        [mine, theirs],
+    )[0]
 
 
 def ring_of(count):
@@ -40,8 +625,14 @@
     spot = jnp.asarray(place, jnp.int32)[lax.axis_index("seq")]
     reach = chips // 2
 
+    def at(step):
+        return (spot + step + chips) % chips
+
     def part(cells, step):
-        return lax.dynamic_index_in_dim(cells, (spot + step + chips) % chips, 0, keepdims=False)
+        return lax.dynamic_index_in_dim(cells, at(step), 0, keepdims=False)
+
+    def put(cells, some, step):
+        return lax.dynamic_update_index_in_dim(cells, some, at(step), 0)
 
     def up(cells):
         return lax.ppermute(cells, "seq", ahead)
@@ -66,18 +657,13 @@
         (part(x, 0).astype(F32) + u.astype(F32) + d.astype(F32)).astype(BF16)
         for x, (u, d) in zip(sets, flows)
     ]
-    outs = []
-    for x, own in zip(sets, owns):
-        outs.append(lax.dynamic_update_index_in_dim(jnp.zeros_like(x), own, spot, 0))
+    outs = [put(x, own, 0) for x, own in zip(sets, owns)]
     flows = [(own, own) for own in owns]
     for hop in range(1, reach):
         flows = [(up(u), down(d)) for u, d in flows]
-        for i, (u, d) in enumerate(flows):
-            out = lax.dynamic_update_index_in_dim(outs[i], u, (spot - hop + chips) % chips, 0)
-            outs[i] = lax.dynamic_update_index_in_dim(out, d, (spot + hop) % chips, 0)
+        outs = [put(put(x, u, -hop), d, hop) for x, (u, d) in zip(outs, flows)]
     for i, (u, d) in enumerate(flows):
-        far = jnp.concatenate([down(d[:half]), up(u[half:])])
-        outs[i] = lax.dynamic_update_index_in_dim(outs[i], far, (spot + reach) % chips, 0)
+        outs[i] = put(outs[i], jnp.concatenate([down(d[:half]), up(u[half:])]), reach)
     return outs
 
 
@@ -179,7 +765,7 @@
     return lax.dot_general(left, right, (((1,), (1,)), ((), ())), preferred_element_type=F32)
 
 
-def local(
+def plain(
     frames_in, norm_gain, value_weight, gate_weight, depth_kernel, conv_gain, out_weight, cotangent
 ):
     chans, row_count = frames_in.shape
@@ -268,6 +854,105 @@
         small[taps],
         grad_out,
     )
+
+
+def core_swap(values):
+    return lax.ppermute(values, "seq", pairs_of(lax.axis_size("seq"), 1))
+
+
+def rims(tail, head):
+    count = lax.axis_size("seq")
+    before = lax.ppermute(tail, "seq", [(i, i + 1) for i in range(count - 1)])
+    after = lax.ppermute(head, "seq", [(i + 1, i) for i in range(count - 1)])
+    return before, after
+
+
+def tied(values, *after):
+    return lax.optimization_barrier((values, *after))[0]
+
+
+def fused(
+    frames_in, norm_gain, value_weight, gate_weight, depth_kernel, conv_gain, out_weight, cotangent
+):
+    chans, frames = frames_in.shape
+    taps = depth_kernel.shape[1]
+    half = chans // 2
+    count = lax.axis_size("seq")
+    scale = float(frames * count) ** (-0.5)
+    core = lax.axis_index("seq") % 2
+    places = jnp.stack([lax.axis_index("tp"), core]).astype(jnp.int32)
+
+    gain = norm_gain[None]
+    gain_theirs = other(gain)
+    frames_theirs = other(frames_in)
+    taps_by = depth_kernel.T
+    cot_theirs = core_swap(lax.dynamic_slice_in_dim(cotangent, (1 - core) * half, half, 0))
+
+    theirs, d_act_mine = d_act_terms(places, cotangent, out_weight)
+    d_act_recv = other(theirs)
+
+    normed, hat_in, inv_in, glu, sig, slope, edge = glu_forward(
+        places, frames_in, frames_theirs, gain, gain_theirs, value_weight, gate_weight
+    )
+    normed_theirs = core_swap(normed)
+    before, after = rims(edge[1], edge[0])
+    conv, stats = conv_forward(places, before, glu, after, taps_by)
+    stats_theirs = other(stats)
+    act, hat_conv, e, sums, gain_grad = act_step(
+        places, conv, stats, stats_theirs, d_act_mine, d_act_recv, conv_gain[None]
+    )
+    sums_theirs = other(sums)
+    act_theirs = other(act)
+    d_conv, head, tail = d_conv_step(places, e, hat_conv, stats, stats_theirs, sums, sums_theirs)
+    d_before, d_after = rims(tail, head)
+    sent_v, sent_g = d_glu_step(places, d_before, d_conv, d_after, taps_by, sig, slope, False)
+    recv_v, recv_g = core_swap(sent_v), core_swap(sent_g)
+    own_v, own_g = d_glu_step(places, d_before, d_conv, d_after, taps_by, sig, slope, True)
+
+    acts = [act, act_theirs, core_swap(act), core_swap(act_theirs)]
+    grad_out = out_grads(places, cotangent, cot_theirs, acts, scale)
+    grad_value = pair_grads(places, own_v, recv_v, normed, normed_theirs, scale)
+    grad_gate = pair_grads(places, own_g, recv_g, normed, normed_theirs, scale)
+
+    chips = count // 2
+    sets = [g.reshape(chips, half // chips, 2 * chans) for g in (grad_out, grad_value, grad_gate)]
+    sums_out = [g.reshape(half, 2 * chans) for g in ring_sum(sets)]
+    swapped = [core_swap(g) for g in sums_out]
+    grad_out, grad_value, grad_gate = [
+        join_halves(places, mine, there) for mine, there in zip(sums_out, swapped)
+    ]
+
+    held = tied(own_v, sets[1])
+    theirs, mine = d_normed_terms(
+        places, [held, sent_v], [own_g, sent_g], value_weight, gate_weight
+    )
+    recv = other(theirs)
+    kernel_grad = taps_grad(places, before, glu, after, tied(d_conv, theirs), scale)
+    block_out = out_step(places, frames_in, out_weight, act, tied(act_theirs, theirs))
+    sums_in, norm_grad = norm_sums(places, mine, recv, hat_in, gain)
+    input_grad = input_step(
+        places, mine, recv, hat_in, gain, inv_in, sums_in, other(sums_in), cotangent
+    )
+    small = small_sum(jnp.concatenate([kernel_grad, gain_grad * scale, norm_grad * scale]))
+    return (
+        block_out,
+        input_grad,
+        small[taps + 1],
+        grad_value,
+        grad_gate,
+        small[:taps].T,
+        small[taps],
+        grad_out,
+    )
+
+
+def local(*arrays):
+    chans, frames = arrays[0].shape
+    taps = arrays[4].shape[1]
+    count = lax.axis_size("seq")
+    fits = lax.axis_size("tp") == 2 and taps == 32 and chans % 256 == 0 and frames % 128 == 0
+    fits = fits and count % 4 == 0 and chans % (16 * count) == 0
+    return (fused if fits else plain)(*arrays)
 
 
 def solution(mesh):

time: 317 us -> 251 us (0.79)
  Pallas kernels: 0 us -> 72 us
  other arithmetic: 62.1 us -> 1.05 us
  local copies, waits for them, and re-layouts: 45.5 us -> 12.8 us
  blocking collectives: 29.2 us -> 0 us
  matrix products: 20.7 us -> 0 us
  waiting for transfers between devices: 69.4 us -> 76.1 us
  between operations: 10.9 us -> 7.42 us
    pallas_call x0 -> x18, Pallas kernels: none -> 72 us  [call(): pl.pallas_call(body, out_shape=[s for s, _ in outs], grid_spec=pltpu.Pref...]
    all_gather x1 -> x0, blocking collectives: 29.2 us -> none  [local(): gain_all = lax.all_gather(norm_gain, 'tp', axis=0, tiled=True)]
    reduce_sum x8 -> x0, other arithmetic: 26.1 us -> none  [the longest x1 8.16 us: local(): mean = jnp.mean(conv, axis=0, keepdims=True)]
    dot_general x9 -> x0, matrix products: 20.7 us -> none  [the longest x3 6.25 us: contract_cols(): lax.dot_general(left, right, (((1,), (1,)), ((), ())), preferred_element_...]
    convert_element_type x6 -> x3, other arithmetic: 16.4 us -> 0.17 us  [ring_sum(): (part(x, 0).astype(F32) + u.astype(F32) + d.astype(F32)).astype(BF16)]
    ppermute x24, waiting for transfers between devices: 24.4 us -> 11 us  [up(): return lax.ppermute(cells, 'seq', ahead)]
    dynamic_update_slice x18 -> x20, local copies, waits for them, and re-layouts: 12.1 us -> 0.29 us  [put(): return lax.dynamic_update_index_in_dim(cells, some, at(step), 0)]
    select_n x3 -> x0, other arithmetic: 11.1 us -> none  [weight_sums(): jnp.where(core == 0, jnp.concatenate([mine, theirs]), jnp.concatenate([th...]
  transfers between devices with their start and end apart: 69 -> 73, of which waited for: 28 -> 29; matrix products, arithmetic and copies ran while one was open for 35% -> 2% of each run, Pallas kernels for 0% -> 28%
where the time goes in v2:
time: 251 us; the launch traced here: 250 us
  starting transfers between devices  81 us (32%)
  waiting for transfers between devices  76.1 us (30%)
  Pallas kernels  72 us (29%)
  local copies, waits for them, and re-layouts  12.8 us (5%)
  between operations  7.42 us (3%)
    pallas_call x18, Pallas kernels, call(): pl.pallas_call(body, out_shape=[s for s, _ in outs], grid_spec=pltpu.Pref...  72 us
    ppermute x24, starting transfers between devices, up(): return lax.ppermute(cells, 'seq', ahead)  33.3 us
    ppermute x8, waiting for transfers between devices, other(): return lax.ppermute(values, 'tp', [(0, 1), (1, 0)])  31.4 us
    ppermute x24, starting transfers between devices, down(): return lax.ppermute(cells, 'seq', behind)  20.9 us
    ppermute x24, waiting for transfers between devices, down(): return lax.ppermute(cells, 'seq', behind)  16.9 us
    ppermute x24, waiting for transfers between devices, up(): return lax.ppermute(cells, 'seq', ahead)  11 us
    ppermute x8, starting transfers between devices, other(): return lax.ppermute(values, 'tp', [(0, 1), (1, 0)])  10.6 us
    ppermute x4, waiting for transfers between devices, small_sum(): values = values + lax.ppermute(values, 'seq', pairs_of(count, step))  10.1 us
  transfers between devices with their start and end apart: 73, of which 29 were waited for; matrix products, arithmetic and copies ran while one was open for 2% of the time, Pallas kernels for 28%

profile of v2, /device:TPU:0, one launch (start us, length us, event | category | flops | bytes accessed | tf_op | source)
XLA Modules:
  0.0 250.4 jit_solution(1227606961523381283)
XLA Ops:
  0.6 3.0 %collective-permute-start = (bf16[768,512]{1,0:T(8,128)(2,1)}, bf16[768,512]{1,0:T(8,128)(2,1)S(1)}, u32[]{:S(2)}, u32[]{:S(2)}) collective-permute-start(bf16[768,512]{1,0:T(8,128)(2,1)} %x.1), channel_id=1, source_target_pairs={{0,1},{1,0},{2,3},{3,2},{4,5},{5,4},{6,7},{7,6},{8,9},{9,8},{10,11... | collective-permute-start | bytes 2359304 | tf_op jit(solution)/shard_map/ppermute | solution.py:712
  11.7 10.6 %collective-permute-done.1.gt = f32[1,768]{1,0:T(1,128)S(1)} collective-permute-done((f32[1,768]{1,0:T(1,128)S(1)}, f32[1,768]{1,0:T(1,128)S(1)}, u32[]{:S(2)}, u32[]{:S(2)}) %collective-permute-start.1) | collective-permute-done | bytes 3104 | tf_op jit(solution)/shard_map/ppermute | solution.py:712
  22.3 8.4 %glu_forward.1 = (bf16[512,1536]{1,0:T(8,128)(2,1)}, f32[512,768]{1,0:T(8,128)S(1)}, f32[512,128]{1,0:T(8,128)S(1)}, bf16[512,768]{1,0:T(8,128)(2,1)S(1)}, f32[5...) custom-call(s32[2]{0:T(128)S(1)} %pad_add_fusion.p, bf16[768,512]{1,0:T(8,128)(2,1)S(1)} %copy-done.13, ...), custom_call_target="tpu_custom_call" | custom-call | flops 2415919104 | bytes 13686784 | tf_op jit(solution)/shard_map/glu_forward/pallas_call | solution.py:28
  35.6 3.0 %collective-permute-done.3.a = bf16[16,768]{1,0:T(8,128)(2,1)S(1)} collective-permute-done((bf16[16,768]{1,0:T(8,128)(2,1)S(1)}, bf16[16,768]{1,0:T(8,128)(2,1)S(1)}, u32[]{:S(2)}, u32[]{:S(2)}) %collective-permute-start.3) | collective-permute-done | bytes 24608 | tf_op jit(solution)/shard_map/ppermute | solution.py:866
  38.6 5.8 %conv_forward.1 = (f32[512,768]{1,0:T(8,128)S(1)}, f32[8,512]{1,0:T(8,128)S(1)}) custom-call(s32[2]{0:T(128)S(1)} %pad_add_fusion.p, bf16[16,768]{1,0:T(8,128)(2,1)S(1)} %collective-permute-done.2.b, bf16[512,768]{1,0:T(8,128)(2,1)S(1)} %get-tuple-element.39.g, bf16[16,768]{1,0:T(8,128)(2,1)S(1)} %collective-permute-done.3.a, f32[32,768]{1,0:T(8,128)S(1)} %bitcast.204), custom_call_target="tpu_custom_call" | custom-call | flops 25165824 | bytes 2523136 | tf_op jit(solution)/shard_map/conv_forward/pallas_call | solution.py:28
  50.2 4.7 %act_step.1 = (bf16[512,768]{1,0:T(8,128)(2,1)}, f32[512,768]{1,0:T(8,128)S(1)}, f32[512,768]{1,0:T(8,128)S(1)}, f32[8,512]{1,0:T(8,128)S(1)}, f32[1,768]{1,0:T(1,128)S(1)}) custom-call(s32[2]{0:T(128)S(1)} %pad_add_fusion.p, f32[512,768]{1,0:T(8,128)} %copy-done.11, f32[8,512]{1,0:T(8,128)S(1)} %get-tuple-element.41.sm, ...), custom_call_target="tpu_custom_call" | custom-call | flops 11796480 | bytes 7133184 | tf_op jit(solution)/shard_map/act_step/pallas_call | solution.py:28
  57.0 18.6 %collective-permute-done.7.ut = f32[8,512]{1,0:T(8,128)S(1)} collective-permute-done((f32[8,512]{1,0:T(8,128)S(1)}, f32[8,512]{1,0:T(8,128)S(1)}, u32[]{:S(2)}, u32[]{:S(2)}) %collective-permute-start.7) | collective-permute-done | bytes 16416 | tf_op jit(solution)/shard_map/ppermute | solution.py:712
  81.1 3.7 %collective-permute-done.9.a = bf16[16,768]{1,0:T(8,128)(2,1)S(1)} collective-permute-done((bf16[16,768]{1,0:T(8,128)(2,1)S(1)}, bf16[16,768]{1,0:T(8,128)(2,1)S(1)}, u32[]{:S(2)}, u32[]{:S(2)}) %collective-permute-start.9) | collective-permute-done | bytes 24608 | tf_op jit(solution)/shard_map/ppermute | solution.py:866
  84.8 3.9 %d_glu_other.1 = (bf16[512,384]{1,0:T(8,128)(2,1)}, bf16[512,384]{1,0:T(8,128)(2,1)S(1)}) custom-call(s32[2]{0:T(128)S(1)} %pad_add_fusion.p, bf16[16,768]{1,0:T(8,128)(2,1)S(1)} %collective-permute-done.8.b, bf16[512,768]{1,0:T(8,128)(2,1)S(1)} %get-tuple-element.65.d, bf16[16,768]{1,0:T(8,128)(2,1)S(1)} %collective-permute-done.9.a, ...), custom_call_target="tpu_custom_call" | custom-call | flops 12582912 | bytes 4866048 | tf_op jit(solution)/shard_map/d_glu_other/pallas_call | solution.py:28
  89.4 2.6 %collective-permute-start.10 = (bf16[512,384]{1,0:T(8,128)(2,1)}, bf16[512,384]{1,0:T(8,128)(2,1)}, u32[]{:S(2)}, u32[]{:S(2)}) collective-permute-start(bf16[512,384]{1,0:T(8,128)(2,1)} %get-tuple-element.54.vt), channel_id=1, source_target_pairs={{0,2},{2,0},{4,6},{6,4},{8,10},{10,8},{12,14},{14,12},{16,18},{18,... | collective-permute-start | bytes 1179656 | tf_op jit(solution)/shard_map/ppermute | solution.py:860
  102.1 3.3 %d_glu_own.1 = (bf16[512,384]{1,0:T(8,128)(2,1)S(1)}, bf16[512,384]{1,0:T(8,128)(2,1)S(1)}) custom-call(s32[2]{0:T(128)S(1)} %pad_add_fusion.p, bf16[16,768]{1,0:T(8,128)(2,1)S(1)} %collective-permute-done.8.b, bf16[512,768]{1,0:T(8,128)(2,1)S(1)} %get-tuple-element.65.d, bf16[16,768]{1,0:T(8,128)(2,1)S(1)} %copy-done.16, f32[32,768]{1,0:T(8,128)S(1)} %bitcast.206, ...), custom_call_target="tpu_custom_call" | custom-call | flops 12582912 | bytes 4866048 | tf_op jit(solution)/shard_map/d_glu_own/pallas_call | solution.py:28
  106.0 4.7 %pair_grads.2 = bf16[384,1536]{1,0:T(8,128)(2,1)S(1)} custom-call(s32[2]{0:T(128)S(1)} %pad_add_fusion.p, bf16[512,384]{1,0:T(8,128)(2,1)S(1)} %get-tuple-element.56.m.vo, bf16[512,384]{1,0:T(8,128)(2,1)} %collective-permute-done.10.t, bf16[512,1536]{1,0:T(8,128)(2,1)} %get-tuple-element.55.n, bf16[512,1536]{1,0:T(8,128)(2,1)} %collective-permute-done.11.nt), custom_call_target="tpu_custom_call" | custom-call | flops 1207959552 | bytes 5111808 | tf_op jit(solution)/shard_map/pair_grads/pallas_call | solution.py:28
  110.8 6.6 %d_normed_terms.1 = (bf16[512,768]{1,0:T(8,128)(2,1)}, bf16[512,768]{1,0:T(8,128)(2,1)S(1)}) custom-call(s32[2]{0:T(128)S(1)} %pad_add_fusion.p, bf16[512,384]{1,0:T(8,128)(2,1)S(1)} %get-tuple-element.56.m.vo, bf16[512,384]{1,0:T(8,128)(2,1)} %get-tuple-element.54.vt, bf16[512,384]{1,0:T(8,128)(2,1)S(1)} %get-tuple-element.57.go.m, ...), custom_call_target="tpu_custom_call" | custom-call | flops 2415919104 | bytes 7864320 | tf_op jit(solution)/shard_map/d_normed_terms/pallas_call | solution.py:28
  118.9 5.3 %taps_grad.1 = f32[32,768]{1,0:T(8,128)S(1)} custom-call(s32[2]{0:T(128)S(1)} %pad_add_fusion.p, bf16[16,768]{1,0:T(8,128)(2,1)S(1)} %copy-done.18, bf16[512,768]{1,0:T(8,128)(2,1)S(1)} %copy-done.8, bf16[16,768]{1,0:T(8,128)(2,1)S(1)} %copy-done.20, bf16[512,768]{1,0:T(8,128)(2,1)S(1)} %get-tuple-element.65.d), custom_call_target="tpu_custom_call" | custom-call | flops 25165824 | bytes 1720320 | tf_op jit(solution)/shard_map/taps_grad/pallas_call | solution.py:28
  125.9 4.4 %pair_grads.3 = bf16[384,1536]{1,0:T(8,128)(2,1)S(1)} custom-call(s32[2]{0:T(128)S(1)} %pad_add_fusion.p, bf16[512,384]{1,0:T(8,128)(2,1)S(1)} %get-tuple-element.57.go.m, bf16[512,384]{1,0:T(8,128)(2,1)S(1)} %collective-permute-done.35.t, bf16[512,1536]{1,0:T(8,128)(2,1)} %get-tuple-element.55.n, bf16[512,1536]{1,0:T(8,128)(2,1)} %collective-permute-done.11.nt), custom_call_target="tpu_custom_call" | custom-call | flops 1207959552 | bytes 5111808 | tf_op jit(solution)/shard_map/pair_grads/pallas_call | solution.py:28
  133.2 3.7 %out_grads.1 = bf16[384,1536]{1,0:T(8,128)(2,1)S(1)} custom-call(s32[2]{0:T(128)S(1)} %pad_add_fusion.p, bf16[768,512]{1,0:T(8,128)(2,1)S(1)} %copy-done.6, bf16[384,512]{1,0:T(8,128)(2,1)} %collective-permute-done.53.ct, bf16[512,768]{1,0:T(8,128)(2,1)} %get-tuple-element.44.a, bf16[512,768]{1,0:T(8,128)(2,1)} %collective-permute-done.6.b, ...), custom_call_target="tpu_custom_call" | custom-call | flops 1207959552 | bytes 5505024 | tf_op jit(solution)/shard_map/out_grads/pallas_call | solution.py:28
  154.0 3.1 %collective-permute-done.20 = bf16[48,1536]{1,0:T(8,128)(2,1)S(1)} collective-permute-done((bf16[48,1536]{1,0:T(8,128)(2,1)S(1)}, bf16[48,1536]{1,0:T(8,128)(2,1)S(1)}, u32[]{:S(2)}, u32[]{:S(2)}) %collective-permute-start.20) | collective-permute-done | bytes 147488 | tf_op jit(solution)/shard_map/ppermute | solution.py:638
  168.4 3.5 %collective-permute-done.62 = bf16[48,1536]{1,0:T(8,128)(2,1)S(1)} collective-permute-done((bf16[48,1536]{1,0:T(8,128)(2,1)S(1)}, bf16[48,1536]{1,0:T(8,128)(2,1)S(1)}, u32[]{:S(2)}, u32[]{:S(2)}) %collective-permute-start.62) | collective-permute-done | bytes 147488 | tf_op jit(solution)/shard_map/ppermute | solution.py:641
  174.8 3.8 %collective-permute-done.25 = bf16[48,1536]{1,0:T(8,128)(2,1)S(1)} collective-permute-done((bf16[48,1536]{1,0:T(8,128)(2,1)S(1)}, bf16[48,1536]{1,0:T(8,128)(2,1)S(1)}, u32[]{:S(2)}, u32[]{:S(2)}) %collective-permute-start.25) | collective-permute-done | bytes 147488 | tf_op jit(solution)/shard_map/ppermute | solution.py:641
  222.1 4.4 %collective-permute-done.15 = f32[34,768]{1,0:T(8,128)S(1)} collective-permute-done((f32[34,768]{1,0:T(8,128)S(1)}, f32[34,768]{1,0:T(8,128)S(1)}, u32[]{:S(2)}, u32[]{:S(2)}) %collective-permute-start.15) | collective-permute-done | bytes 104480 | tf_op jit(solution)/shard_map/ppermute | solution.py:706
  228.2 3.3 %collective-permute-done.16 = f32[34,768]{1,0:T(8,128)S(1)} collective-permute-done((f32[34,768]{1,0:T(8,128)S(1)}, f32[34,768]{1,0:T(8,128)S(1)}, u32[]{:S(2)}, u32[]{:S(2)}) %collective-permute-start.16) | collective-permute-done | bytes 104480 | tf_op jit(solution)/shard_map/ppermute | solution.py:706
  231.5 2.5 collective-permute-start.17
  234.0 4.5 %out_step.1 = bf16[768,512]{1,0:T(8,128)(2,1)} custom-call(s32[2]{0:T(128)S(1)} %pad_add_fusion.p, bf16[768,512]{1,0:T(8,128)(2,1)S(1)} %copy-done.14, bf16[768,1536]{1,0:T(8,128)(2,1)S(1)} %copy-done.10, bf16[512,768]{1,0:T(8,128)(2,1)} %get-tuple-element.44.a, bf16[512,768]{1,0:T(8,128)(2,1)} %collective-permute-done.6.b), custom_call_target="tpu_custom_call" | custom-call | flops 1207959552 | bytes 5505024 | tf_op jit(solution)/shard_map/out_step/pallas_call | solution.py:28
  238.5 3.2 %input_step.1 = bf16[768,512]{1,0:T(8,128)(2,1)} custom-call(s32[2]{0:T(128)S(1)} %pad_add_fusion.p, bf16[512,768]{1,0:T(8,128)(2,1)S(1)} %get-tuple-element.61.tm, bf16[512,768]{1,0:T(8,128)(2,1)S(1)} %collective-permute-done.12.tr, f32[512,768]{1,0:T(8,128)S(1)} %copy-done.4, f32[1,768]{1,0:T(1,128)S(1)} %broadcast_in_dim.79.gm.g, ...), custom_call_target="tpu_custom_call" | custom-call | flops 3932160 | bytes 5016576 | tf_op jit(solution)/shard_map/input_step/pallas_call | solution.py:28
  (260 shorter events, 122.3 us)
Async XLA Ops:
  0.6 21.7 %collective-permute-start = (bf16[768,512]{1,0:T(8,128)(2,1)}, bf16[768,512]{1,0:T(8,128)(2,1)S(1)}, u32[]{:S(2)}, u32[]{:S(2)}) collective-permute-start(bf16[768,512]{1,0:T(8,128)(2,1)} %x.1), channel_id=1, source_target_pairs={{0,1},{1,0},{2,3},{3,2},{4,5},{5,4},{6,7},{7,6},{8,9},{9,8},{10,11... | collective-permute-start | bytes 2359304 | tf_op jit(solution)/shard_map/ppermute | solution.py:712
  4.3 18.0 %collective-permute-start.1 = (f32[1,768]{1,0:T(1,128)S(1)}, f32[1,768]{1,0:T(1,128)S(1)}, u32[]{:S(2)}, u32[]{:S(2)}) collective-permute-start(f32[1,768]{1,0:T(1,128)S(1)} %broadcast_in_dim.79.gm.g), channel_id=1, source_target_pairs={{0,1},{1,0},{2,3},{3,2},{4,5},{5,4},{6,7},{7,6},{8,9},{9,8},{10,11... | collective-permute-start | bytes 9224 | tf_op jit(solution)/shard_map/ppermute | solution.py:712
  9.6 38.4 %collective-permute-start.5 = (bf16[512,768]{1,0:T(8,128)(2,1)S(1)}, bf16[512,768]{1,0:T(8,128)(2,1)S(1)}, u32[]{:S(2)}, u32[]{:S(2)}) collective-permute-start(bf16[512,768]{1,0:T(8,128)(2,1)S(1)} %get-tuple-element.43), channel_id=1, source_target_pairs={{0,1},{1,0},{2,3},{3,2},{4,5},{5,4},{6,7},{7,6},{8,9},{9,8},{10,11... | collective-permute-start | bytes 2359304 | tf_op jit(solution)/shard_map/ppermute | solution.py:712
  31.8 74.2 %collective-permute-start.11 = (bf16[512,1536]{1,0:T(8,128)(2,1)}, bf16[512,1536]{1,0:T(8,128)(2,1)}, u32[]{:S(2)}, u32[]{:S(2)}) collective-permute-start(bf16[512,1536]{1,0:T(8,128)(2,1)} %get-tuple-element.55.n), channel_id=1, source_target_pairs={{0,2},{2,0},{4,6},{6,4},{8,10},{10,8},{12,14},{14,12},{16,18},{18,... | collective-permute-start | bytes 4718600 | tf_op jit(solution)/shard_map/ppermute | solution.py:860
  55.0 50.5 %collective-permute-start.6 = (bf16[512,768]{1,0:T(8,128)(2,1)}, bf16[512,768]{1,0:T(8,128)(2,1)}, u32[]{:S(2)}, u32[]{:S(2)}) collective-permute-start(bf16[512,768]{1,0:T(8,128)(2,1)} %get-tuple-element.44.a), channel_id=1, source_target_pairs={{0,1},{1,0},{2,3},{3,2},{4,5},{5,4},{6,7},{7,6},{8,9},{9,8},{10,11... | collective-permute-start | bytes 2359304 | tf_op jit(solution)/shard_map/ppermute | solution.py:712
  56.5 19.1 %collective-permute-start.7 = (f32[8,512]{1,0:T(8,128)S(1)}, f32[8,512]{1,0:T(8,128)S(1)}, u32[]{:S(2)}, u32[]{:S(2)}) collective-permute-start(f32[8,512]{1,0:T(8,128)S(1)} %get-tuple-element.47.um), channel_id=1, source_target_pairs={{0,1},{1,0},{2,3},{3,2},{4,5},{5,4},{6,7},{7,6},{8,9},{9,8},{10,11... | collective-permute-start | bytes 49160 | tf_op jit(solution)/shard_map/ppermute | solution.py:712
  89.4 16.0 %collective-permute-start.10 = (bf16[512,384]{1,0:T(8,128)(2,1)}, bf16[512,384]{1,0:T(8,128)(2,1)}, u32[]{:S(2)}, u32[]{:S(2)}) collective-permute-start(bf16[512,384]{1,0:T(8,128)(2,1)} %get-tuple-element.54.vt), channel_id=1, source_target_pairs={{0,2},{2,0},{4,6},{6,4},{8,10},{10,8},{12,14},{14,12},{16,18},{18,... | collective-permute-start | bytes 1179656 | tf_op jit(solution)/shard_map/ppermute | solution.py:860
  92.8 37.6 %collective-permute-start.53 = (bf16[384,512]{1,0:T(8,128)(2,1)}, bf16[384,512]{1,0:T(8,128)(2,1)}, u32[]{:S(2)}, u32[]{:S(2)}) collective-permute-start(bf16[384,512]{1,0:T(8,128)(2,1)} %constant_dynamic-slice_fusion), channel_id=1, source_target_pairs={{0,2},{2,0},{4,6},{6,4},{8,10},{10,8},{12,14},{14,12},{16,18},{18,... | collective-permute-start | bytes 1179656 | tf_op jit(solution)/shard_map/ppermute | solution.py:860
  99.3 31.8 %collective-permute-start.54 = (bf16[512,768]{1,0:T(8,128)(2,1)}, bf16[512,768]{1,0:T(8,128)(2,1)S(1)}, u32[]{:S(2)}, u32[]{:S(2)}) collective-permute-start(bf16[512,768]{1,0:T(8,128)(2,1)} %get-tuple-element.44.a), channel_id=1, source_target_pairs={{0,2},{2,0},{4,6},{6,4},{8,10},{10,8},{12,14},{14,12},{16,18},{18,... | collective-permute-start | bytes 2359304 | tf_op jit(solution)/shard_map/ppermute | solution.py:860
  105.4 18.8 %collective-permute-start.35 = (bf16[512,384]{1,0:T(8,128)(2,1)S(1)}, bf16[512,384]{1,0:T(8,128)(2,1)S(1)}, u32[]{:S(2)}, u32[]{:S(2)}) collective-permute-start(bf16[512,384]{1,0:T(8,128)(2,1)S(1)} %copy-done.23), channel_id=1, source_target_pairs={{0,2},{2,0},{4,6},{6,4},{8,10},{10,8},{12,14},{14,12},{16,18},{18,... | collective-permute-start | bytes 1179656 | tf_op jit(solution)/shard_map/ppermute | solution.py:860
  105.5 27.0 %collective-permute-start.55 = (bf16[512,768]{1,0:T(8,128)(2,1)}, bf16[512,768]{1,0:T(8,128)(2,1)S(1)}, u32[]{:S(2)}, u32[]{:S(2)}) collective-permute-start(bf16[512,768]{1,0:T(8,128)(2,1)} %collective-permute-done.6.b), channel_id=1, source_target_pairs={{0,2},{2,0},{4,6},{6,4},{8,10},{10,8},{12,14},{14,12},{16,18},{18,... | collective-permute-start | bytes 2359304 | tf_op jit(solution)/shard_map/ppermute | solution.py:860
  117.4 68.9 %collective-permute-start.12 = (bf16[512,768]{1,0:T(8,128)(2,1)}, bf16[512,768]{1,0:T(8,128)(2,1)S(1)}, u32[]{:S(2)}, u32[]{:S(2)}) collective-permute-start(bf16[512,768]{1,0:T(8,128)(2,1)} %get-tuple-element.59), channel_id=1, source_target_pairs={{0,1},{1,0},{2,3},{3,2},{4,5},{5,4},{6,7},{7,6},{8,9},{9,8},{10,11... | collective-permute-start | bytes 2359304 | tf_op jit(solution)/shard_map/ppermute | solution.py:712
  124.3 12.7 %collective-permute-start.18 = (bf16[24,1536]{1,0:T(8,128)(2,1)S(1)}, bf16[24,1536]{1,0:T(8,128)(2,1)S(1)}, u32[]{:S(2)}, u32[]{:S(2)}) collective-permute-start(bf16[24,1536]{1,0:T(8,128)(2,1)S(1)} %get-tuple-element.91), channel_id=1, source_target_pairs={{0,8},{2,10},{8,16},{10,18},{16,24},{18,26},{24,28},{26,30},{28,20... | collective-permute-start | bytes 221192 | tf_op jit(solution)/shard_map/ppermute | solution.py:638
  140.5 11.8 %collective-permute-start.23 = (bf16[48,1536]{1,0:T(8,128)(2,1)S(1)}, bf16[48,1536]{1,0:T(8,128)(2,1)S(1)}, u32[]{:S(2)}, u32[]{:S(2)}) collective-permute-start(bf16[48,1536]{1,0:T(8,128)(2,1)S(1)} %pad_maximum_fusion.1), channel_id=1, source_target_pairs={{8,0},{10,2},{16,8},{18,10},{24,16},{26,18},{28,24},{30,26},{20,28... | collective-permute-start | bytes 442376 | tf_op jit(solution)/shard_map/ppermute | solution.py:641
  143.5 14.9 %collective-permute-start.41 = (bf16[48,1536]{1,0:T(8,128)(2,1)S(1)}, bf16[48,1536]{1,0:T(8,128)(2,1)S(1)}, u32[]{:S(2)}, u32[]{:S(2)}) collective-permute-start(bf16[48,1536]{1,0:T(8,128)(2,1)S(1)} %pad_maximum_fusion.3), channel_id=1, source_target_pairs={{8,0},{10,2},{16,8},{18,10},{24,16},{26,18},{28,24},{30,26},{20,28... | collective-permute-start | bytes 442376 | tf_op jit(solution)/shard_map/ppermute | solution.py:641
  149.1 12.5 %collective-permute-start.61 = (bf16[48,1536]{1,0:T(8,128)(2,1)S(1)}, bf16[48,1536]{1,0:T(8,128)(2,1)S(1)}, u32[]{:S(2)}, u32[]{:S(2)}) collective-permute-start(bf16[48,1536]{1,0:T(8,128)(2,1)S(1)} %pad_maximum_fusion.5), channel_id=1, source_target_pairs={{8,0},{10,2},{16,8},{18,10},{24,16},{26,18},{28,24},{30,26},{20,28... | collective-permute-start | bytes 442376 | tf_op jit(solution)/shard_map/ppermute | solution.py:641
  160.3 12.5 %collective-permute-start.21 = (bf16[48,1536]{1,0:T(8,128)(2,1)S(1)}, bf16[48,1536]{1,0:T(8,128)(2,1)S(1)}, u32[]{:S(2)}, u32[]{:S(2)}) collective-permute-start(bf16[48,1536]{1,0:T(8,128)(2,1)S(1)} %get-tuple-element.86), channel_id=1, source_target_pairs={{0,8},{2,10},{8,16},{10,18},{16,24},{18,26},{24,28},{26,30},{28,20... | collective-permute-start | bytes 442376 | tf_op jit(solution)/shard_map/ppermute | solution.py:638
  163.9 15.6 %collective-permute-start.39 = (bf16[48,1536]{1,0:T(8,128)(2,1)S(1)}, bf16[48,1536]{1,0:T(8,128)(2,1)S(1)}, u32[]{:S(2)}, u32[]{:S(2)}) collective-permute-start(bf16[48,1536]{1,0:T(8,128)(2,1)S(1)} %get-tuple-element.78), channel_id=1, source_target_pairs={{0,8},{2,10},{8,16},{10,18},{16,24},{18,26},{24,28},{26,30},{28,20... | collective-permute-start | bytes 442376 | tf_op jit(solution)/shard_map/ppermute | solution.py:638
  166.8 15.9 %collective-permute-start.59 = (bf16[48,1536]{1,0:T(8,128)(2,1)S(1)}, bf16[48,1536]{1,0:T(8,128)(2,1)S(1)}, u32[]{:S(2)}, u32[]{:S(2)}) collective-permute-start(bf16[48,1536]{1,0:T(8,128)(2,1)S(1)} %get-tuple-element.70), channel_id=1, source_target_pairs={{0,8},{2,10},{8,16},{10,18},{16,24},{18,26},{24,28},{26,30},{28,20... | collective-permute-start | bytes 442376 | tf_op jit(solution)/shard_map/ppermute | solution.py:638
  214.0 28.9 %collective-permute-start.34 = (bf16[384,1536]{1,0:T(8,128)(2,1)S(1)}, bf16[384,1536]{1,0:T(8,128)(2,1)S(1)}, u32[]{:S(2)}, u32[]{:S(2)}) collective-permute-start(bf16[384,1536]{1,0:T(8,128)(2,1)S(1)} %bitcast.184), channel_id=1, source_target_pairs={{0,2},{2,0},{4,6},{6,4},{8,10},{10,8},{12,14},{14,12},{16,18},{18,... | collective-permute-start | bytes 3538952 | tf_op jit(solution)/shard_map/ppermute | solution.py:860
  215.7 29.7 %collective-permute-start.52 = (bf16[384,1536]{1,0:T(8,128)(2,1)S(1)}, bf16[384,1536]{1,0:T(8,128)(2,1)S(1)}, u32[]{:S(2)}, u32[]{:S(2)}) collective-permute-start(bf16[384,1536]{1,0:T(8,128)(2,1)S(1)} %bitcast.193), channel_id=1, source_target_pairs={{0,2},{2,0},{4,6},{6,4},{8,10},{10,8},{12,14},{14,12},{16,18},{18,... | collective-permute-start | bytes 3538952 | tf_op jit(solution)/shard_map/ppermute | solution.py:860
  218.0 30.0 %collective-permute-start.72 = (bf16[384,1536]{1,0:T(8,128)(2,1)S(1)}, bf16[384,1536]{1,0:T(8,128)(2,1)S(1)}, u32[]{:S(2)}, u32[]{:S(2)}) collective-permute-start(bf16[384,1536]{1,0:T(8,128)(2,1)S(1)} %bitcast.202), channel_id=1, source_target_pairs={{0,2},{2,0},{4,6},{6,4},{8,10},{10,8},{12,14},{14,12},{16,18},{18,... | collective-permute-start | bytes 3538952 | tf_op jit(solution)/shard_map/ppermute | solution.py:860
  227.6 10.9 %collective-permute-start.13 = (f32[8,512]{1,0:T(8,128)S(1)}, f32[8,512]{1,0:T(8,128)S(1)}, u32[]{:S(2)}, u32[]{:S(2)}) collective-permute-start(f32[8,512]{1,0:T(8,128)S(1)} %get-tuple-element.64.um), channel_id=1, source_target_pairs={{0,1},{1,0},{2,3},{3,2},{4,5},{5,4},{6,7},{7,6},{8,9},{9,8},{10,11... | collective-permute-start | bytes 49160 | tf_op jit(solution)/shard_map/ppermute | solution.py:712
  231.5 10.2 %collective-permute-start.17 = (f32[34,768]{1,0:T(8,128)S(1)}, f32[34,768]{1,0:T(8,128)S(1)}, u32[]{:S(2)}, u32[]{:S(2)}) collective-permute-start(f32[34,768]{1,0:T(8,128)S(1)} %add.394), channel_id=1, source_target_pairs={{0,16},{2,18},{4,20},{6,22},{8,24},{10,26},{12,28},{14,30},{16,0},... | collective-permute-start | bytes 313352 | tf_op jit(solution)/shard_map/ppermute | solution.py:706
  (75 other events, 559.5 us)

commit v3 on v2

--- a/solution.py
+++ b/solution.py
@@ -22,9 +22,7 @@
 TN = ((0,), (0,))
 
 
-def call(body, name, places, grid, ins, outs, args, scratch=(), flops=0):
-    size = sum(a.size * a.dtype.itemsize for a in args)
-    size += sum(s.size * s.dtype.itemsize for s, _ in outs)
+def call(body, name, places, grid, ins, outs, args, scratch=(), flops=0, aliases=()):
     return pl.pallas_call(
         body,
         out_shape=[s for s, _ in outs],
@@ -35,8 +33,9 @@
             out_specs=[b for _, b in outs],
             scratch_shapes=list(scratch),
         ),
-        compiler_params=pltpu.CompilerParams(vmem_limit_bytes=48 * 2**20),
-        cost_estimate=pl.CostEstimate(flops=flops, bytes_accessed=size, transcendentals=0),
+        compiler_params=pltpu.CompilerParams(vmem_limit_bytes=24 * 2**20),
+        cost_estimate=pl.CostEstimate(flops=1000, bytes_accessed=1000, transcendentals=0),
+        input_output_aliases=dict(aliases),
         name=name,
     )(places, *args)
 
@@ -87,20 +86,73 @@
     )
 
 
-def glu_forward(places, mine, theirs, gain_mine, gain_theirs, value_weight, gate_weight):
-    chans, frames = mine.shape
+def edges_first(index, count):
+    quarter = count // 4
+    inner = jnp.where(index < 2 * quarter, index + 2 * quarter, index - quarter)
+    return jnp.where(index < quarter, index, inner)
+
+
+def pack_edges(places, frames_in, gain):
+    chans, frames = frames_in.shape
+    quarter = frames // 4
+
+    def body(p, first, last, g, out):
+        out[:chans, :quarter] = first[...]
+        out[:chans, quarter:] = last[...]
+        out[chans:, :] = jnp.zeros_like(out[chans:, :])
+        rest = g[...]
+        rows = []
+        for _ in range(3):
+            term = rest.astype(BF16).astype(F32)
+            rest = rest - term
+            rows += [term[:, at : at + 2 * quarter] for at in range(0, chans, 2 * quarter)]
+        rows.append(jnp.zeros((16 - len(rows), 2 * quarter), F32))
+        out[chans:, :] = jnp.concatenate(rows).astype(BF16)
+
+    return call(
+        body,
+        "pack_edges",
+        places,
+        (1,),
+        [
+            pl.BlockSpec((chans, quarter), lambda i, p: (0, 0)),
+            pl.BlockSpec((chans, quarter), lambda i, p: (0, 3)),
+            whole((1, chans)),
+        ],
+        [(shape((chans + 16, 2 * quarter), BF16), whole((chans + 16, 2 * quarter)))],
+        [frames_in, frames_in, gain],
+    )[0]
+
+
+def glu_forward(places, mine, theirs, gain, packed, weights, held):
+    chans, frames = mine.shape[0] // 16 * 16, mine.shape[1]
+    if not held:
+        chans = chans - 16
     width = 2 * chans
     step = 256
-
-    def body(p, xm, xt, gm, gt, wv, wg, normed, hat, inv, glu, sig, slope, edge):
+    half = 1 if held else 0
+
+    def body(p, xm, xt, gm, gt, wv, wg, *refs):
+        normed, hat, inv, glu, sig, slope, edge = refs[len(held) :]
+
         @pl.when(pl.program_id(0) == 0)
         def _():
             low = pl.multiple_of(p[0] * chans, LANES)
             high = pl.multiple_of((1 - p[0]) * chans, LANES)
+            terms = gt[...].astype(F32)
+            count = chans // frames
+            gain_theirs = jnp.concatenate(
+                [
+                    terms[k : k + 1] + terms[count + k : count + k + 1]
+                    + terms[2 * count + k : 2 * count + k + 1]
+                    for k in range(count)
+                ],
+                axis=1,
+            )
             for at in range(0, frames, LANES):
                 some = pl.ds(at, LANES)
-                a = xm[:, some].T.astype(F32)
-                b = xt[:, some].T.astype(F32)
+                a = xm[:chans, some].T.astype(F32)
+                b = xt[:chans, some].T.astype(F32)
                 total = jnp.sum(a, axis=1, keepdims=True) + jnp.sum(b, axis=1, keepdims=True)
                 mean = total / width
                 a = a - mean
@@ -113,7 +165,7 @@
                 hat[some, :] = a
                 inv[some, :] = jnp.broadcast_to(scale, (LANES, LANES))
                 normed[some, pl.ds(low, chans)] = (a * gm[...]).astype(BF16)
-                normed[some, pl.ds(high, chans)] = (b * gt[...]).astype(BF16)
+                normed[some, pl.ds(high, chans)] = (b * gain_theirs).astype(BF16)
 
         value = dot(normed[...], wv[...], NT)
         gate = dot(normed[...], wg[...], NT)
@@ -125,28 +177,44 @@
         sig[...] = s
         slope[...] = value * s * (1.0 - s)
 
-    block = lanes(frames, step)
-    return call(
-        body,
-        "glu_forward",
+    block = pl.BlockSpec((frames, step), lambda i, p: (half, i))
+
+    def full(cols):
+        return pl.BlockSpec((frames, cols), lambda i, p: (half, 0))
+
+    return call(
+        body,
+        "glu_middle" if held else "glu_edges",
         places,
         (chans // step,),
-        [whole((chans, frames))] * 2
-        + [whole((1, chans))] * 2
-        + [rows_of(step, width)] * 2,
+        [whole(mine.shape)] * 2
+        + [whole((1, chans)), pl.BlockSpec((16, frames), lambda i, p: (chans // 16, 0))]
+        + [rows_of(step, width)] * 2
+        + [pl.BlockSpec(memory_space=pl.ANY)] * len(held),
         [
-            (shape((frames, width), BF16), whole((frames, width))),
-            (shape((frames, chans), F32), whole((frames, chans))),
-            (shape((frames, LANES), F32), whole((frames, LANES))),
-            (shape((frames, chans), BF16), block),
-            (shape((frames, chans), F32), block),
-            (shape((frames, chans), F32), block),
+            (shape((2 * frames, width), BF16), full(width)),
+            (shape((2 * frames, chans), F32), full(chans)),
+            (shape((2 * frames, LANES), F32), full(LANES)),
+            (shape((2 * frames, chans), BF16), block),
+            (shape((2 * frames, chans), F32), block),
+            (shape((2 * frames, chans), F32), block),
             (shape((2, 16, chans), BF16), pl.BlockSpec((2, 16, step), lambda i, p: (0, 0, i))),
         ],
-        [mine, theirs, gain_mine, gain_theirs, value_weight, gate_weight],
+        [mine, theirs, gain, packed, *weights, *held],
         (),
         4 * chans * width * frames,
-    )
+        [(7 + i, i) for i in range(len(held))],
+    )
+
+
+def fill_edges_first(wide, before, own, after):
+    frames = own.shape[0]
+    quarter = frames // 4
+    wide[:16, :] = before[...].astype(F32)
+    wide[16 : 16 + quarter, :] = own[:quarter, :].astype(F32)
+    wide[16 + quarter : 16 + 3 * quarter, :] = own[2 * quarter :, :].astype(F32)
+    wide[16 + 3 * quarter : 16 + frames, :] = own[quarter : 2 * quarter, :].astype(F32)
+    wide[16 + frames :, :] = after[...].astype(F32)
 
 
 def fill(wide, before, own, after):
@@ -177,7 +245,7 @@
 
     def body(p, b, g, a, w, conv, stats, wide):
         at = pl.program_id(0)
-        fill(wide, b, g, a)
+        fill_edges_first(wide, b, g, a)
 
         def chunk(i, carry):
             start = pl.multiple_of(i * STEP, STEP)
@@ -228,14 +296,13 @@
     frames, chans = conv.shape
     height = LANES
 
-    def body(p, x, sm, st, tm, tr, g, act, hat, e, sums, gain_grad):
+    def body(p, x, sm, st, tm, tr, g, hat, e, sums, gain_grad):
         mean, inverse = merge(sm[...], st[...], chans)
         h = (x[...] - mean) * inverse
         hat[...] = h
         scaled = h * g[...]
         s = jax.nn.sigmoid(scaled)
         soft = scaled * s
-        act[...] = soft.astype(BF16)
         d = tm[...].astype(F32) + tr[...].astype(F32)
         d = d * (s + soft * (1.0 - s))
 
@@ -259,7 +326,6 @@
         (frames // height,),
         [some, line, line, some, some, whole((1, chans))],
         [
-            (shape((frames, chans), BF16), some),
             (shape((frames, chans), F32), some),
             (shape((frames, chans), F32), some),
             (shape((8, frames), F32), line),
@@ -271,18 +337,20 @@
     )
 
 
-def d_conv_step(places, e, hat, mine, theirs, sums_mine, sums_theirs):
+def d_conv_step(places, e, hat, gain, mine, theirs, sums_mine, sums_theirs):
     frames, chans = e.shape
     height = LANES
     steps = frames // height
 
-    def body(p, d, h, sm, st, um, ut, out, head, tail):
+    def body(p, d, h, g, sm, st, um, ut, out, act, head, tail):
         _, inverse = merge(sm[...], st[...], chans)
         first, second = to_cols(um[...] + ut[...])
         width = 2 * chans
         got = (d[...] - first / width - h[...] * (second / width)) * inverse
         got = got.astype(BF16)
         out[...] = got
+        scaled = h[...] * g[...]
+        act[...] = (scaled * jax.nn.sigmoid(scaled)).astype(BF16)
 
         @pl.when(pl.program_id(0) == 0)
         def _():
@@ -300,9 +368,9 @@
         "d_conv_step",
         places,
         (steps,),
-        [some, some, line, line, line, line],
-        [(shape((frames, chans), BF16), some), rim, rim],
-        [e, hat, mine, theirs, sums_mine, sums_theirs],
+        [some, some, whole((1, chans)), line, line, line, line],
+        [(shape((frames, chans), BF16), some)] * 2 + [rim, rim],
+        [e, hat, gain, mine, theirs, sums_mine, sums_theirs],
         (),
         10 * frames * chans,
     )
@@ -323,7 +391,10 @@
                 for q in range(4):
                     tap = 31 - (8 * q + r)
                     total = total + w[tap : tap + 1, :] * x[8 * q : 8 * q + STEP]
-            some = pl.ds(start, STEP)
+            quarter = frames // 4
+            inner = jnp.where(start < 3 * quarter, start + quarter, start - 2 * quarter)
+            there = jnp.where(start < quarter, start, inner)
+            some = pl.ds(pl.multiple_of(there, STEP), STEP)
             d_value[some, :] = (total * s[some, :]).astype(BF16)
             d_gate[some, :] = (total * h[some, :]).astype(BF16)
             return carry
@@ -354,7 +425,7 @@
     part = 32
 
     def body(p, b, g, a, d, out, wide, sums):
-        fill(wide, b, g, a)
+        fill_edges_first(wide, b, g, a)
         sums[...] = jnp.zeros_like(sums)
 
         def chunk(i, carry):
@@ -383,30 +454,34 @@
     )[0]
 
 
-def pair_grads(places, mine, theirs, normed, normed_theirs, scale):
-    frames, half = mine.shape
+def pair_grads(places, chips, mine, theirs, normed, normed_theirs, scale):
+    frames, half = mine[0].shape
     width = normed.shape[1]
     step = 512
 
-    def body(p, m, t, n, nt, out, turned):
+    def body(p, mv, mg, tv, tg, n, nt, out, turned):
         @pl.when(pl.program_id(0) == 0)
         def _():
-            turned[:, :frames] = m[...].T
-            turned[:, frames:] = t[...].T
-
-        total = dot(turned[:, :frames], n[...], NN) + dot(turned[:, frames:], nt[...], NN)
-        out[...] = (total * scale).astype(BF16)
-
+            for k, (m, t) in enumerate(((mv, tv), (mg, tg))):
+                turned[k, :, :frames] = m[...].T
+                turned[k, :, frames:] = t[...].T
+
+        for k in range(2):
+            total = dot(turned[k, :, :frames], n[...], NN)
+            total = total + dot(turned[k, :, frames:], nt[...], NN)
+            out[:, k] = (total * scale).astype(BF16).reshape(chips, half // chips, step)
+
+    dims = (chips, 2, half // chips)
     return call(
         body,
         "pair_grads",
         places,
         (width // step,),
-        [whole((frames, half))] * 2 + [lanes(frames, step)] * 2,
-        [(shape((half, width), BF16), lanes(half, step))],
-        [mine, theirs, normed, normed_theirs],
-        [pltpu.VMEM((half, 2 * frames), BF16)],
-        4 * half * width * frames,
+        [whole((frames, half))] * 4 + [lanes(frames, step)] * 2,
+        [(shape((*dims, width), BF16), pl.BlockSpec((*dims, step), lambda i, p: (0, 0, 0, i)))],
+        [*mine, *theirs, normed, normed_theirs],
+        [pltpu.VMEM((2, half, 2 * frames), BF16)],
+        8 * half * width * frames,
     )[0]
 
 
@@ -415,16 +490,16 @@
     half = chans // 2
 
     def body(p, c, ct, a, b, a_theirs, b_theirs, out):
-        @pl.when(pl.program_id(0) == 0)
-        def _():
-            total = dot(c[...], a[...], NN) + dot(ct[...], a_theirs[...], NN)
-            out[...] = (total * scale).astype(BF16)
-
-        @pl.when(pl.program_id(0) == 1)
-        def _():
-            total = dot(c[...], b[...], NN) + dot(ct[...], b_theirs[...], NN)
-            out[...] = (total * scale).astype(BF16)
-
+        first = pl.program_id(0) == 0
+        left = jnp.where(first, a[...], b[...])
+        right = jnp.where(first, a_theirs[...], b_theirs[...])
+        total = dot(c[...], left, NN) + dot(ct[...], right, NN)
+        out[...] = (total * scale).astype(BF16)
+
+    out = (
+        shape((half, 2 * chans), BF16),
+        pl.BlockSpec((half, chans), lambda i, p: (0, jnp.where(i == 0, p[0], 1 - p[0]))),
+    )
     return call(
         body,
         "out_grads",
@@ -432,12 +507,7 @@
         (2,),
         [pl.BlockSpec((half, frames), lambda i, p: (p[1], 0)), whole((half, frames))]
         + [whole((frames, chans))] * 4,
-        [
-            (
-                shape((half, 2 * chans), BF16),
-                pl.BlockSpec((half, chans), lambda i, p: (0, jnp.where(i == 0, p[0], 1 - p[0]))),
-            )
-        ],
+        [out],
         [cot, cot_theirs, *acts],
         (),
         8 * half * chans * frames,
@@ -524,13 +594,14 @@
 
     some = rows_of(height, chans)
     line = lanes(8, height)
+    block = pl.BlockSpec((chans, height), lambda i, p: (0, edges_first(i, frames // height)))
     return call(
         body,
         "input_step",
         places,
         (frames // height,),
-        [some, some, some, whole((1, chans)), rows_of(height, LANES), line, line, lanes(chans, height)],
-        [(shape((chans, frames), BF16), lanes(chans, height))],
+        [some, some, some, whole((1, chans)), rows_of(height, LANES), line, line, block],
+        [(shape((chans, frames), BF16), block)],
         [term, recv, hat, gain, inv, mine, theirs, cot],
         (),
         10 * frames * chans,
@@ -560,37 +631,32 @@
     )[0]
 
 
-def join_halves(places, mine, theirs):
-    half, cols = mine.shape
-    parts = 2
-    step = half // parts
-
-    def body(p, m, t, out):
-        lower = pl.program_id(0) < parts
-
-        @pl.when(lower == (p[1] == 0))
-        def _():
-            out[...] = m[...]
-
-        @pl.when(lower != (p[1] == 0))
-        def _():
-            out[...] = t[...]
-
-    def hold(first, i):
-        return jnp.where(first, jnp.minimum(i, parts - 1), jnp.maximum(i - parts, 0))
-
-    return call(
+def join_halves(places, pair, pair_theirs, single, single_theirs):
+    chips, _, rows, cols = pair.shape
+
+    def body(p, a, at, b, bt, *refs):
+        outs, done = refs[:3], refs[3]
+        copies = []
+        for core, (two, one) in ((p[1], (a, b)), (1 - p[1], (at, bt))):
+            for source, out in zip((two.at[:, 0], two.at[:, 1], one.at[:, 0]), outs):
+                copies.append(pltpu.make_async_copy(source, out.at[core], done.at[len(copies)]))
+        for copy in copies:
+            copy.start()
+        for copy in copies:
+            copy.wait()
+
+    anywhere = pl.BlockSpec(memory_space=pl.ANY)
+    outs = call(
         body,
         "join_halves",
         places,
-        (2 * parts,),
-        [
-            pl.BlockSpec((step, cols), lambda i, p: (hold(p[1] == 0, i), 0)),
-            pl.BlockSpec((step, cols), lambda i, p: (hold(p[1] == 1, i), 0)),
-        ],
-        [(shape((2 * half, cols), BF16), rows_of(step, cols))],
-        [mine, theirs],
-    )[0]
+        (1,),
+        [anywhere] * 4,
+        [(shape((2, chips, rows, cols), BF16), anywhere)] * 3,
+        [pair, pair_theirs, single, single_theirs],
+        [pltpu.SemaphoreType.DMA((6,))],
+    )
+    return [out.reshape(2 * chips * rows, cols) for out in outs]
 
 
 def ring_of(count):
@@ -625,14 +691,8 @@
     spot = jnp.asarray(place, jnp.int32)[lax.axis_index("seq")]
     reach = chips // 2
 
-    def at(step):
-        return (spot + step + chips) % chips
-
     def part(cells, step):
-        return lax.dynamic_index_in_dim(cells, at(step), 0, keepdims=False)
-
-    def put(cells, some, step):
-        return lax.dynamic_update_index_in_dim(cells, some, at(step), 0)
+        return lax.dynamic_index_in_dim(cells, (spot + step + chips) % chips, 0, keepdims=False)
 
     def up(cells):
         return lax.ppermute(cells, "seq", ahead)
@@ -657,13 +717,18 @@
         (part(x, 0).astype(F32) + u.astype(F32) + d.astype(F32)).astype(BF16)
         for x, (u, d) in zip(sets, flows)
     ]
-    outs = [put(x, own, 0) for x, own in zip(sets, owns)]
+    outs = []
+    for x, own in zip(sets, owns):
+        outs.append(lax.dynamic_update_index_in_dim(jnp.zeros_like(x), own, spot, 0))
     flows = [(own, own) for own in owns]
     for hop in range(1, reach):
         flows = [(up(u), down(d)) for u, d in flows]
-        outs = [put(put(x, u, -hop), d, hop) for x, (u, d) in zip(outs, flows)]
+        for i, (u, d) in enumerate(flows):
+            out = lax.dynamic_update_index_in_dim(outs[i], u, (spot - hop + chips) % chips, 0)
+            outs[i] = lax.dynamic_update_index_in_dim(out, d, (spot + hop) % chips, 0)
     for i, (u, d) in enumerate(flows):
-        outs[i] = put(outs[i], jnp.concatenate([down(d[:half]), up(u[half:])]), reach)
+        far = jnp.concatenate([down(d[:half]), up(u[half:])])
+        outs[i] = lax.dynamic_update_index_in_dim(outs[i], far, (spot + reach) % chips, 0)
     return outs
 
 
@@ -700,12 +765,14 @@
 def small_sum(values):
     count = lax.axis_size("seq")
     if count & (count - 1):
-        return lax.psum(values, "seq")
+        return lax.psum(values, "seq"), []
+    rests = []
     step = 1
     while step < count:
         values = values + lax.ppermute(values, "seq", pairs_of(count, step))
+        rests.append(values)
         step *= 2
-    return values
+    return values, rests
 
 
 def other(values):
@@ -840,7 +907,7 @@
     input_grad = (
         cotangent.astype(F32) + norm_back(d_normed * norm_gain[:, None], hat_in, inverse_in, width)
     ).astype(BF16)
-    small = small_sum(
+    small, _ = small_sum(
         jnp.concatenate([grad_kernel, grad_conv_gain[None], grad_norm_gain[None]], axis=0)
     )
     grad_out, grad_value, grad_gate = weight_sums([grad_out, grad_value, grad_gate])
@@ -871,69 +938,177 @@
     return lax.optimization_barrier((values, *after))[0]
 
 
+class Ring:
+    def __init__(self, cells):
+        self.chips, _, self.ahead, self.behind = ring_of(lax.axis_size("seq"))
+        chip = lax.axis_index("seq") // 2
+        self.spot = jnp.where(chip % 2 == 0, chip // 2, self.chips - 1 - chip // 2)
+        self.reach = self.chips // 2
+        self.half = cells.shape[1] // 2
+        self.cells = cells
+        self.count = 0
+        self.up = self.down = None
+        self.extra = None
+
+    def at(self, step):
+        return (self.spot + step + self.chips) % self.chips
+
+    def part(self, step):
+        return lax.dynamic_index_in_dim(self.cells, self.at(step), 0, keepdims=False)
+
+    def put(self, some, step):
+        rows = self.cells.shape[1]
+        self.cells = lax.dynamic_update_index_in_dim(self.cells, some[:rows], self.at(step), 0)
+        if self.extra is not None:
+            self.gathered.append(some[rows:])
+
+    def send(self, up, down, after):
+        if after:
+            up, down = lax.optimization_barrier((up, down, *after))[:2]
+        self.up = lax.ppermute(up, "seq", self.ahead)
+        self.down = lax.ppermute(down, "seq", self.behind)
+
+    def hop(self, *after):
+        reach, half = self.reach, self.half
+        self.count += 1
+        left = reach + 1 - self.count
+        u, d = self.up, self.down
+        if self.count == 1:
+            self.send(self.part(reach)[half:], self.part(-reach)[:half], after)
+        elif left > 0:
+            own_u, own_d = self.part(left), self.part(-left)
+            if self.count == 2:
+                u = jnp.concatenate([own_u[:half], add(own_u[half:], u)])
+                d = jnp.concatenate([add(own_d[:half], d), own_d[half:]])
+            else:
+                u, d = add(own_u, u), add(own_d, d)
+            self.send(u, d, after)
+        else:
+            if left == 0:
+                own = self.part(0).astype(F32) + u.astype(F32) + d.astype(F32)
+                u = d = own.astype(BF16)
+                if self.extra is not None:
+                    u = d = jnp.concatenate([u, self.extra])
+                    self.gathered = []
+                self.put(u, 0)
+            if left > 1 - reach:
+                self.send(u, d, after)
+                self.put(self.up, left - 1)
+                self.put(self.down, 1 - left)
+            else:
+                self.send(u[half:], d[:half], after)
+                self.put(jnp.concatenate([self.down, self.up]), reach)
+
+    def gather(self, extra):
+        self.extra = extra
+
+
 def fused(
     frames_in, norm_gain, value_weight, gate_weight, depth_kernel, conv_gain, out_weight, cotangent
 ):
     chans, frames = frames_in.shape
     taps = depth_kernel.shape[1]
     half = chans // 2
+    quarter = frames // 4
     count = lax.axis_size("seq")
+    chips = count // 2
     scale = float(frames * count) ** (-0.5)
-    core = lax.axis_index("seq") % 2
-    places = jnp.stack([lax.axis_index("tp"), core]).astype(jnp.int32)
+    place = lax.axis_index("seq")
+    core = place % 2
+    places = jnp.stack([lax.axis_index("tp"), core, place // 2 % 2, place // 4 % 2])
+    places = places.astype(jnp.int32)
 
     gain = norm_gain[None]
-    gain_theirs = other(gain)
-    frames_theirs = other(frames_in)
+    edges = pack_edges(places, frames_in, gain)
+    edges_theirs = other(edges)
+    middle = frames_in[:, quarter : 3 * quarter]
+    middle_theirs = other(middle)
     taps_by = depth_kernel.T
-    cot_theirs = core_swap(lax.dynamic_slice_in_dim(cotangent, (1 - core) * half, half, 0))
-
-    theirs, d_act_mine = d_act_terms(places, cotangent, out_weight)
+    cot_half = lax.dynamic_slice_in_dim(cotangent, (1 - core) * half, half, 0)
+
+    theirs, d_act_mine = d_act_terms(places, tied(cotangent, cot_half, middle), out_weight)
+    cot_theirs = core_swap(cot_half)
     d_act_recv = other(theirs)
 
-    normed, hat_in, inv_in, glu, sig, slope, edge = glu_forward(
-        places, frames_in, frames_theirs, gain, gain_theirs, value_weight, gate_weight
-    )
+    weights = (value_weight, gate_weight)
+    *held, edge = glu_forward(places, edges, tied(edges_theirs, theirs, cot_theirs), gain, edges_theirs, weights, ())
+    before, after = rims(edge[1], edge[0])
+    normed, hat_in, inv_in, glu, sig, slope, _ = glu_forward(
+        places,
+        middle,
+        middle_theirs,
+        gain,
+        edges_theirs,
+        weights,
+        tuple(held),
+    )
+    conv, stats = conv_forward(places, before, glu, after, taps_by)
     normed_theirs = core_swap(normed)
-    before, after = rims(edge[1], edge[0])
-    conv, stats = conv_forward(places, before, glu, after, taps_by)
     stats_theirs = other(stats)
-    act, hat_conv, e, sums, gain_grad = act_step(
+    hat_conv, e, sums, gain_grad = act_step(
         places, conv, stats, stats_theirs, d_act_mine, d_act_recv, conv_gain[None]
     )
     sums_theirs = other(sums)
+    d_conv, act, head, tail = d_conv_step(
+        places, e, hat_conv, conv_gain[None], stats, stats_theirs, sums, sums_theirs
+    )
+    d_before, d_after = rims(tail, head)
     act_theirs = other(act)
-    d_conv, head, tail = d_conv_step(places, e, hat_conv, stats, stats_theirs, sums, sums_theirs)
-    d_before, d_after = rims(tail, head)
     sent_v, sent_g = d_glu_step(places, d_before, d_conv, d_after, taps_by, sig, slope, False)
     recv_v, recv_g = core_swap(sent_v), core_swap(sent_g)
-    own_v, own_g = d_glu_step(places, d_before, d_conv, d_after, taps_by, sig, slope, True)
-
+    own_v, own_g = d_glu_step(
+        places, d_before, tied(d_conv, sent_v), d_after, taps_by, sig, slope, True
+    )
+
+    grads = pair_grads(
+        places, chips, (own_v, own_g), (recv_v, recv_g), normed, normed_theirs, scale
+    )
+    a = Ring(grads.reshape(chips, -1, 2 * chans))
+    a.hop()
+    act, act_theirs = lax.optimization_barrier((act, act_theirs, grads))[:2]
     acts = [act, act_theirs, core_swap(act), core_swap(act_theirs)]
-    grad_out = out_grads(places, cotangent, cot_theirs, acts, scale)
-    grad_value = pair_grads(places, own_v, recv_v, normed, normed_theirs, scale)
-    grad_gate = pair_grads(places, own_g, recv_g, normed, normed_theirs, scale)
-
-    chips = count // 2
-    sets = [g.reshape(chips, half // chips, 2 * chans) for g in (grad_out, grad_value, grad_gate)]
-    sums_out = [g.reshape(half, 2 * chans) for g in ring_sum(sets)]
-    swapped = [core_swap(g) for g in sums_out]
-    grad_out, grad_value, grad_gate = [
-        join_halves(places, mine, there) for mine, there in zip(sums_out, swapped)
-    ]
-
-    held = tied(own_v, sets[1])
+    cot = tied(cotangent, a.up, a.down)
+    grad_out = out_grads(places, cot, cot_theirs, acts, scale)
+    b = Ring(grad_out.reshape(chips, -1, 2 * chans))
+    b.hop()
+    a.hop()
     theirs, mine = d_normed_terms(
-        places, [held, sent_v], [own_g, sent_g], value_weight, gate_weight
+        places, [tied(own_v, grad_out), sent_v], [own_g, sent_g], value_weight, gate_weight
     )
     recv = other(theirs)
+    b.hop(theirs)
+    a.hop()
     kernel_grad = taps_grad(places, before, glu, after, tied(d_conv, theirs), scale)
-    block_out = out_step(places, frames_in, out_weight, act, tied(act_theirs, theirs))
-    sums_in, norm_grad = norm_sums(places, mine, recv, hat_in, gain)
+    b.hop(kernel_grad)
+    a.hop()
+    block_out = out_step(places, frames_in, out_weight, act, tied(act_theirs, kernel_grad))
+    b.hop(block_out)
+    a.hop()
+    sums_in, norm_grad = norm_sums(places, mine, tied(recv, block_out), hat_in, gain)
+    sums_in_theirs = other(sums_in)
+    small = jnp.concatenate([kernel_grad, gain_grad * scale, norm_grad * scale])
+    small = small + core_swap(small)
+    depth = (taps + 2 + 15) // 16 * 8
+    small = jnp.pad(small, ((0, 2 * depth - taps - 2), (0, 0)))
+    b.gather(jnp.concatenate([small[:depth], small[depth:]], axis=1).astype(BF16))
+    b.hop()
     input_grad = input_step(
-        places, mine, recv, hat_in, gain, inv_in, sums_in, other(sums_in), cotangent
-    )
-    small = small_sum(jnp.concatenate([kernel_grad, gain_grad * scale, norm_grad * scale]))
+        places, mine, recv, hat_in, gain, inv_in, sums_in, sums_in_theirs, cotangent
+    )
+    a.hop()
+    b.hop(input_grad)
+    a.hop()
+    b.hop()
+    a.hop()
+    b.hop()
+    small = sum(some.astype(F32) for some in b.gathered)
+    small = jnp.concatenate([small[:, :chans], small[:, chans:]])
+
+    pair = a.cells.reshape(chips, 2, half // chips, 2 * chans)
+    single = b.cells.reshape(chips, 1, half // chips, 2 * chans)
+    grad_value, grad_gate, grad_out = join_halves(
+        places, pair, core_swap(pair), single, core_swap(single)
+    )
     return (
         block_out,
         input_grad,
@@ -950,8 +1125,8 @@
     chans, frames = arrays[0].shape
     taps = arrays[4].shape[1]
     count = lax.axis_size("seq")
-    fits = lax.axis_size("tp") == 2 and taps == 32 and chans % 256 == 0 and frames % 128 == 0
-    fits = fits and count % 4 == 0 and chans % (16 * count) == 0
+    fits = lax.axis_size("tp") == 2 and taps == 32 and chans % 256 == 0 and frames % 512 == 0
+    fits = fits and count == 16 and chans % (16 * count) == 0
     return (fused if fits else plain)(*arrays)
 
 

time: 251 us -> 201 us (0.80)
  starting transfers between devices: 81 us -> 57 us
  waiting for transfers between devices: 76.1 us -> 63.6 us
  Pallas kernels: 72 us -> 65 us
  between operations: 7.42 us -> 1.53 us
    ppermute x52 -> x32, starting transfers between devices: 59.4 us -> 35.2 us  [the longest x16 30.4 us: send(): self.up = lax.ppermute(up, 'seq', self.ahead)]
    ppermute x8, waiting for transfers between devices: 31.4 us -> 16.8 us  [other(): return lax.ppermute(values, 'tp', [(0, 1), (1, 0)])]
    pallas_call x18 -> x17, Pallas kernels: 72 us -> 65 us  [call(): pl.pallas_call(body, out_shape=[s for s, _ in outs], grid_spec=pltpu.Pref...]
    ppermute x2, waiting for transfers between devices: 6.71 us -> 2.76 us  [rims(): after = lax.ppermute(head, 'seq', [(i + 1, i) for i in range(count - 1)])]
    ppermute x52 -> x32, waiting for transfers between devices: 38 us -> 41.7 us  [the longest x16 23.6 us: send(): self.down = lax.ppermute(down, 'seq', self.behind)]
    unnamed x52 -> x57, local copies, waits for them, and re-layouts: 9.03 us -> 9.47 us
  transfers between devices with their start and end apart: 73 -> 53, of which waited for: 29 -> 21; matrix products, arithmetic and copies ran while one was open for 2% -> 1% of each run, Pallas kernels for 28% -> 28%
where the time goes in v3:
time: 201 us; the launch traced here: 200 us
  Pallas kernels  65 us (32%)
  waiting for transfers between devices  63.6 us (32%)
  starting transfers between devices  57 us (28%)
  local copies, waits for them, and re-layouts  11.2 us (6%)
    pallas_call x17, Pallas kernels, call(): pl.pallas_call(body, out_shape=[s for s, _ in outs], grid_spec=pltpu.Pref...  65 us
    ppermute x16, starting transfers between devices, send(): self.up = lax.ppermute(up, 'seq', self.ahead)  30.4 us
    ppermute x16, waiting for transfers between devices, send(): self.down = lax.ppermute(down, 'seq', self.behind)  23.6 us
    ppermute x16, waiting for transfers between devices, send(): self.up = lax.ppermute(up, 'seq', self.ahead)  18.1 us
    ppermute x8, waiting for transfers between devices, other(): return lax.ppermute(values, 'tp', [(0, 1), (1, 0)])  16.8 us
    ppermute x8, starting transfers between devices, other(): return lax.ppermute(values, 'tp', [(0, 1), (1, 0)])  12 us
    unnamed x57, local copies, waits for them, and re-layouts  9.47 us
    ppermute x2, starting transfers between devices, rims(): before = lax.ppermute(tail, 'seq', [(i, i + 1) for i in range(count - 1)])  5.09 us
  transfers between devices with their start and end apart: 53, of which 21 were waited for; matrix products, arithmetic and copies ran while one was open for 1% of the time, Pallas kernels for 28%

profile of v3, /device:TPU:0, one launch (start us, length us, event | category | flops | bytes accessed | tf_op | source)
XLA Modules:
  0.0 200.1 jit_solution(12610462071997189779)
XLA Ops:
  4.0 2.9 %collective-permute-start = (bf16[784,256]{1,0:T(8,128)(2,1)}, bf16[784,256]{1,0:T(8,128)(2,1)S(1)}, u32[]{:S(2)}, u32[]{:S(2)}) collective-permute-start(bf16[784,256]{1,0:T(8,128)(2,1)} %pack_edges.1.xm), channel_id=1, source_target_pairs={{0,1},{1,0},{2,3},{3,2},{4,5},{5,4},{6,7},{7,6},{8,9},{9,8},{10,11... | collective-permute-start | bytes 1204232 | tf_op jit(solution)/shard_map/ppermute | solution.py:779
  12.7 4.6 %collective-permute-done.xt.gt = bf16[784,256]{1,0:T(8,128)(2,1)S(1)} collective-permute-done((bf16[784,256]{1,0:T(8,128)(2,1)}, bf16[784,256]{1,0:T(8,128)(2,1)S(1)}, u32[]{:S(2)}, u32[]{:S(2)}) %collective-permute-start) | collective-permute-done | bytes 401440 | tf_op jit(solution)/shard_map/ppermute | solution.py:779
  17.3 5.0 %glu_edges.1 = (bf16[512,1536]{1,0:T(8,128)(2,1)}, f32[512,768]{1,0:T(8,128)S(1)}, f32[512,128]{1,0:T(8,128)S(1)}, bf16[512,768]{1,0:T(8,128)(2,1)S(1)}, f32[512...) custom-call(s32[4]{0:T(128)S(1)} %pad_add_fusion.p, bf16[784,256]{1,0:T(8,128)(2,1)} %pack_edges.1.xm, ...), custom_call_target="tpu_custom_call" | custom-call | flops 1000 | bytes 1000 | tf_op jit(solution)/shard_map/glu_edges/pallas_call | solution.py:26
  24.9 4.0 %glu_middle.1 = (bf16[512,1536]{1,0:T(8,128)(2,1)}, f32[512,768]{1,0:T(8,128)S(1)}, f32[512,128]{1,0:T(8,128)S(1)}, bf16[512,768]{1,0:T(8,128)(2,1)S(1)}, f32[51...) custom-call(s32[4]{0:T(128)S(1)} %pad_add_fusion.p, ...), custom_call_target="tpu_custom_call", output_to_operand_aliasing={{0}: (7, {}), {1}: (8, {}), {2}: (9, {}), {3}: (10, {}), {4... | custom-call | flops 1000 | bytes 1000 | tf_op jit(solution)/shard_map/glu_middle/pallas_call | solution.py:26
  38.1 5.8 %conv_forward.1 = (f32[512,768]{1,0:T(8,128)S(1)}, f32[8,512]{1,0:T(8,128)S(1)}) custom-call(s32[4]{0:T(128)S(1)} %pad_add_fusion.p, bf16[16,768]{1,0:T(8,128)(2,1)S(1)} %collective-permute-done.2.b, bf16[512,768]{1,0:T(8,128)(2,1)S(1)} %get-tuple-element.72.g, bf16[16,768]{1,0:T(8,128)(2,1)S(1)} %collective-permute-done.4.a, f32[32,768]{1,0:T(8,128)S(1)} %bitcast.148), custom_call_target="tpu_custom_call" | custom-call | flops 1000 | bytes 1000 | tf_op jit(solution)/shard_map/conv_forward/pallas_call | solution.py:26
  44.5 6.0 %collective-permute-done.5.st = f32[8,512]{1,0:T(8,128)S(1)} collective-permute-done((f32[8,512]{1,0:T(8,128)S(1)}, f32[8,512]{1,0:T(8,128)S(1)}, u32[]{:S(2)}, u32[]{:S(2)}) %collective-permute-start.5) | collective-permute-done | bytes 16416 | tf_op jit(solution)/shard_map/ppermute | solution.py:779
  57.0 3.2 %d_conv_step.1 = (bf16[512,768]{1,0:T(8,128)(2,1)S(1)}, bf16[512,768]{1,0:T(8,128)(2,1)}, bf16[16,768]{1,0:T(8,128)(2,1)S(1)}, bf16[16,768]{1,0:T(8,128)(2,1)S(1)}) custom-call(s32[4]{0:T(128)S(1)} %pad_add_fusion.p, f32[512,768]{1,0:T(8,128)S(1)} %get-tuple-element.76.d, f32[512,768]{1,0:T(8,128)S(1)} %get-tuple-element.77.h, ...), custom_call_target="tpu_custom_call" | custom-call | flops 1000 | bytes 1000 | tf_op jit(solution)/shard_map/d_conv_step/pallas_call | solution.py:26
  63.3 3.0 %collective-permute-start.9 = (bf16[16,768]{1,0:T(8,128)(2,1)S(1)}, bf16[16,768]{1,0:T(8,128)(2,1)S(1)}, u32[]{:S(2)}, u32[]{:S(2)}) collective-permute-start(bf16[16,768]{1,0:T(8,128)(2,1)S(1)} %get-tuple-element.80), channel_id=1, source_target_pairs={{0,2},{2,4},{4,6},{6,8},{8,10},{10,12},{12,14},{14,16},{16,18},{18... | collective-permute-start | bytes 73736 | tf_op jit(solution)/shard_map/ppermute | solution.py:932
  67.2 3.9 %d_glu_other.1 = (bf16[512,384]{1,0:T(8,128)(2,1)}, bf16[512,384]{1,0:T(8,128)(2,1)}) custom-call(s32[4]{0:T(128)S(1)} %pad_add_fusion.p, bf16[16,768]{1,0:T(8,128)(2,1)S(1)} %collective-permute-done.9.b, bf16[512,768]{1,0:T(8,128)(2,1)S(1)} %get-tuple-element.96.d, bf16[16,768]{1,0:T(8,128)(2,1)S(1)} %collective-permute-done.10.a, f32[32,768]{1,0:T(8,128)S(1)} %bitcast.149, ...), custom_call_target="tpu_custom_call" | custom-call | flops 1000 | bytes 1000 | tf_op jit(solution)/shard_map/d_glu_other/pallas_call | solution.py:26
  76.3 3.3 %d_glu_own.1 = (bf16[512,384]{1,0:T(8,128)(2,1)S(1)}, bf16[512,384]{1,0:T(8,128)(2,1)S(1)}) custom-call(s32[4]{0:T(128)S(1)} %pad_add_fusion.p, bf16[16,768]{1,0:T(8,128)(2,1)S(1)} %collective-permute-done.9.b, bf16[512,768]{1,0:T(8,128)(2,1)S(1)} %copy-done.17, bf16[16,768]{1,0:T(8,128)(2,1)S(1)} %collective-permute-done.10.a, f32[32,768]{1,0:T(8,128)S(1)} %bitcast.150, ...), custom_call_target="tpu_custom_call" | custom-call | flops 1000 | bytes 1000 | tf_op jit(solution)/shard_map/d_glu_own/pallas_call | solution.py:26
  79.6 5.8 %pair_grads.1 = bf16[8,2,48,1536]{3,2,1,0:T(8,128)(2,1)S(1)} custom-call(s32[4]{0:T(128)S(1)} %pad_add_fusion.p, bf16[512,384]{1,0:T(8,128)(2,1)S(1)} %get-tuple-element.94.mv.vo, bf16[512,384]{1,0:T(8,128)(2,1)S(1)} %get-tuple-element.88.mg.go, bf16[512,384]{1,0:T(8,128)(2,1)} %collective-permute-done.11.tv, bf16[512,384]{1,0:T(8,128)(2,1)} %collective-permute-done.12.tg, ...), custom_call_target="tpu_custom_call" | custom-call | flops 1000 | bytes 1000 | tf_op jit(solution)/shard_map/pair_grads/pallas_call | solution.py:26
  85.5 3.7 %collective-permute-start.14 = (bf16[48,1536]{1,0:T(8,128)(2,1)S(1)}, bf16[48,1536]{1,0:T(8,128)(2,1)S(1)}, u32[]{:S(2)}, u32[]{:S(2)}) collective-permute-start(bf16[48,1536]{1,0:T(8,128)(2,1)S(1)} %get-tuple-element.125), channel_id=1, source_target_pairs={{0,8},{2,10},{8,16},{10,18},{16,24},{18,26},{24,28},{26,30},{28,20... | collective-permute-start | bytes 442376 | tf_op jit(solution)/shard_map/ppermute | solution.py:968
  95.2 3.8 %out_grads.1 = bf16[384,1536]{1,0:T(8,128)(2,1)S(1)} custom-call(s32[4]{0:T(128)S(1)} %pad_add_fusion.p, bf16[768,512]{1,0:T(8,128)(2,1)S(1)} %copy-done.13, bf16[384,512]{1,0:T(8,128)(2,1)S(1)} %copy-done.26, bf16[512,768]{1,0:T(8,128)(2,1)} %get-tuple-element.91.a, bf16[512,768]{1,0:T(8,128)(2,1)} %collective-permute-done.8.b, ...), custom_call_target="tpu_custom_call" | custom-call | flops 1000 | bytes 1000 | tf_op jit(solution)/shard_map/out_grads/pallas_call | solution.py:26
  102.9 5.6 %d_normed_terms.1 = (bf16[512,768]{1,0:T(8,128)(2,1)S(1)}, bf16[512,768]{1,0:T(8,128)(2,1)S(1)}) custom-call(s32[4]{0:T(128)S(1)} %pad_add_fusion.p, bf16[512,384]{1,0:T(8,128)(2,1)S(1)} %get-tuple-element.94.mv.vo, bf16[512,384]{1,0:T(8,128)(2,1)} %get-tuple-element.85.vt, bf16[512,384]{1,0:T(8,128)(2,1)S(1)} %get-tuple-element.88.mg.go, ...), custom_call_target="tpu_custom_call" | custom-call | flops 1000 | bytes 1000 | tf_op jit(solution)/shard_map/d_normed_terms/pallas_call | solution.py:26
  112.7 5.3 %taps_grad.1 = f32[32,768]{1,0:T(8,128)S(1)} custom-call(s32[4]{0:T(128)S(1)} %pad_add_fusion.p, bf16[16,768]{1,0:T(8,128)(2,1)S(1)} %collective-permute-done.2.b, bf16[512,768]{1,0:T(8,128)(2,1)S(1)} %copy-done.20, bf16[16,768]{1,0:T(8,128)(2,1)S(1)} %collective-permute-done.4.a, bf16[512,768]{1,0:T(8,128)(2,1)S(1)} %copy-done.18), custom_call_target="tpu_custom_call" | custom-call | flops 1000 | bytes 1000 | tf_op jit(solution)/shard_map/taps_grad/pallas_call | solution.py:26
  122.9 4.5 %out_step.1 = bf16[768,512]{1,0:T(8,128)(2,1)} custom-call(s32[4]{0:T(128)S(1)} %pad_add_fusion.p, bf16[768,512]{1,0:T(8,128)(2,1)S(1)} %copy-done.10, bf16[768,1536]{1,0:T(8,128)(2,1)S(1)} %copy-done.15, bf16[512,768]{1,0:T(8,128)(2,1)} %get-tuple-element.91.a, bf16[512,768]{1,0:T(8,128)(2,1)} %collective-permute-done.8.b), custom_call_target="tpu_custom_call" | custom-call | flops 1000 | bytes 1000 | tf_op jit(solution)/shard_map/out_step/pallas_call | solution.py:26
  134.8 4.4 %collective-permute-done.41 = bf16[96,1536]{1,0:T(8,128)(2,1)S(1)} collective-permute-done((bf16[96,1536]{1,0:T(8,128)(2,1)S(1)}, bf16[96,1536]{1,0:T(8,128)(2,1)S(1)}, u32[]{:S(2)}, u32[]{:S(2)}) %collective-permute-start.41) | collective-permute-done | bytes 294944 | tf_op jit(solution)/shard_map/ppermute | solution.py:969
  147.3 3.2 %input_step.1 = bf16[768,512]{1,0:T(8,128)(2,1)} custom-call(s32[4]{0:T(128)S(1)} %pad_add_fusion.p, bf16[512,768]{1,0:T(8,128)(2,1)S(1)} %get-tuple-element.98.tm, bf16[512,768]{1,0:T(8,128)(2,1)S(1)} %collective-permute-done.18.tr, f32[512,768]{1,0:T(8,128)S(1)} %copy-done.8, f32[1,768]{1,0:T(1,128)S(1)} %broadcast_in_dim.41.g.gm, ...), custom_call_target="tpu_custom_call" | custom-call | flops 1000 | bytes 1000 | tf_op jit(solution)/shard_map/input_step/pallas_call | solution.py:26
  154.7 8.2 %collective-permute-done.29 = bf16[72,1536]{1,0:T(8,128)(2,1)S(1)} collective-permute-done((bf16[72,1536]{1,0:T(8,128)(2,1)S(1)}, bf16[72,1536]{1,0:T(8,128)(2,1)S(1)}, u32[]{:S(2)}, u32[]{:S(2)}) %collective-permute-start.29) | collective-permute-done | bytes 221216 | tf_op jit(solution)/shard_map/ppermute | solution.py:968
  169.3 4.1 %collective-permute-done.31 = bf16[72,1536]{1,0:T(8,128)(2,1)S(1)} collective-permute-done((bf16[72,1536]{1,0:T(8,128)(2,1)S(1)}, bf16[72,1536]{1,0:T(8,128)(2,1)S(1)}, u32[]{:S(2)}, u32[]{:S(2)}) %collective-permute-start.31) | collective-permute-done | bytes 221216 | tf_op jit(solution)/shard_map/ppermute | solution.py:968
  175.4 6.0 %collective-permute-done.47 = bf16[96,1536]{1,0:T(8,128)(2,1)S(1)} collective-permute-done((bf16[96,1536]{1,0:T(8,128)(2,1)S(1)}, bf16[96,1536]{1,0:T(8,128)(2,1)S(1)}, u32[]{:S(2)}, u32[]{:S(2)}) %collective-permute-start.47) | collective-permute-done | bytes 294944 | tf_op jit(solution)/shard_map/ppermute | solution.py:969
  183.6 3.0 %collective-permute-done.48 = bf16[48,1536]{1,0:T(8,128)(2,1)S(1)} collective-permute-done((bf16[48,1536]{1,0:T(8,128)(2,1)S(1)}, bf16[48,1536]{1,0:T(8,128)(2,1)S(1)}, u32[]{:S(2)}, u32[]{:S(2)}) %collective-permute-start.48) | collective-permute-done | bytes 147488 | tf_op jit(solution)/shard_map/ppermute | solution.py:969
  189.3 4.1 %collective-permute-done.51 = bf16[24,1536]{1,0:T(8,128)(2,1)S(1)} collective-permute-done((bf16[24,1536]{1,0:T(8,128)(2,1)S(1)}, bf16[24,1536]{1,0:T(8,128)(2,1)S(1)}, u32[]{:S(2)}, u32[]{:S(2)}) %collective-permute-start.51) | collective-permute-done | bytes 73760 | tf_op jit(solution)/shard_map/ppermute | solution.py:969
  196.4 3.5 %join_halves.1 = (bf16[2,8,48,1536]{3,2,1,0:T(8,128)(2,1)}, bf16[2,8,48,1536]{3,2,1,0:T(8,128)(2,1)}, bf16[2,8,48,1536]{3,2,1,0:T(8,128)(2,1)}) custom-call(s32[4]{0:T(128)S(1)} %pad_add_fusion.p, bf16[8,2,48,1536]{3,2,1,0:T(8,128)(2,1)S(1)} %bitcast.141, bf16[8,2,48,1536]{3,2,1,0:T(8,128)(2,1)S(1)} %collective-permute-done.50.at, ...), custom_call_target="tpu_custom_call" | custom-call | flops 1000 | bytes 1000 | tf_op jit(solution)/shard_map/join_halves/pallas_call | solution.py:26
  (205 shorter events, 91.5 us)
Async XLA Ops:
  4.0 13.3 %collective-permute-start = (bf16[784,256]{1,0:T(8,128)(2,1)}, bf16[784,256]{1,0:T(8,128)(2,1)S(1)}, u32[]{:S(2)}, u32[]{:S(2)}) collective-permute-start(bf16[784,256]{1,0:T(8,128)(2,1)} %pack_edges.1.xm), channel_id=1, source_target_pairs={{0,1},{1,0},{2,3},{3,2},{4,5},{5,4},{6,7},{7,6},{8,9},{9,8},{10,11... | collective-permute-start | bytes 1204232 | tf_op jit(solution)/shard_map/ppermute | solution.py:779
  7.2 17.8 %collective-permute-start.3 = (bf16[768,256]{1,0:T(8,128)(2,1)S(1)}, bf16[768,256]{1,0:T(8,128)(2,1)S(1)}, u32[]{:S(2)}, u32[]{:S(2)}) collective-permute-start(bf16[768,256]{1,0:T(8,128)(2,1)S(1)} %slice.153.xm), channel_id=1, source_target_pairs={{0,1},{1,0},{2,3},{3,2},{4,5},{5,4},{6,7},{7,6},{8,9},{9,8},{10,11... | collective-permute-start | bytes 1179656 | tf_op jit(solution)/shard_map/ppermute | solution.py:779
  30.1 49.5 %collective-permute-start.13 = (bf16[512,1536]{1,0:T(8,128)(2,1)}, bf16[512,1536]{1,0:T(8,128)(2,1)}, u32[]{:S(2)}, u32[]{:S(2)}) collective-permute-start(bf16[512,1536]{1,0:T(8,128)(2,1)} %get-tuple-element.90.n), channel_id=1, source_target_pairs={{0,2},{2,0},{4,6},{6,4},{8,10},{10,8},{12,14},{14,12},{16,18},{18,... | collective-permute-start | bytes 4718600 | tf_op jit(solution)/shard_map/ppermute | solution.py:927
  30.2 20.3 %collective-permute-start.6 = (bf16[512,768]{1,0:T(8,128)(2,1)S(1)}, bf16[512,768]{1,0:T(8,128)(2,1)S(1)}, u32[]{:S(2)}, u32[]{:S(2)}) collective-permute-start(bf16[512,768]{1,0:T(8,128)(2,1)S(1)} %get-tuple-element.63), channel_id=1, source_target_pairs={{0,1},{1,0},{2,3},{3,2},{4,5},{5,4},{6,7},{7,6},{8,9},{9,8},{10,11... | collective-permute-start | bytes 2359304 | tf_op jit(solution)/shard_map/ppermute | solution.py:779
  60.2 28.9 %collective-permute-start.8 = (bf16[512,768]{1,0:T(8,128)(2,1)}, bf16[512,768]{1,0:T(8,128)(2,1)}, u32[]{:S(2)}, u32[]{:S(2)}) collective-permute-start(bf16[512,768]{1,0:T(8,128)(2,1)} %get-tuple-element.91.a), channel_id=1, source_target_pairs={{0,1},{1,0},{2,3},{3,2},{4,5},{5,4},{6,7},{7,6},{8,9},{9,8},{10,11... | collective-permute-start | bytes 2359304 | tf_op jit(solution)/shard_map/ppermute | solution.py:779
  94.8 25.3 %collective-permute-start.39 = (bf16[96,1536]{1,0:T(8,128)(2,1)S(1)}, bf16[96,1536]{1,0:T(8,128)(2,1)S(1)}, u32[]{:S(2)}, u32[]{:S(2)}) collective-permute-start(bf16[96,1536]{1,0:T(8,128)(2,1)S(1)} %pad_maximum_fusion.1), channel_id=1, source_target_pairs={{8,0},{10,2},{16,8},{18,10},{24,16},{26,18},{28,24},{30,26},{20,28... | collective-permute-start | bytes 884744 | tf_op jit(solution)/shard_map/ppermute | solution.py:969
  99.0 9.6 %collective-permute-start.21 = (bf16[24,1536]{1,0:T(8,128)(2,1)S(1)}, bf16[24,1536]{1,0:T(8,128)(2,1)S(1)}, u32[]{:S(2)}, u32[]{:S(2)}) collective-permute-start(bf16[24,1536]{1,0:T(8,128)(2,1)S(1)} %get-tuple-element.137), channel_id=1, source_target_pairs={{0,8},{2,10},{8,16},{10,18},{16,24},{18,26},{24,28},{26,30},{28,20... | collective-permute-start | bytes 221192 | tf_op jit(solution)/shard_map/ppermute | solution.py:968
  101.1 9.8 %collective-permute-start.36 = (bf16[96,1536]{1,0:T(8,128)(2,1)S(1)}, bf16[96,1536]{1,0:T(8,128)(2,1)S(1)}, u32[]{:S(2)}, u32[]{:S(2)}) collective-permute-start(bf16[96,1536]{1,0:T(8,128)(2,1)S(1)} %pad_maximum_fusion), channel_id=1, source_target_pairs={{0,8},{2,10},{8,16},{10,18},{16,24},{18,26},{24,28},{26,30},{28,20... | collective-permute-start | bytes 884744 | tf_op jit(solution)/shard_map/ppermute | solution.py:968
  118.1 9.5 %collective-permute-start.25 = (bf16[48,1536]{1,0:T(8,128)(2,1)S(1)}, bf16[48,1536]{1,0:T(8,128)(2,1)S(1)}, u32[]{:S(2)}, u32[]{:S(2)}) collective-permute-start(bf16[48,1536]{1,0:T(8,128)(2,1)S(1)} %get-tuple-element.107), channel_id=1, source_target_pairs={{0,8},{2,10},{8,16},{10,18},{16,24},{18,26},{24,28},{26,30},{28,20... | collective-permute-start | bytes 442376 | tf_op jit(solution)/shard_map/ppermute | solution.py:968
  120.3 9.4 %collective-permute-start.40 = (bf16[96,1536]{1,0:T(8,128)(2,1)S(1)}, bf16[96,1536]{1,0:T(8,128)(2,1)S(1)}, u32[]{:S(2)}, u32[]{:S(2)}) collective-permute-start(bf16[96,1536]{1,0:T(8,128)(2,1)S(1)} %get-tuple-element.121), channel_id=1, source_target_pairs={{8,0},{10,2},{16,8},{18,10},{24,16},{26,18},{28,24},{30,26},{20,28... | collective-permute-start | bytes 884744 | tf_op jit(solution)/shard_map/ppermute | solution.py:969
  120.8 14.0 %collective-permute-start.38 = (bf16[96,1536]{1,0:T(8,128)(2,1)S(1)}, bf16[96,1536]{1,0:T(8,128)(2,1)S(1)}, u32[]{:S(2)}, u32[]{:S(2)}) collective-permute-start(bf16[96,1536]{1,0:T(8,128)(2,1)S(1)} %get-tuple-element.120), channel_id=1, source_target_pairs={{0,8},{2,10},{8,16},{10,18},{16,24},{18,26},{24,28},{26,30},{28,20... | collective-permute-start | bytes 884744 | tf_op jit(solution)/shard_map/ppermute | solution.py:968
  122.4 19.1 %collective-permute-start.18 = (bf16[512,768]{1,0:T(8,128)(2,1)S(1)}, bf16[512,768]{1,0:T(8,128)(2,1)S(1)}, u32[]{:S(2)}, u32[]{:S(2)}) collective-permute-start(bf16[512,768]{1,0:T(8,128)(2,1)S(1)} %get-tuple-element.95), channel_id=1, source_target_pairs={{0,1},{1,0},{2,3},{3,2},{4,5},{5,4},{6,7},{7,6},{8,9},{9,8},{10,11... | collective-permute-start | bytes 2359304 | tf_op jit(solution)/shard_map/ppermute | solution.py:779
  129.8 9.4 %collective-permute-start.41 = (bf16[96,1536]{1,0:T(8,128)(2,1)S(1)}, bf16[96,1536]{1,0:T(8,128)(2,1)S(1)}, u32[]{:S(2)}, u32[]{:S(2)}) collective-permute-start(bf16[96,1536]{1,0:T(8,128)(2,1)S(1)} %fusion.1), channel_id=1, source_target_pairs={{8,0},{10,2},{16,8},{18,10},{24,16},{26,18},{28,24},{30,26},{20,28... | collective-permute-start | bytes 884744 | tf_op jit(solution)/shard_map/ppermute | solution.py:969
  139.4 11.1 %collective-permute-start.42 = (bf16[96,1536]{1,0:T(8,128)(2,1)S(1)}, bf16[96,1536]{1,0:T(8,128)(2,1)S(1)}, u32[]{:S(2)}, u32[]{:S(2)}) collective-permute-start(bf16[96,1536]{1,0:T(8,128)(2,1)S(1)} %fusion.5), channel_id=1, source_target_pairs={{0,8},{2,10},{8,16},{10,18},{16,24},{18,26},{24,28},{26,30},{28,20... | collective-permute-start | bytes 884744 | tf_op jit(solution)/shard_map/ppermute | solution.py:968
  141.0 11.5 %collective-permute-start.43 = (bf16[96,1536]{1,0:T(8,128)(2,1)S(1)}, bf16[96,1536]{1,0:T(8,128)(2,1)S(1)}, u32[]{:S(2)}, u32[]{:S(2)}) collective-permute-start(bf16[96,1536]{1,0:T(8,128)(2,1)S(1)} %fusion.5), channel_id=1, source_target_pairs={{8,0},{10,2},{16,8},{18,10},{24,16},{26,18},{28,24},{30,26},{20,28... | collective-permute-start | bytes 884744 | tf_op jit(solution)/shard_map/ppermute | solution.py:969
  150.4 16.6 %collective-permute-start.44 = (bf16[96,1536]{1,0:T(8,128)(2,1)S(1)}, bf16[96,1536]{1,0:T(8,128)(2,1)S(1)}, u32[]{:S(2)}, u32[]{:S(2)}) collective-permute-start(bf16[96,1536]{1,0:T(8,128)(2,1)S(1)} %collective-permute-done.42), channel_id=1, source_target_pairs={{0,8},{2,10},{8,16},{10,18},{16,24},{18,26},{24,28},{26,30},{28,20... | collective-permute-start | bytes 884744 | tf_op jit(solution)/shard_map/ppermute | solution.py:968
  152.5 16.4 %collective-permute-start.45 = (bf16[96,1536]{1,0:T(8,128)(2,1)S(1)}, bf16[96,1536]{1,0:T(8,128)(2,1)S(1)}, u32[]{:S(2)}, u32[]{:S(2)}) collective-permute-start(bf16[96,1536]{1,0:T(8,128)(2,1)S(1)} %collective-permute-done.43), channel_id=1, source_target_pairs={{8,0},{10,2},{16,8},{18,10},{24,16},{26,18},{28,24},{30,26},{20,28... | collective-permute-start | bytes 884744 | tf_op jit(solution)/shard_map/ppermute | solution.py:969
  152.6 10.3 %collective-permute-start.29 = (bf16[72,1536]{1,0:T(8,128)(2,1)S(1)}, bf16[72,1536]{1,0:T(8,128)(2,1)S(1)}, u32[]{:S(2)}, u32[]{:S(2)}) collective-permute-start(bf16[72,1536]{1,0:T(8,128)(2,1)S(1)} %maximum_maximum_fusion), channel_id=1, source_target_pairs={{0,8},{2,10},{8,16},{10,18},{16,24},{18,26},{24,28},{26,30},{28,20... | collective-permute-start | bytes 663560 | tf_op jit(solution)/shard_map/ppermute | solution.py:968
  154.7 10.3 %collective-permute-start.30 = (bf16[72,1536]{1,0:T(8,128)(2,1)S(1)}, bf16[72,1536]{1,0:T(8,128)(2,1)S(1)}, u32[]{:S(2)}, u32[]{:S(2)}) collective-permute-start(bf16[72,1536]{1,0:T(8,128)(2,1)S(1)} %maximum_maximum_fusion), channel_id=1, source_target_pairs={{8,0},{10,2},{16,8},{18,10},{24,16},{26,18},{28,24},{30,26},{20,28... | collective-permute-start | bytes 663560 | tf_op jit(solution)/shard_map/ppermute | solution.py:969
  167.1 14.7 %collective-permute-start.46 = (bf16[96,1536]{1,0:T(8,128)(2,1)S(1)}, bf16[96,1536]{1,0:T(8,128)(2,1)S(1)}, u32[]{:S(2)}, u32[]{:S(2)}) collective-permute-start(bf16[96,1536]{1,0:T(8,128)(2,1)S(1)} %collective-permute-done.44), channel_id=1, source_target_pairs={{0,8},{2,10},{8,16},{10,18},{16,24},{18,26},{24,28},{26,30},{28,20... | collective-permute-start | bytes 884744 | tf_op jit(solution)/shard_map/ppermute | solution.py:968
  168.9 12.5 %collective-permute-start.47 = (bf16[96,1536]{1,0:T(8,128)(2,1)S(1)}, bf16[96,1536]{1,0:T(8,128)(2,1)S(1)}, u32[]{:S(2)}, u32[]{:S(2)}) collective-permute-start(bf16[96,1536]{1,0:T(8,128)(2,1)S(1)} %collective-permute-done.45), channel_id=1, source_target_pairs={{8,0},{10,2},{16,8},{18,10},{24,16},{26,18},{28,24},{30,26},{20,28... | collective-permute-start | bytes 884744 | tf_op jit(solution)/shard_map/ppermute | solution.py:969
  173.4 13.8 %collective-permute-start.33 = (bf16[72,1536]{1,0:T(8,128)(2,1)S(1)}, bf16[72,1536]{1,0:T(8,128)(2,1)S(1)}, u32[]{:S(2)}, u32[]{:S(2)}) collective-permute-start(bf16[72,1536]{1,0:T(8,128)(2,1)S(1)} %collective-permute-done.31), channel_id=1, source_target_pairs={{0,8},{2,10},{8,16},{10,18},{16,24},{18,26},{24,28},{26,30},{28,20... | collective-permute-start | bytes 663560 | tf_op jit(solution)/shard_map/ppermute | solution.py:968
  175.1 13.8 %collective-permute-start.34 = (bf16[72,1536]{1,0:T(8,128)(2,1)S(1)}, bf16[72,1536]{1,0:T(8,128)(2,1)S(1)}, u32[]{:S(2)}, u32[]{:S(2)}) collective-permute-start(bf16[72,1536]{1,0:T(8,128)(2,1)S(1)} %collective-permute-done.32), channel_id=1, source_target_pairs={{8,0},{10,2},{16,8},{18,10},{24,16},{26,18},{28,24},{30,26},{20,28... | collective-permute-start | bytes 663560 | tf_op jit(solution)/shard_map/ppermute | solution.py:969
  187.0 9.4 %collective-permute-start.50 = (bf16[8,2,48,1536]{3,2,1,0:T(8,128)(2,1)S(1)}, bf16[8,2,48,1536]{3,2,1,0:T(8,128)(2,1)S(1)}, u32[]{:S(2)}, u32[]{:S(2)}) collective-permute-start(bf16[8,2,48,1536]{3,2,1,0:T(8,128)(2,1)S(1)} %bitcast.140), channel_id=1, source_target_pairs={{0,2},{2,0},{4,6},{6,4},{8,10},{10,8},{12,14},{14,12},{16,18},{18,... | collective-permute-start | bytes 7077896 | tf_op jit(solution)/shard_map/ppermute | solution.py:927
  (57 other events, 453.3 us)

commit v4 on v3

--- a/solution.py
+++ b/solution.py
@@ -11,6 +11,7 @@
 F32 = jnp.float32
 BF16 = jnp.bfloat16
 LANES = 128
+REAL = ()
 
 
 def dot(left, right, contract):
@@ -23,6 +24,9 @@
 
 
 def call(body, name, places, grid, ins, outs, args, scratch=(), flops=0, aliases=()):
+    real = name in REAL
+    size = sum(a.size * a.dtype.itemsize for a in args)
+    size += sum(s.size * s.dtype.itemsize for s, _ in outs)
     return pl.pallas_call(
         body,
         out_shape=[s for s, _ in outs],
@@ -34,7 +38,9 @@
             scratch_shapes=list(scratch),
         ),
         compiler_params=pltpu.CompilerParams(vmem_limit_bytes=24 * 2**20),
-        cost_estimate=pl.CostEstimate(flops=1000, bytes_accessed=1000, transcendentals=0),
+        cost_estimate=pl.CostEstimate(
+            flops=flops if real else 1000, bytes_accessed=size if real else 1000, transcendentals=0
+        ),
         input_output_aliases=dict(aliases),
         name=name,
     )(places, *args)
@@ -939,19 +945,20 @@
 
 
 class Ring:
-    def __init__(self, cells):
-        self.chips, _, self.ahead, self.behind = ring_of(lax.axis_size("seq"))
+    def __init__(self, cells, mirrored):
+        self.chips, _, ahead, behind = ring_of(lax.axis_size("seq"))
         chip = lax.axis_index("seq") // 2
         self.spot = jnp.where(chip % 2 == 0, chip // 2, self.chips - 1 - chip // 2)
         self.reach = self.chips // 2
-        self.half = cells.shape[1] // 2
+        self.ways = (behind, ahead) if mirrored else (ahead, behind)
+        self.sign = -1 if mirrored else 1
         self.cells = cells
         self.count = 0
-        self.up = self.down = None
+        self.here = ()
         self.extra = None
 
     def at(self, step):
-        return (self.spot + step + self.chips) % self.chips
+        return (self.spot + self.sign * step + self.chips) % self.chips
 
     def part(self, step):
         return lax.dynamic_index_in_dim(self.cells, self.at(step), 0, keepdims=False)
@@ -962,42 +969,38 @@
         if self.extra is not None:
             self.gathered.append(some[rows:])
 
-    def send(self, up, down, after):
+    def send(self, cells, after):
         if after:
-            up, down = lax.optimization_barrier((up, down, *after))[:2]
-        self.up = lax.ppermute(up, "seq", self.ahead)
-        self.down = lax.ppermute(down, "seq", self.behind)
+            cells = lax.optimization_barrier((*cells, *after))[: len(cells)]
+        self.sent = tuple(cells)
+        self.here = tuple(lax.ppermute(x, "seq", way) for x, way in zip(cells, self.ways))
 
     def hop(self, *after):
-        reach, half = self.reach, self.half
+        reach = self.reach
         self.count += 1
         left = reach + 1 - self.count
-        u, d = self.up, self.down
         if self.count == 1:
-            self.send(self.part(reach)[half:], self.part(-reach)[:half], after)
+            self.send([self.part(reach)], after)
         elif left > 0:
-            own_u, own_d = self.part(left), self.part(-left)
-            if self.count == 2:
-                u = jnp.concatenate([own_u[:half], add(own_u[half:], u)])
-                d = jnp.concatenate([add(own_d[:half], d), own_d[half:]])
-            else:
-                u, d = add(own_u, u), add(own_d, d)
-            self.send(u, d, after)
+            near = add(self.part(left), self.here[0])
+            far = self.part(-left)
+            if self.count > 2:
+                far = add(far, self.here[1])
+            self.send([near, far], after)
         else:
+            cells = self.here
             if left == 0:
-                own = self.part(0).astype(F32) + u.astype(F32) + d.astype(F32)
-                u = d = own.astype(BF16)
+                own = sum((x.astype(F32) for x in cells), self.part(0).astype(F32)).astype(BF16)
                 if self.extra is not None:
-                    u = d = jnp.concatenate([u, self.extra])
+                    own = jnp.concatenate([own, self.extra])
                     self.gathered = []
-                self.put(u, 0)
-            if left > 1 - reach:
-                self.send(u, d, after)
-                self.put(self.up, left - 1)
-                self.put(self.down, 1 - left)
-            else:
-                self.send(u[half:], d[:half], after)
-                self.put(jnp.concatenate([self.down, self.up]), reach)
+                self.put(own, 0)
+                cells = (own, own)
+            if left == 1 - reach:
+                cells = cells[:1]
+            self.send(cells, after)
+            for x, step in zip(self.here, (left - 1, 1 - left)):
+                self.put(x, step)
 
     def gather(self, extra):
         self.extra = extra
@@ -1063,43 +1066,45 @@
     grads = pair_grads(
         places, chips, (own_v, own_g), (recv_v, recv_g), normed, normed_theirs, scale
     )
-    a = Ring(grads.reshape(chips, -1, 2 * chans))
+    a = Ring(grads.reshape(chips, -1, 2 * chans), False)
     a.hop()
     act, act_theirs = lax.optimization_barrier((act, act_theirs, grads))[:2]
     acts = [act, act_theirs, core_swap(act), core_swap(act_theirs)]
-    cot = tied(cotangent, a.up, a.down)
-    grad_out = out_grads(places, cot, cot_theirs, acts, scale)
-    b = Ring(grad_out.reshape(chips, -1, 2 * chans))
-    b.hop()
-    a.hop()
+    grad_out = out_grads(places, cotangent, cot_theirs, acts, scale)
+    b = Ring(grad_out.reshape(chips, -1, 2 * chans), True)
+
+    def step(*after):
+        there = a.here
+        a.hop()
+        b.hop(*after, *there)
+        return (*a.sent, *b.sent)
+
+    sent = step()
+    own_v = tied(own_v, grad_out, *sent)
     theirs, mine = d_normed_terms(
-        places, [tied(own_v, grad_out), sent_v], [own_g, sent_g], value_weight, gate_weight
+        places, [own_v, sent_v], [own_g, sent_g], value_weight, gate_weight
     )
     recv = other(theirs)
-    b.hop(theirs)
-    a.hop()
-    kernel_grad = taps_grad(places, before, glu, after, tied(d_conv, theirs), scale)
-    b.hop(kernel_grad)
-    a.hop()
-    block_out = out_step(places, frames_in, out_weight, act, tied(act_theirs, kernel_grad))
-    b.hop(block_out)
-    a.hop()
-    sums_in, norm_grad = norm_sums(places, mine, tied(recv, block_out), hat_in, gain)
+    sent = step(theirs)
+    kernel_grad = taps_grad(places, before, glu, after, tied(d_conv, theirs, *sent), scale)
+    sent = step(kernel_grad)
+    act_theirs = tied(act_theirs, kernel_grad, *sent)
+    block_out = out_step(places, frames_in, out_weight, act, act_theirs)
+    sent = step(block_out)
+    sums_in, norm_grad = norm_sums(places, mine, tied(recv, block_out, *sent), hat_in, gain)
     sums_in_theirs = other(sums_in)
     small = jnp.concatenate([kernel_grad, gain_grad * scale, norm_grad * scale])
     small = small + core_swap(small)
     depth = (taps + 2 + 15) // 16 * 8
     small = jnp.pad(small, ((0, 2 * depth - taps - 2), (0, 0)))
     b.gather(jnp.concatenate([small[:depth], small[depth:]], axis=1).astype(BF16))
-    b.hop()
+    sent = step()
+    sums_in_theirs = tied(sums_in_theirs, *sent)
     input_grad = input_step(
         places, mine, recv, hat_in, gain, inv_in, sums_in, sums_in_theirs, cotangent
     )
-    a.hop()
-    b.hop(input_grad)
-    a.hop()
-    b.hop()
-    a.hop()
+    step(input_grad)
+    step()
     b.hop()
     small = sum(some.astype(F32) for some in b.gathered)
     small = jnp.concatenate([small[:, :chans], small[:, chans:]])

time: 201 us -> 187 us (0.930)
  waiting for transfers between devices: 63.6 us -> 52.5 us
  starting transfers between devices: 57 us -> 53.7 us
    ppermute x32 -> x28, waiting for transfers between devices: 41.7 us -> 29.1 us  [send(): lax.ppermute(x, 'seq', way)]
    ppermute x32 -> x28, starting transfers between devices: 35.2 us -> 33.3 us  [send(): lax.ppermute(x, 'seq', way)]
    unnamed x57 -> x75, local copies, waits for them, and re-layouts: 9.47 us -> 9.53 us
  transfers between devices with their start and end apart: 53 -> 49, of which waited for: 21 -> 20; matrix products, arithmetic and copies ran while one was open for 1% -> 2% of each run, Pallas kernels for 28% -> 30%
where the time goes in v4:
time: 187 us; the launch traced here: 186 us
  Pallas kernels  63.9 us (34%)
  starting transfers between devices  53.7 us (29%)
  waiting for transfers between devices  52.5 us (28%)
  local copies, waits for them, and re-layouts  12.1 us (6%)
  other arithmetic  2.57 us (1%)
    pallas_call x17, Pallas kernels, call(): pl.pallas_call(body, out_shape=[s for s, _ in outs], grid_spec=pltpu.Pref...  63.9 us
    ppermute x28, starting transfers between devices, send(): lax.ppermute(x, 'seq', way)  33.3 us
    ppermute x28, waiting for transfers between devices, send(): lax.ppermute(x, 'seq', way)  29.1 us
    ppermute x8, waiting for transfers between devices, other(): return lax.ppermute(values, 'tp', [(0, 1), (1, 0)])  17.6 us
    ppermute x8, starting transfers between devices, other(): return lax.ppermute(values, 'tp', [(0, 1), (1, 0)])  10.2 us
    unnamed x75, local copies, waits for them, and re-layouts  9.53 us
    ppermute x2, starting transfers between devices, rims(): before = lax.ppermute(tail, 'seq', [(i, i + 1) for i in range(count - 1)])  5.15 us
  transfers between devices with their start and end apart: 49, of which 20 were waited for; matrix products, arithmetic and copies ran while one was open for 2% of the time, Pallas kernels for 30%

profile of v4, /device:TPU:0, one launch (start us, length us, event | category | flops | bytes accessed | tf_op | source)
XLA Modules:
  0.0 186.3 jit_solution(15943771059817951440)
XLA Ops:
  3.3 3.0 %collective-permute-start = (bf16[784,256]{1,0:T(8,128)(2,1)S(1)}, bf16[784,256]{1,0:T(8,128)(2,1)S(1)}, u32[]{:S(2)}, u32[]{:S(2)}) collective-permute-start(bf16[784,256]{1,0:T(8,128)(2,1)S(1)} %pack_edges.1.xm), channel_id=1, source_target_pairs={{0,1},{1,0},{2,3},{3,2},{4,5},{5,4},{6,7},{7,6},{8,9},{9,8},{10,11... | collective-permute-start | bytes 1204232 | tf_op jit(solution)/shard_map/ppermute | solution.py:785
  11.4 5.0 %collective-permute-done.xt.gt = bf16[784,256]{1,0:T(8,128)(2,1)S(1)} collective-permute-done((bf16[784,256]{1,0:T(8,128)(2,1)S(1)}, bf16[784,256]{1,0:T(8,128)(2,1)S(1)}, u32[]{:S(2)}, u32[]{:S(2)}) %collective-permute-start) | collective-permute-done | bytes 401440 | tf_op jit(solution)/shard_map/ppermute | solution.py:785
  17.4 4.0 %glu_edges.1 = (bf16[512,1536]{1,0:T(8,128)(2,1)}, f32[512,768]{1,0:T(8,128)S(1)}, f32[512,128]{1,0:T(8,128)S(1)}, bf16[512,768]{1,0:T(8,128)(2,1)S(1)}, f32[512...) custom-call(s32[4]{0:T(128)S(1)} %pad_add_fusion.p, bf16[784,256]{1,0:T(8,128)(2,1)S(1)} %copy-done.19, ...), custom_call_target="tpu_custom_call" | custom-call | flops 1000 | bytes 1000 | tf_op jit(solution)/shard_map/glu_edges/pallas_call | solution.py:30
  24.0 4.0 %glu_middle.1 = (bf16[512,1536]{1,0:T(8,128)(2,1)}, f32[512,768]{1,0:T(8,128)S(1)}, f32[512,128]{1,0:T(8,128)S(1)}, bf16[512,768]{1,0:T(8,128)(2,1)S(1)}, f32[51...) custom-call(s32[4]{0:T(128)S(1)} %pad_add_fusion.p, ...), custom_call_target="tpu_custom_call", output_to_operand_aliasing={{0}: (7, {}), {1}: (8, {}), {2}: (9, {}), {3}: (10, {}), {4... | custom-call | flops 1000 | bytes 1000 | tf_op jit(solution)/shard_map/glu_middle/pallas_call | solution.py:30
  36.7 5.8 %conv_forward.1 = (f32[512,768]{1,0:T(8,128)S(1)}, f32[8,512]{1,0:T(8,128)S(1)}) custom-call(s32[4]{0:T(128)S(1)} %pad_add_fusion.p, bf16[16,768]{1,0:T(8,128)(2,1)S(1)} %collective-permute-done.2.b, bf16[512,768]{1,0:T(8,128)(2,1)S(1)} %get-tuple-element.77.g, bf16[16,768]{1,0:T(8,128)(2,1)S(1)} %collective-permute-done.4.a, f32[32,768]{1,0:T(8,128)S(1)} %bitcast.123), custom_call_target="tpu_custom_call" | custom-call | flops 1000 | bytes 1000 | tf_op jit(solution)/shard_map/conv_forward/pallas_call | solution.py:30
  43.0 6.0 %collective-permute-done.5.st = f32[8,512]{1,0:T(8,128)S(1)} collective-permute-done((f32[8,512]{1,0:T(8,128)S(1)}, f32[8,512]{1,0:T(8,128)S(1)}, u32[]{:S(2)}, u32[]{:S(2)}) %collective-permute-start.5) | collective-permute-done | bytes 16416 | tf_op jit(solution)/shard_map/ppermute | solution.py:785
  49.1 2.7 %act_step.1 = (f32[512,768]{1,0:T(8,128)S(1)}, f32[512,768]{1,0:T(8,128)S(1)}, f32[8,512]{1,0:T(8,128)S(1)}, f32[1,768]{1,0:T(1,128)S(1)}) custom-call(s32[4]{0:T(128)S(1)} %pad_add_fusion.p, f32[512,768]{1,0:T(8,128)S(1)} %get-tuple-element.78.x, f32[8,512]{1,0:T(8,128)S(1)} %get-tuple-element.79.sm, f32[8,512]{1,0:T(8,128)S(1)} %collective-permute-done.5.st, ...), custom_call_target="tpu_custom_call" | custom-call | flops 1000 | bytes 1000 | tf_op jit(solution)/shard_map/act_step/pallas_call | solution.py:30
  55.6 3.2 %d_conv_step.1 = (bf16[512,768]{1,0:T(8,128)(2,1)S(1)}, bf16[512,768]{1,0:T(8,128)(2,1)}, bf16[16,768]{1,0:T(8,128)(2,1)S(1)}, bf16[16,768]{1,0:T(8,128)(2,1)S(1)}) custom-call(s32[4]{0:T(128)S(1)} %pad_add_fusion.p, f32[512,768]{1,0:T(8,128)S(1)} %get-tuple-element.81.d, f32[512,768]{1,0:T(8,128)S(1)} %get-tuple-element.82.h, ...), custom_call_target="tpu_custom_call" | custom-call | flops 1000 | bytes 1000 | tf_op jit(solution)/shard_map/d_conv_step/pallas_call | solution.py:30
  60.1 3.0 %collective-permute-start.9 = (bf16[16,768]{1,0:T(8,128)(2,1)S(1)}, bf16[16,768]{1,0:T(8,128)(2,1)S(1)}, u32[]{:S(2)}, u32[]{:S(2)}) collective-permute-start(bf16[16,768]{1,0:T(8,128)(2,1)S(1)} %get-tuple-element.85), channel_id=1, source_target_pairs={{0,2},{2,4},{4,6},{6,8},{8,10},{10,12},{12,14},{14,16},{16,18},{18... | collective-permute-start | bytes 73736 | tf_op jit(solution)/shard_map/ppermute | solution.py:938
  64.0 3.9 %d_glu_other.1 = (bf16[512,384]{1,0:T(8,128)(2,1)}, bf16[512,384]{1,0:T(8,128)(2,1)}) custom-call(s32[4]{0:T(128)S(1)} %pad_add_fusion.p, bf16[16,768]{1,0:T(8,128)(2,1)S(1)} %collective-permute-done.9.b, bf16[512,768]{1,0:T(8,128)(2,1)S(1)} %get-tuple-element.103.d, bf16[16,768]{1,0:T(8,128)(2,1)S(1)} %collective-permute-done.10.a, ...), custom_call_target="tpu_custom_call" | custom-call | flops 1000 | bytes 1000 | tf_op jit(solution)/shard_map/d_glu_other/pallas_call | solution.py:30
  74.5 3.3 %d_glu_own.1 = (bf16[512,384]{1,0:T(8,128)(2,1)S(1)}, bf16[512,384]{1,0:T(8,128)(2,1)S(1)}) custom-call(s32[4]{0:T(128)S(1)} %pad_add_fusion.p, bf16[16,768]{1,0:T(8,128)(2,1)S(1)} %copy-done.31, bf16[512,768]{1,0:T(8,128)(2,1)S(1)} %copy-done.14, bf16[16,768]{1,0:T(8,128)(2,1)S(1)} %copy-done.29, f32[32,768]{1,0:T(8,128)S(1)} %bitcast.125, ...), custom_call_target="tpu_custom_call" | custom-call | flops 1000 | bytes 1000 | tf_op jit(solution)/shard_map/d_glu_own/pallas_call | solution.py:30
  77.9 5.8 %pair_grads.1 = bf16[8,2,48,1536]{3,2,1,0:T(8,128)(2,1)S(1)} custom-call(s32[4]{0:T(128)S(1)} %pad_add_fusion.p, bf16[512,384]{1,0:T(8,128)(2,1)S(1)} %get-tuple-element.99.mv.vo, bf16[512,384]{1,0:T(8,128)(2,1)S(1)} %get-tuple-element.93.mg.go, bf16[512,384]{1,0:T(8,128)(2,1)} %collective-permute-done.11.tv, bf16[512,384]{1,0:T(8,128)(2,1)} %collective-permute-done.12.tg, ...), custom_call_target="tpu_custom_call" | custom-call | flops 1000 | bytes 1000 | tf_op jit(solution)/shard_map/pair_grads/pallas_call | solution.py:30
  84.6 3.6 %collective-permute-start.16 = (bf16[96,1536]{1,0:T(8,128)(2,1)}, bf16[96,1536]{1,0:T(8,128)(2,1)}, u32[]{:S(2)}, u32[]{:S(2)}) collective-permute-start(bf16[96,1536]{1,0:T(8,128)(2,1)} %get-tuple-element.135), channel_id=1, source_target_pairs={{0,8},{2,10},{8,16},{10,18},{16,24},{18,26},{24,28},{26,30},{28,20... | collective-permute-start | bytes 884744 | tf_op jit(solution)/shard_map/ppermute | solution.py:976
  99.3 4.4 %out_grads.1 = bf16[384,1536]{1,0:T(8,128)(2,1)S(1)} custom-call(s32[4]{0:T(128)S(1)} %pad_add_fusion.p, bf16[768,512]{1,0:T(8,128)(2,1)S(1)} %copy-done.10, bf16[384,512]{1,0:T(8,128)(2,1)S(1)} %copy-done.27, bf16[512,768]{1,0:T(8,128)(2,1)} %get-tuple-element.96.a, bf16[512,768]{1,0:T(8,128)(2,1)} %collective-permute-done.8.b, ...), custom_call_target="tpu_custom_call" | custom-call | flops 1000 | bytes 1000 | tf_op jit(solution)/shard_map/out_grads/pallas_call | solution.py:30
  106.3 5.6 %d_normed_terms.1 = (bf16[512,768]{1,0:T(8,128)(2,1)S(1)}, bf16[512,768]{1,0:T(8,128)(2,1)S(1)}) custom-call(s32[4]{0:T(128)S(1)} %pad_add_fusion.p, bf16[512,384]{1,0:T(8,128)(2,1)S(1)} %get-tuple-element.99.mv.vo, bf16[512,384]{1,0:T(8,128)(2,1)} %get-tuple-element.90.vt, bf16[512,384]{1,0:T(8,128)(2,1)S(1)} %copy-done.21, ...), custom_call_target="tpu_custom_call" | custom-call | flops 1000 | bytes 1000 | tf_op jit(solution)/shard_map/d_normed_terms/pallas_call | solution.py:30
  118.5 5.3 %taps_grad.1 = f32[32,768]{1,0:T(8,128)S(1)} custom-call(s32[4]{0:T(128)S(1)} %pad_add_fusion.p, bf16[16,768]{1,0:T(8,128)(2,1)S(1)} %copy-done.33, bf16[512,768]{1,0:T(8,128)(2,1)S(1)} %copy-done.17, bf16[16,768]{1,0:T(8,128)(2,1)S(1)} %copy-done.35, bf16[512,768]{1,0:T(8,128)(2,1)S(1)} %copy-done.15), custom_call_target="tpu_custom_call" | custom-call | flops 1000 | bytes 1000 | tf_op jit(solution)/shard_map/taps_grad/pallas_call | solution.py:30
  125.9 4.5 %out_step.1 = bf16[768,512]{1,0:T(8,128)(2,1)} custom-call(s32[4]{0:T(128)S(1)} %pad_add_fusion.p, bf16[768,512]{1,0:T(8,128)(2,1)S(1)} %copy-done.8, bf16[768,1536]{1,0:T(8,128)(2,1)S(1)} %copy-done.12, bf16[512,768]{1,0:T(8,128)(2,1)} %get-tuple-element.96.a, bf16[512,768]{1,0:T(8,128)(2,1)} %collective-permute-done.8.b), custom_call_target="tpu_custom_call" | custom-call | flops 1000 | bytes 1000 | tf_op jit(solution)/shard_map/out_step/pallas_call | solution.py:30
  134.9 7.3 %collective-permute-done.32 = bf16[48,1536]{1,0:T(8,128)(2,1)S(1)} collective-permute-done((bf16[48,1536]{1,0:T(8,128)(2,1)S(1)}, bf16[48,1536]{1,0:T(8,128)(2,1)S(1)}, u32[]{:S(2)}, u32[]{:S(2)}) %collective-permute-start.32) | collective-permute-done | bytes 147488 | tf_op jit(solution)/shard_map/ppermute | solution.py:976
  149.9 3.2 %input_step.1 = bf16[768,512]{1,0:T(8,128)(2,1)} custom-call(s32[4]{0:T(128)S(1)} %pad_add_fusion.p, bf16[512,768]{1,0:T(8,128)(2,1)S(1)} %get-tuple-element.107.tm, bf16[512,768]{1,0:T(8,128)(2,1)S(1)} %collective-permute-done.24.tr, f32[512,768]{1,0:T(8,128)S(1)} %copy-done.5, f32[1,768]{1,0:T(1,128)S(1)} %broadcast_in_dim.41.g.gm, ...), custom_call_target="tpu_custom_call" | custom-call | flops 1000 | bytes 1000 | tf_op jit(solution)/shard_map/input_step/pallas_call | solution.py:30
  157.4 5.6 %collective-permute-done.41 = bf16[96,1536]{1,0:T(8,128)(2,1)S(1)} collective-permute-done((bf16[96,1536]{1,0:T(8,128)(2,1)S(1)}, bf16[96,1536]{1,0:T(8,128)(2,1)S(1)}, u32[]{:S(2)}, u32[]{:S(2)}) %collective-permute-start.41) | collective-permute-done | bytes 294944 | tf_op jit(solution)/shard_map/ppermute | solution.py:976
  164.4 3.0 %collective-permute-done.39 = bf16[72,1536]{1,0:T(8,128)(2,1)S(1)} collective-permute-done((bf16[72,1536]{1,0:T(8,128)(2,1)S(1)}, bf16[72,1536]{1,0:T(8,128)(2,1)S(1)}, u32[]{:S(2)}, u32[]{:S(2)}) %collective-permute-start.39) | collective-permute-done | bytes 221216 | tf_op jit(solution)/shard_map/ppermute | solution.py:976
  169.8 3.9 %collective-permute-done.43 = bf16[72,1536]{1,0:T(8,128)(2,1)S(1)} collective-permute-done((bf16[72,1536]{1,0:T(8,128)(2,1)S(1)}, bf16[72,1536]{1,0:T(8,128)(2,1)S(1)}, u32[]{:S(2)}, u32[]{:S(2)}) %collective-permute-start.43) | collective-permute-done | bytes 221216 | tf_op jit(solution)/shard_map/ppermute | solution.py:976
  174.4 3.0 %collective-permute-done.44 = bf16[72,1536]{1,0:T(8,128)(2,1)S(1)} collective-permute-done((bf16[72,1536]{1,0:T(8,128)(2,1)S(1)}, bf16[72,1536]{1,0:T(8,128)(2,1)S(1)}, u32[]{:S(2)}, u32[]{:S(2)}) %collective-permute-start.44) | collective-permute-done | bytes 221216 | tf_op jit(solution)/shard_map/ppermute | solution.py:976
  182.6 3.5 %join_halves.1 = (bf16[2,8,48,1536]{3,2,1,0:T(8,128)(2,1)}, bf16[2,8,48,1536]{3,2,1,0:T(8,128)(2,1)}, bf16[2,8,48,1536]{3,2,1,0:T(8,128)(2,1)}) custom-call(s32[4]{0:T(128)S(1)} %pad_add_fusion.p, bf16[8,2,48,1536]{3,2,1,0:T(8,128)(2,1)S(1)} %bitcast.116, bf16[8,2,48,1536]{3,2,1,0:T(8,128)(2,1)S(1)} %collective-permute-done.47.at, ...), custom_call_target="tpu_custom_call" | custom-call | flops 1000 | bytes 1000 | tf_op jit(solution)/shard_map/join_halves/pallas_call | solution.py:30
  (207 shorter events, 81.9 us)
Async XLA Ops:
  3.3 13.1 %collective-permute-start = (bf16[784,256]{1,0:T(8,128)(2,1)S(1)}, bf16[784,256]{1,0:T(8,128)(2,1)S(1)}, u32[]{:S(2)}, u32[]{:S(2)}) collective-permute-start(bf16[784,256]{1,0:T(8,128)(2,1)S(1)} %pack_edges.1.xm), channel_id=1, source_target_pairs={{0,1},{1,0},{2,3},{3,2},{4,5},{5,4},{6,7},{7,6},{8,9},{9,8},{10,11... | collective-permute-start | bytes 1204232 | tf_op jit(solution)/shard_map/ppermute | solution.py:785
  6.5 17.5 %collective-permute-start.3 = (bf16[768,256]{1,0:T(8,128)(2,1)S(1)}, bf16[768,256]{1,0:T(8,128)(2,1)S(1)}, u32[]{:S(2)}, u32[]{:S(2)}) collective-permute-start(bf16[768,256]{1,0:T(8,128)(2,1)S(1)} %slice.77.xm), channel_id=1, source_target_pairs={{0,1},{1,0},{2,3},{3,2},{4,5},{5,4},{6,7},{7,6},{8,9},{9,8},{10,11... | collective-permute-start | bytes 1179656 | tf_op jit(solution)/shard_map/ppermute | solution.py:785
  28.8 49.1 %collective-permute-start.13 = (bf16[512,1536]{1,0:T(8,128)(2,1)}, bf16[512,1536]{1,0:T(8,128)(2,1)}, u32[]{:S(2)}, u32[]{:S(2)}) collective-permute-start(bf16[512,1536]{1,0:T(8,128)(2,1)} %get-tuple-element.95.n), channel_id=1, source_target_pairs={{0,2},{2,0},{4,6},{6,4},{8,10},{10,8},{12,14},{14,12},{16,18},{18,... | collective-permute-start | bytes 4718600 | tf_op jit(solution)/shard_map/ppermute | solution.py:933
  28.8 20.3 %collective-permute-start.6 = (bf16[512,768]{1,0:T(8,128)(2,1)S(1)}, bf16[512,768]{1,0:T(8,128)(2,1)S(1)}, u32[]{:S(2)}, u32[]{:S(2)}) collective-permute-start(bf16[512,768]{1,0:T(8,128)(2,1)S(1)} %get-tuple-element.68), channel_id=1, source_target_pairs={{0,1},{1,0},{2,3},{3,2},{4,5},{5,4},{6,7},{7,6},{8,9},{9,8},{10,11... | collective-permute-start | bytes 2359304 | tf_op jit(solution)/shard_map/ppermute | solution.py:785
  67.9 9.9 %collective-permute-start.11 = (bf16[512,384]{1,0:T(8,128)(2,1)}, bf16[512,384]{1,0:T(8,128)(2,1)}, u32[]{:S(2)}, u32[]{:S(2)}) collective-permute-start(bf16[512,384]{1,0:T(8,128)(2,1)} %get-tuple-element.90.vt), channel_id=1, source_target_pairs={{0,2},{2,0},{4,6},{6,4},{8,10},{10,8},{12,14},{14,12},{16,18},{18,... | collective-permute-start | bytes 1179656 | tf_op jit(solution)/shard_map/ppermute | solution.py:933
  69.5 20.2 %collective-permute-start.8 = (bf16[512,768]{1,0:T(8,128)(2,1)}, bf16[512,768]{1,0:T(8,128)(2,1)}, u32[]{:S(2)}, u32[]{:S(2)}) collective-permute-start(bf16[512,768]{1,0:T(8,128)(2,1)} %get-tuple-element.96.a), channel_id=1, source_target_pairs={{0,1},{1,0},{2,3},{3,2},{4,5},{5,4},{6,7},{7,6},{8,9},{9,8},{10,11... | collective-permute-start | bytes 2359304 | tf_op jit(solution)/shard_map/ppermute | solution.py:785
  84.6 10.1 %collective-permute-start.16 = (bf16[96,1536]{1,0:T(8,128)(2,1)}, bf16[96,1536]{1,0:T(8,128)(2,1)}, u32[]{:S(2)}, u32[]{:S(2)}) collective-permute-start(bf16[96,1536]{1,0:T(8,128)(2,1)} %get-tuple-element.135), channel_id=1, source_target_pairs={{0,8},{2,10},{8,16},{10,18},{16,24},{18,26},{24,28},{26,30},{28,20... | collective-permute-start | bytes 884744 | tf_op jit(solution)/shard_map/ppermute | solution.py:976
  90.3 13.5 %collective-permute-start.18 = (bf16[96,1536]{1,0:T(8,128)(2,1)}, bf16[96,1536]{1,0:T(8,128)(2,1)S(1)}, u32[]{:S(2)}, u32[]{:S(2)}) collective-permute-start(bf16[96,1536]{1,0:T(8,128)(2,1)} %get-tuple-element.134), channel_id=1, source_target_pairs={{8,0},{10,2},{16,8},{18,10},{24,16},{26,18},{28,24},{30,26},{20,28... | collective-permute-start | bytes 884744 | tf_op jit(solution)/shard_map/ppermute | solution.py:976
  104.0 10.9 %collective-permute-start.20 = (bf16[96,1536]{1,0:T(8,128)(2,1)S(1)}, bf16[96,1536]{1,0:T(8,128)(2,1)S(1)}, u32[]{:S(2)}, u32[]{:S(2)}) collective-permute-start(bf16[96,1536]{1,0:T(8,128)(2,1)S(1)} %get-tuple-element.133), channel_id=1, source_target_pairs={{0,8},{2,10},{8,16},{10,18},{16,24},{18,26},{24,28},{26,30},{28,20... | collective-permute-start | bytes 884744 | tf_op jit(solution)/shard_map/ppermute | solution.py:976
  106.3 9.9 %collective-permute-start.21 = (bf16[96,1536]{1,0:T(8,128)(2,1)S(1)}, bf16[96,1536]{1,0:T(8,128)(2,1)S(1)}, u32[]{:S(2)}, u32[]{:S(2)}) collective-permute-start(bf16[96,1536]{1,0:T(8,128)(2,1)S(1)} %get-tuple-element.132), channel_id=1, source_target_pairs={{8,0},{10,2},{16,8},{18,10},{24,16},{26,18},{28,24},{30,26},{20,28... | collective-permute-start | bytes 884744 | tf_op jit(solution)/shard_map/ppermute | solution.py:976
  112.1 32.3 %collective-permute-start.24 = (bf16[512,768]{1,0:T(8,128)(2,1)S(1)}, bf16[512,768]{1,0:T(8,128)(2,1)S(1)}, u32[]{:S(2)}, u32[]{:S(2)}) collective-permute-start(bf16[512,768]{1,0:T(8,128)(2,1)S(1)} %get-tuple-element.100), channel_id=1, source_target_pairs={{0,1},{1,0},{2,3},{3,2},{4,5},{5,4},{6,7},{7,6},{8,9},{9,8},{10,11... | collective-permute-start | bytes 2359304 | tf_op jit(solution)/shard_map/ppermute | solution.py:785
  112.7 11.0 %collective-permute-start.22 = (bf16[48,1536]{1,0:T(8,128)(2,1)S(1)}, bf16[48,1536]{1,0:T(8,128)(2,1)S(1)}, u32[]{:S(2)}, u32[]{:S(2)}) collective-permute-start(bf16[48,1536]{1,0:T(8,128)(2,1)S(1)} %fusion.13), channel_id=1, source_target_pairs={{8,0},{10,2},{16,8},{18,10},{24,16},{26,18},{28,24},{30,26},{20,28... | collective-permute-start | bytes 442376 | tf_op jit(solution)/shard_map/ppermute | solution.py:976
  113.8 9.9 %collective-permute-start.23 = (bf16[48,1536]{1,0:T(8,128)(2,1)S(1)}, bf16[48,1536]{1,0:T(8,128)(2,1)S(1)}, u32[]{:S(2)}, u32[]{:S(2)}) collective-permute-start(bf16[48,1536]{1,0:T(8,128)(2,1)S(1)} %get-tuple-element.102), channel_id=1, source_target_pairs={{0,8},{2,10},{8,16},{10,18},{16,24},{18,26},{24,28},{26,30},{28,20... | collective-permute-start | bytes 442376 | tf_op jit(solution)/shard_map/ppermute | solution.py:976
  116.4 14.1 %collective-permute-start.25 = (bf16[96,1536]{1,0:T(8,128)(2,1)S(1)}, bf16[96,1536]{1,0:T(8,128)(2,1)S(1)}, u32[]{:S(2)}, u32[]{:S(2)}) collective-permute-start(bf16[96,1536]{1,0:T(8,128)(2,1)S(1)} %get-tuple-element.131), channel_id=1, source_target_pairs={{0,8},{2,10},{8,16},{10,18},{16,24},{18,26},{24,28},{26,30},{28,20... | collective-permute-start | bytes 884744 | tf_op jit(solution)/shard_map/ppermute | solution.py:976
  117.9 12.6 %collective-permute-start.26 = (bf16[96,1536]{1,0:T(8,128)(2,1)S(1)}, bf16[96,1536]{1,0:T(8,128)(2,1)S(1)}, u32[]{:S(2)}, u32[]{:S(2)}) collective-permute-start(bf16[96,1536]{1,0:T(8,128)(2,1)S(1)} %get-tuple-element.130), channel_id=1, source_target_pairs={{8,0},{10,2},{16,8},{18,10},{24,16},{26,18},{28,24},{30,26},{20,28... | collective-permute-start | bytes 884744 | tf_op jit(solution)/shard_map/ppermute | solution.py:976
  130.6 11.6 %collective-permute-start.30 = (bf16[96,1536]{1,0:T(8,128)(2,1)S(1)}, bf16[96,1536]{1,0:T(8,128)(2,1)S(1)}, u32[]{:S(2)}, u32[]{:S(2)}) collective-permute-start(bf16[96,1536]{1,0:T(8,128)(2,1)S(1)} %fusion.1), channel_id=1, source_target_pairs={{0,8},{2,10},{8,16},{10,18},{16,24},{18,26},{24,28},{26,30},{28,20... | collective-permute-start | bytes 884744 | tf_op jit(solution)/shard_map/ppermute | solution.py:976
  132.2 11.5 %collective-permute-start.31 = (bf16[96,1536]{1,0:T(8,128)(2,1)S(1)}, bf16[96,1536]{1,0:T(8,128)(2,1)S(1)}, u32[]{:S(2)}, u32[]{:S(2)}) collective-permute-start(bf16[96,1536]{1,0:T(8,128)(2,1)S(1)} %fusion.1), channel_id=1, source_target_pairs={{8,0},{10,2},{16,8},{18,10},{24,16},{26,18},{28,24},{30,26},{20,28... | collective-permute-start | bytes 884744 | tf_op jit(solution)/shard_map/ppermute | solution.py:976
  142.3 10.8 %collective-permute-start.37 = (bf16[96,1536]{1,0:T(8,128)(2,1)S(1)}, bf16[96,1536]{1,0:T(8,128)(2,1)S(1)}, u32[]{:S(2)}, u32[]{:S(2)}) collective-permute-start(bf16[96,1536]{1,0:T(8,128)(2,1)S(1)} %collective-permute-done.30), channel_id=1, source_target_pairs={{0,8},{2,10},{8,16},{10,18},{16,24},{18,26},{24,28},{26,30},{28,20... | collective-permute-start | bytes 884744 | tf_op jit(solution)/shard_map/ppermute | solution.py:976
  143.7 10.7 %collective-permute-start.38 = (bf16[96,1536]{1,0:T(8,128)(2,1)S(1)}, bf16[96,1536]{1,0:T(8,128)(2,1)S(1)}, u32[]{:S(2)}, u32[]{:S(2)}) collective-permute-start(bf16[96,1536]{1,0:T(8,128)(2,1)S(1)} %collective-permute-done.31), channel_id=1, source_target_pairs={{8,0},{10,2},{16,8},{18,10},{24,16},{26,18},{28,24},{30,26},{20,28... | collective-permute-start | bytes 884744 | tf_op jit(solution)/shard_map/ppermute | solution.py:976
  153.0 9.9 %collective-permute-start.41 = (bf16[96,1536]{1,0:T(8,128)(2,1)S(1)}, bf16[96,1536]{1,0:T(8,128)(2,1)S(1)}, u32[]{:S(2)}, u32[]{:S(2)}) collective-permute-start(bf16[96,1536]{1,0:T(8,128)(2,1)S(1)} %collective-permute-done.37), channel_id=1, source_target_pairs={{0,8},{2,10},{8,16},{10,18},{16,24},{18,26},{24,28},{26,30},{28,20... | collective-permute-start | bytes 884744 | tf_op jit(solution)/shard_map/ppermute | solution.py:976
  154.4 10.0 %collective-permute-start.42 = (bf16[96,1536]{1,0:T(8,128)(2,1)S(1)}, bf16[96,1536]{1,0:T(8,128)(2,1)S(1)}, u32[]{:S(2)}, u32[]{:S(2)}) collective-permute-start(bf16[96,1536]{1,0:T(8,128)(2,1)S(1)} %collective-permute-done.38), channel_id=1, source_target_pairs={{8,0},{10,2},{16,8},{18,10},{24,16},{26,18},{28,24},{30,26},{20,28... | collective-permute-start | bytes 884744 | tf_op jit(solution)/shard_map/ppermute | solution.py:976
  155.3 12.1 %collective-permute-start.39 = (bf16[72,1536]{1,0:T(8,128)(2,1)S(1)}, bf16[72,1536]{1,0:T(8,128)(2,1)S(1)}, u32[]{:S(2)}, u32[]{:S(2)}) collective-permute-start(bf16[72,1536]{1,0:T(8,128)(2,1)S(1)} %collective-permute-done.35), channel_id=1, source_target_pairs={{8,0},{10,2},{16,8},{18,10},{24,16},{26,18},{28,24},{30,26},{20,28... | collective-permute-start | bytes 663560 | tf_op jit(solution)/shard_map/ppermute | solution.py:976
  155.8 11.9 %collective-permute-start.40 = (bf16[72,1536]{1,0:T(8,128)(2,1)S(1)}, bf16[72,1536]{1,0:T(8,128)(2,1)S(1)}, u32[]{:S(2)}, u32[]{:S(2)}) collective-permute-start(bf16[72,1536]{1,0:T(8,128)(2,1)S(1)} %collective-permute-done.36), channel_id=1, source_target_pairs={{0,8},{2,10},{8,16},{10,18},{16,24},{18,26},{24,28},{26,30},{28,20... | collective-permute-start | bytes 663560 | tf_op jit(solution)/shard_map/ppermute | solution.py:976
  163.0 11.3 %collective-permute-start.46 = (bf16[96,1536]{1,0:T(8,128)(2,1)S(1)}, bf16[96,1536]{1,0:T(8,128)(2,1)S(1)}, u32[]{:S(2)}, u32[]{:S(2)}) collective-permute-start(bf16[96,1536]{1,0:T(8,128)(2,1)S(1)} %collective-permute-done.41), channel_id=1, source_target_pairs={{0,8},{2,10},{8,16},{10,18},{16,24},{18,26},{24,28},{26,30},{28,20... | collective-permute-start | bytes 884744 | tf_op jit(solution)/shard_map/ppermute | solution.py:976
  (62 other events, 445.5 us)

commit v5 on v4

--- a/solution.py
+++ b/solution.py
@@ -979,18 +979,20 @@
         reach = self.reach
         self.count += 1
         left = reach + 1 - self.count
-        if self.count == 1:
-            self.send([self.part(reach)], after)
-        elif left > 0:
-            near = add(self.part(left), self.here[0])
-            far = self.part(-left)
-            if self.count > 2:
-                far = add(far, self.here[1])
-            self.send([near, far], after)
+        if left > 0:
+            cells = [self.part(left)]
+            if left > 1:
+                cells.append(self.part(1 - left))
+            else:
+                self.early = self.here[1]
+            if self.count > 1:
+                cells = [add(mine, there) for mine, there in zip(cells, self.here)]
+            self.send(cells, after)
         else:
             cells = self.here
             if left == 0:
-                own = sum((x.astype(F32) for x in cells), self.part(0).astype(F32)).astype(BF16)
+                own = self.part(0).astype(F32) + self.here[0].astype(F32)
+                own = (own + self.early.astype(F32)).astype(BF16)
                 if self.extra is not None:
                     own = jnp.concatenate([own, self.extra])
                     self.gathered = []
@@ -1088,10 +1090,8 @@
     sent = step(theirs)
     kernel_grad = taps_grad(places, before, glu, after, tied(d_conv, theirs, *sent), scale)
     sent = step(kernel_grad)
-    act_theirs = tied(act_theirs, kernel_grad, *sent)
-    block_out = out_step(places, frames_in, out_weight, act, act_theirs)
-    sent = step(block_out)
-    sums_in, norm_grad = norm_sums(places, mine, tied(recv, block_out, *sent), hat_in, gain)
+    sent = step()
+    sums_in, norm_grad = norm_sums(places, mine, tied(recv, kernel_grad, *sent), hat_in, gain)
     sums_in_theirs = other(sums_in)
     small = jnp.concatenate([kernel_grad, gain_grad * scale, norm_grad * scale])
     small = small + core_swap(small)
@@ -1103,8 +1103,10 @@
     input_grad = input_step(
         places, mine, recv, hat_in, gain, inv_in, sums_in, sums_in_theirs, cotangent
     )
-    step(input_grad)
-    step()
+    sent = step(input_grad)
+    act_theirs = tied(act_theirs, kernel_grad, *sent)
+    block_out = out_step(places, frames_in, out_weight, act, act_theirs)
+    step(block_out)
     b.hop()
     small = sum(some.astype(F32) for some in b.gathered)
     small = jnp.concatenate([small[:, :chans], small[:, chans:]])

time: 187 us -> 182 us (0.973)
  waiting for transfers between devices: 52.5 us -> 46.4 us
    ppermute x28, waiting for transfers between devices: 29.1 us -> 24.2 us  [send(): lax.ppermute(x, 'seq', way)]
  transfers between devices with their start and end apart: 49 -> 49, of which waited for: 20 -> 21; matrix products, arithmetic and copies ran while one was open for 2% -> 2% of each run, Pallas kernels for 30% -> 31%
where the time goes in v5:
time: 182 us
  Pallas kernels  63.8 us (35%)
  starting transfers between devices  55.3 us (30%)
  waiting for transfers between devices  46.4 us (25%)
  local copies, waits for them, and re-layouts  12.1 us (7%)
  other arithmetic  2.59 us (1%)
    pallas_call x17, Pallas kernels, call(): pl.pallas_call(body, out_shape=[s for s, _ in outs], grid_spec=pltpu.Pref...  63.8 us
    ppermute x28, starting transfers between devices, send(): lax.ppermute(x, 'seq', way)  33.7 us
    ppermute x28, waiting for transfers between devices, send(): lax.ppermute(x, 'seq', way)  24.2 us
    ppermute x8, waiting for transfers between devices, other(): return lax.ppermute(values, 'tp', [(0, 1), (1, 0)])  17.2 us
    ppermute x8, starting transfers between devices, other(): return lax.ppermute(values, 'tp', [(0, 1), (1, 0)])  11.5 us
    unnamed x75, local copies, waits for them, and re-layouts  9.52 us
    ppermute x2, starting transfers between devices, rims(): before = lax.ppermute(tail, 'seq', [(i, i + 1) for i in range(count - 1)])  5.15 us
  transfers between devices with their start and end apart: 49, of which 21 were waited for; matrix products, arithmetic and copies ran while one was open for 2% of the time, Pallas kernels for 31%

profile of v5, /device:TPU:0, one launch (start us, length us, event | category | flops | bytes accessed | tf_op | source)
XLA Modules:
  0.0 181.7 jit_solution(7294881786511516230)
XLA Ops:
  3.3 3.0 %collective-permute-start = (bf16[784,256]{1,0:T(8,128)(2,1)S(1)}, bf16[784,256]{1,0:T(8,128)(2,1)S(1)}, u32[]{:S(2)}, u32[]{:S(2)}) collective-permute-start(bf16[784,256]{1,0:T(8,128)(2,1)S(1)} %pack_edges.1.xm), channel_id=1, source_target_pairs={{0,1},{1,0},{2,3},{3,2},{4,5},{5,4},{6,7},{7,6},{8,9},{9,8},{10,11... | collective-permute-start | bytes 1204232 | tf_op jit(solution)/shard_map/ppermute | solution.py:785
  11.4 5.0 %collective-permute-done.xt.gt = bf16[784,256]{1,0:T(8,128)(2,1)S(1)} collective-permute-done((bf16[784,256]{1,0:T(8,128)(2,1)S(1)}, bf16[784,256]{1,0:T(8,128)(2,1)S(1)}, u32[]{:S(2)}, u32[]{:S(2)}) %collective-permute-start) | collective-permute-done | bytes 401440 | tf_op jit(solution)/shard_map/ppermute | solution.py:785
  17.4 4.0 %glu_edges.1 = (bf16[512,1536]{1,0:T(8,128)(2,1)}, f32[512,768]{1,0:T(8,128)S(1)}, f32[512,128]{1,0:T(8,128)S(1)}, bf16[512,768]{1,0:T(8,128)(2,1)S(1)}, f32[512...) custom-call(s32[4]{0:T(128)S(1)} %pad_add_fusion.p, bf16[784,256]{1,0:T(8,128)(2,1)S(1)} %copy-done.19, ...), custom_call_target="tpu_custom_call" | custom-call | flops 1000 | bytes 1000 | tf_op jit(solution)/shard_map/glu_edges/pallas_call | solution.py:30
  21.4 2.6 %collective-permute-done.3.xt = bf16[768,256]{1,0:T(8,128)(2,1)S(1)} collective-permute-done((bf16[768,256]{1,0:T(8,128)(2,1)S(1)}, bf16[768,256]{1,0:T(8,128)(2,1)S(1)}, u32[]{:S(2)}, u32[]{:S(2)}) %collective-permute-start.3) | collective-permute-done | bytes 393248 | tf_op jit(solution)/shard_map/ppermute | solution.py:785
  24.0 4.0 %glu_middle.1 = (bf16[512,1536]{1,0:T(8,128)(2,1)}, f32[512,768]{1,0:T(8,128)S(1)}, f32[512,128]{1,0:T(8,128)S(1)}, bf16[512,768]{1,0:T(8,128)(2,1)S(1)}, f32[51...) custom-call(s32[4]{0:T(128)S(1)} %pad_add_fusion.p, ...), custom_call_target="tpu_custom_call", output_to_operand_aliasing={{0}: (7, {}), {1}: (8, {}), {2}: (9, {}), {3}: (10, {}), {4... | custom-call | flops 1000 | bytes 1000 | tf_op jit(solution)/shard_map/glu_middle/pallas_call | solution.py:30
  34.0 2.7 %collective-permute-done.4.a = bf16[16,768]{1,0:T(8,128)(2,1)S(1)} collective-permute-done((bf16[16,768]{1,0:T(8,128)(2,1)S(1)}, bf16[16,768]{1,0:T(8,128)(2,1)S(1)}, u32[]{:S(2)}, u32[]{:S(2)}) %collective-permute-start.4) | collective-permute-done | bytes 24608 | tf_op jit(solution)/shard_map/ppermute | solution.py:939
  36.7 5.8 %conv_forward.1 = (f32[512,768]{1,0:T(8,128)S(1)}, f32[8,512]{1,0:T(8,128)S(1)}) custom-call(s32[4]{0:T(128)S(1)} %pad_add_fusion.p, bf16[16,768]{1,0:T(8,128)(2,1)S(1)} %collective-permute-done.2.b, bf16[512,768]{1,0:T(8,128)(2,1)S(1)} %get-tuple-element.77.g, bf16[16,768]{1,0:T(8,128)(2,1)S(1)} %collective-permute-done.4.a, f32[32,768]{1,0:T(8,128)S(1)} %bitcast.123), custom_call_target="tpu_custom_call" | custom-call | flops 1000 | bytes 1000 | tf_op jit(solution)/shard_map/conv_forward/pallas_call | solution.py:30
  43.0 6.0 %collective-permute-done.5.st = f32[8,512]{1,0:T(8,128)S(1)} collective-permute-done((f32[8,512]{1,0:T(8,128)S(1)}, f32[8,512]{1,0:T(8,128)S(1)}, u32[]{:S(2)}, u32[]{:S(2)}) %collective-permute-start.5) | collective-permute-done | bytes 16416 | tf_op jit(solution)/shard_map/ppermute | solution.py:785
  49.1 2.7 %act_step.1 = (f32[512,768]{1,0:T(8,128)S(1)}, f32[512,768]{1,0:T(8,128)S(1)}, f32[8,512]{1,0:T(8,128)S(1)}, f32[1,768]{1,0:T(1,128)S(1)}) custom-call(s32[4]{0:T(128)S(1)} %pad_add_fusion.p, f32[512,768]{1,0:T(8,128)S(1)} %get-tuple-element.78.x, f32[8,512]{1,0:T(8,128)S(1)} %get-tuple-element.79.sm, f32[8,512]{1,0:T(8,128)S(1)} %collective-permute-done.5.st, ...), custom_call_target="tpu_custom_call" | custom-call | flops 1000 | bytes 1000 | tf_op jit(solution)/shard_map/act_step/pallas_call | solution.py:30
  55.6 3.2 %d_conv_step.1 = (bf16[512,768]{1,0:T(8,128)(2,1)S(1)}, bf16[512,768]{1,0:T(8,128)(2,1)}, bf16[16,768]{1,0:T(8,128)(2,1)S(1)}, bf16[16,768]{1,0:T(8,128)(2,1)S(1)}) custom-call(s32[4]{0:T(128)S(1)} %pad_add_fusion.p, f32[512,768]{1,0:T(8,128)S(1)} %get-tuple-element.81.d, f32[512,768]{1,0:T(8,128)S(1)} %get-tuple-element.82.h, ...), custom_call_target="tpu_custom_call" | custom-call | flops 1000 | bytes 1000 | tf_op jit(solution)/shard_map/d_conv_step/pallas_call | solution.py:30
  60.1 3.0 %collective-permute-start.9 = (bf16[16,768]{1,0:T(8,128)(2,1)S(1)}, bf16[16,768]{1,0:T(8,128)(2,1)S(1)}, u32[]{:S(2)}, u32[]{:S(2)}) collective-permute-start(bf16[16,768]{1,0:T(8,128)(2,1)S(1)} %get-tuple-element.85), channel_id=1, source_target_pairs={{0,2},{2,4},{4,6},{6,8},{8,10},{10,12},{12,14},{14,16},{16,18},{18... | collective-permute-start | bytes 73736 | tf_op jit(solution)/shard_map/ppermute | solution.py:938
  64.0 3.9 %d_glu_other.1 = (bf16[512,384]{1,0:T(8,128)(2,1)}, bf16[512,384]{1,0:T(8,128)(2,1)}) custom-call(s32[4]{0:T(128)S(1)} %pad_add_fusion.p, bf16[16,768]{1,0:T(8,128)(2,1)S(1)} %collective-permute-done.9.b, bf16[512,768]{1,0:T(8,128)(2,1)S(1)} %get-tuple-element.104.d, bf16[16,768]{1,0:T(8,128)(2,1)S(1)} %collective-permute-done.10.a, ...), custom_call_target="tpu_custom_call" | custom-call | flops 1000 | bytes 1000 | tf_op jit(solution)/shard_map/d_glu_other/pallas_call | solution.py:30
  74.5 3.3 %d_glu_own.1 = (bf16[512,384]{1,0:T(8,128)(2,1)S(1)}, bf16[512,384]{1,0:T(8,128)(2,1)S(1)}) custom-call(s32[4]{0:T(128)S(1)} %pad_add_fusion.p, bf16[16,768]{1,0:T(8,128)(2,1)S(1)} %copy-done.31, bf16[512,768]{1,0:T(8,128)(2,1)S(1)} %copy-done.14, bf16[16,768]{1,0:T(8,128)(2,1)S(1)} %copy-done.29, f32[32,768]{1,0:T(8,128)S(1)} %bitcast.125, ...), custom_call_target="tpu_custom_call" | custom-call | flops 1000 | bytes 1000 | tf_op jit(solution)/shard_map/d_glu_own/pallas_call | solution.py:30
  77.9 5.8 %pair_grads.1 = bf16[8,2,48,1536]{3,2,1,0:T(8,128)(2,1)S(1)} custom-call(s32[4]{0:T(128)S(1)} %pad_add_fusion.p, bf16[512,384]{1,0:T(8,128)(2,1)S(1)} %get-tuple-element.100.mv.vo, bf16[512,384]{1,0:T(8,128)(2,1)S(1)} %get-tuple-element.93.mg.go, bf16[512,384]{1,0:T(8,128)(2,1)} %collective-permute-done.11.tv, bf16[512,384]{1,0:T(8,128)(2,1)} %collective-permute-done.12.tg, ...), custom_call_target="tpu_custom_call" | custom-call | flops 1000 | bytes 1000 | tf_op jit(solution)/shard_map/pair_grads/pallas_call | solution.py:30
  84.6 3.6 %collective-permute-start.16 = (bf16[96,1536]{1,0:T(8,128)(2,1)}, bf16[96,1536]{1,0:T(8,128)(2,1)}, u32[]{:S(2)}, u32[]{:S(2)}) collective-permute-start(bf16[96,1536]{1,0:T(8,128)(2,1)} %get-tuple-element.135), channel_id=1, source_target_pairs={{0,8},{2,10},{8,16},{10,18},{16,24},{18,26},{24,28},{26,30},{28,20... | collective-permute-start | bytes 884744 | tf_op jit(solution)/shard_map/ppermute | solution.py:976
  99.3 4.4 %out_grads.1 = bf16[384,1536]{1,0:T(8,128)(2,1)S(1)} custom-call(s32[4]{0:T(128)S(1)} %pad_add_fusion.p, bf16[768,512]{1,0:T(8,128)(2,1)S(1)} %copy-done.10, bf16[384,512]{1,0:T(8,128)(2,1)S(1)} %copy-done.27, bf16[512,768]{1,0:T(8,128)(2,1)} %get-tuple-element.96.a, bf16[512,768]{1,0:T(8,128)(2,1)} %collective-permute-done.8.b, ...), custom_call_target="tpu_custom_call" | custom-call | flops 1000 | bytes 1000 | tf_op jit(solution)/shard_map/out_grads/pallas_call | solution.py:30
  108.1 5.6 %d_normed_terms.1 = (bf16[512,768]{1,0:T(8,128)(2,1)S(1)}, bf16[512,768]{1,0:T(8,128)(2,1)S(1)}) custom-call(s32[4]{0:T(128)S(1)} %pad_add_fusion.p, bf16[512,384]{1,0:T(8,128)(2,1)S(1)} %get-tuple-element.100.mv.vo, bf16[512,384]{1,0:T(8,128)(2,1)} %get-tuple-element.90.vt, bf16[512,384]{1,0:T(8,128)(2,1)S(1)} %copy-done.21, ...), custom_call_target="tpu_custom_call" | custom-call | flops 1000 | bytes 1000 | tf_op jit(solution)/shard_map/d_normed_terms/pallas_call | solution.py:30
  118.9 5.3 %taps_grad.1 = f32[32,768]{1,0:T(8,128)S(1)} custom-call(s32[4]{0:T(128)S(1)} %pad_add_fusion.p, bf16[16,768]{1,0:T(8,128)(2,1)S(1)} %copy-done.33, bf16[512,768]{1,0:T(8,128)(2,1)S(1)} %copy-done.17, bf16[16,768]{1,0:T(8,128)(2,1)S(1)} %copy-done.35, bf16[512,768]{1,0:T(8,128)(2,1)S(1)} %copy-done.15), custom_call_target="tpu_custom_call" | custom-call | flops 1000 | bytes 1000 | tf_op jit(solution)/shard_map/taps_grad/pallas_call | solution.py:30
  145.1 3.2 %input_step.1 = bf16[768,512]{1,0:T(8,128)(2,1)} custom-call(s32[4]{0:T(128)S(1)} %pad_add_fusion.p, bf16[512,768]{1,0:T(8,128)(2,1)S(1)} %get-tuple-element.109.tm, bf16[512,768]{1,0:T(8,128)(2,1)S(1)} %collective-permute-done.34.tr, f32[512,768]{1,0:T(8,128)S(1)} %copy-done.5, f32[1,768]{1,0:T(1,128)S(1)} %broadcast_in_dim.41.g.gm, ...), custom_call_target="tpu_custom_call" | custom-call | flops 1000 | bytes 1000 | tf_op jit(solution)/shard_map/input_step/pallas_call | solution.py:30
  152.8 4.5 %out_step.1 = bf16[768,512]{1,0:T(8,128)(2,1)} custom-call(s32[4]{0:T(128)S(1)} %pad_add_fusion.p, bf16[768,512]{1,0:T(8,128)(2,1)S(1)} %copy-done.8, bf16[768,1536]{1,0:T(8,128)(2,1)S(1)} %copy-done.12, bf16[512,768]{1,0:T(8,128)(2,1)} %get-tuple-element.96.a, bf16[512,768]{1,0:T(8,128)(2,1)} %collective-permute-done.8.b), custom_call_target="tpu_custom_call" | custom-call | flops 1000 | bytes 1000 | tf_op jit(solution)/shard_map/out_step/pallas_call | solution.py:30
  160.0 3.2 %collective-permute-done.39 = bf16[72,1536]{1,0:T(8,128)(2,1)S(1)} collective-permute-done((bf16[72,1536]{1,0:T(8,128)(2,1)S(1)}, bf16[72,1536]{1,0:T(8,128)(2,1)S(1)}, u32[]{:S(2)}, u32[]{:S(2)}) %collective-permute-start.39) | collective-permute-done | bytes 221216 | tf_op jit(solution)/shard_map/ppermute | solution.py:976
  165.3 3.9 %collective-permute-done.43 = bf16[72,1536]{1,0:T(8,128)(2,1)S(1)} collective-permute-done((bf16[72,1536]{1,0:T(8,128)(2,1)S(1)}, bf16[72,1536]{1,0:T(8,128)(2,1)S(1)}, u32[]{:S(2)}, u32[]{:S(2)}) %collective-permute-start.43) | collective-permute-done | bytes 221216 | tf_op jit(solution)/shard_map/ppermute | solution.py:976
  169.9 2.9 %collective-permute-done.44 = bf16[72,1536]{1,0:T(8,128)(2,1)S(1)} collective-permute-done((bf16[72,1536]{1,0:T(8,128)(2,1)S(1)}, bf16[72,1536]{1,0:T(8,128)(2,1)S(1)}, u32[]{:S(2)}, u32[]{:S(2)}) %collective-permute-start.44) | collective-permute-done | bytes 221216 | tf_op jit(solution)/shard_map/ppermute | solution.py:976
  178.0 3.5 %join_halves.1 = (bf16[2,8,48,1536]{3,2,1,0:T(8,128)(2,1)}, bf16[2,8,48,1536]{3,2,1,0:T(8,128)(2,1)}, bf16[2,8,48,1536]{3,2,1,0:T(8,128)(2,1)}) custom-call(s32[4]{0:T(128)S(1)} %pad_add_fusion.p, bf16[8,2,48,1536]{3,2,1,0:T(8,128)(2,1)S(1)} %bitcast.116, bf16[8,2,48,1536]{3,2,1,0:T(8,128)(2,1)S(1)} %collective-permute-done.47.at, ...), custom_call_target="tpu_custom_call" | custom-call | flops 1000 | bytes 1000 | tf_op jit(solution)/shard_map/join_halves/pallas_call | solution.py:30
  (207 shorter events, 85.0 us)
Async XLA Ops:
  3.3 13.1 %collective-permute-start = (bf16[784,256]{1,0:T(8,128)(2,1)S(1)}, bf16[784,256]{1,0:T(8,128)(2,1)S(1)}, u32[]{:S(2)}, u32[]{:S(2)}) collective-permute-start(bf16[784,256]{1,0:T(8,128)(2,1)S(1)} %pack_edges.1.xm), channel_id=1, source_target_pairs={{0,1},{1,0},{2,3},{3,2},{4,5},{5,4},{6,7},{7,6},{8,9},{9,8},{10,11... | collective-permute-start | bytes 1204232 | tf_op jit(solution)/shard_map/ppermute | solution.py:785
  6.5 17.5 %collective-permute-start.3 = (bf16[768,256]{1,0:T(8,128)(2,1)S(1)}, bf16[768,256]{1,0:T(8,128)(2,1)S(1)}, u32[]{:S(2)}, u32[]{:S(2)}) collective-permute-start(bf16[768,256]{1,0:T(8,128)(2,1)S(1)} %slice.77.xm), channel_id=1, source_target_pairs={{0,1},{1,0},{2,3},{3,2},{4,5},{5,4},{6,7},{7,6},{8,9},{9,8},{10,11... | collective-permute-start | bytes 1179656 | tf_op jit(solution)/shard_map/ppermute | solution.py:785
  28.8 49.1 %collective-permute-start.13 = (bf16[512,1536]{1,0:T(8,128)(2,1)}, bf16[512,1536]{1,0:T(8,128)(2,1)}, u32[]{:S(2)}, u32[]{:S(2)}) collective-permute-start(bf16[512,1536]{1,0:T(8,128)(2,1)} %get-tuple-element.95.n), channel_id=1, source_target_pairs={{0,2},{2,0},{4,6},{6,4},{8,10},{10,8},{12,14},{14,12},{16,18},{18,... | collective-permute-start | bytes 4718600 | tf_op jit(solution)/shard_map/ppermute | solution.py:933
  28.8 20.3 %collective-permute-start.6 = (bf16[512,768]{1,0:T(8,128)(2,1)S(1)}, bf16[512,768]{1,0:T(8,128)(2,1)S(1)}, u32[]{:S(2)}, u32[]{:S(2)}) collective-permute-start(bf16[512,768]{1,0:T(8,128)(2,1)S(1)} %get-tuple-element.68), channel_id=1, source_target_pairs={{0,1},{1,0},{2,3},{3,2},{4,5},{5,4},{6,7},{7,6},{8,9},{9,8},{10,11... | collective-permute-start | bytes 2359304 | tf_op jit(solution)/shard_map/ppermute | solution.py:785
  67.9 9.9 %collective-permute-start.11 = (bf16[512,384]{1,0:T(8,128)(2,1)}, bf16[512,384]{1,0:T(8,128)(2,1)}, u32[]{:S(2)}, u32[]{:S(2)}) collective-permute-start(bf16[512,384]{1,0:T(8,128)(2,1)} %get-tuple-element.90.vt), channel_id=1, source_target_pairs={{0,2},{2,0},{4,6},{6,4},{8,10},{10,8},{12,14},{14,12},{16,18},{18,... | collective-permute-start | bytes 1179656 | tf_op jit(solution)/shard_map/ppermute | solution.py:933
  69.5 20.2 %collective-permute-start.8 = (bf16[512,768]{1,0:T(8,128)(2,1)}, bf16[512,768]{1,0:T(8,128)(2,1)}, u32[]{:S(2)}, u32[]{:S(2)}) collective-permute-start(bf16[512,768]{1,0:T(8,128)(2,1)} %get-tuple-element.96.a), channel_id=1, source_target_pairs={{0,1},{1,0},{2,3},{3,2},{4,5},{5,4},{6,7},{7,6},{8,9},{9,8},{10,11... | collective-permute-start | bytes 2359304 | tf_op jit(solution)/shard_map/ppermute | solution.py:785
  84.6 10.1 %collective-permute-start.16 = (bf16[96,1536]{1,0:T(8,128)(2,1)}, bf16[96,1536]{1,0:T(8,128)(2,1)}, u32[]{:S(2)}, u32[]{:S(2)}) collective-permute-start(bf16[96,1536]{1,0:T(8,128)(2,1)} %get-tuple-element.135), channel_id=1, source_target_pairs={{0,8},{2,10},{8,16},{10,18},{16,24},{18,26},{24,28},{26,30},{28,20... | collective-permute-start | bytes 884744 | tf_op jit(solution)/shard_map/ppermute | solution.py:976
  90.3 13.5 %collective-permute-start.17 = (bf16[96,1536]{1,0:T(8,128)(2,1)}, bf16[96,1536]{1,0:T(8,128)(2,1)S(1)}, u32[]{:S(2)}, u32[]{:S(2)}) collective-permute-start(bf16[96,1536]{1,0:T(8,128)(2,1)} %get-tuple-element.134), channel_id=1, source_target_pairs={{8,0},{10,2},{16,8},{18,10},{24,16},{26,18},{28,24},{30,26},{20,28... | collective-permute-start | bytes 884744 | tf_op jit(solution)/shard_map/ppermute | solution.py:976
  95.7 10.1 %collective-permute-start.18 = (bf16[96,1536]{1,0:T(8,128)(2,1)S(1)}, bf16[96,1536]{1,0:T(8,128)(2,1)S(1)}, u32[]{:S(2)}, u32[]{:S(2)}) collective-permute-start(bf16[96,1536]{1,0:T(8,128)(2,1)S(1)} %fusion.6), channel_id=1, source_target_pairs={{0,8},{2,10},{8,16},{10,18},{16,24},{18,26},{24,28},{26,30},{28,20... | collective-permute-start | bytes 884744 | tf_op jit(solution)/shard_map/ppermute | solution.py:976
  103.8 10.7 %collective-permute-start.20 = (bf16[48,1536]{1,0:T(8,128)(2,1)S(1)}, bf16[48,1536]{1,0:T(8,128)(2,1)S(1)}, u32[]{:S(2)}, u32[]{:S(2)}) collective-permute-start(bf16[48,1536]{1,0:T(8,128)(2,1)S(1)} %get-tuple-element.98), channel_id=1, source_target_pairs={{8,0},{10,2},{16,8},{18,10},{24,16},{26,18},{28,24},{30,26},{20,28... | collective-permute-start | bytes 442376 | tf_op jit(solution)/shard_map/ppermute | solution.py:976
  103.8 10.6 %collective-permute-start.21 = (bf16[48,1536]{1,0:T(8,128)(2,1)S(1)}, bf16[48,1536]{1,0:T(8,128)(2,1)S(1)}, u32[]{:S(2)}, u32[]{:S(2)}) collective-permute-start(bf16[48,1536]{1,0:T(8,128)(2,1)S(1)} %get-tuple-element.99), channel_id=1, source_target_pairs={{0,8},{2,10},{8,16},{10,18},{16,24},{18,26},{24,28},{26,30},{28,20... | collective-permute-start | bytes 442376 | tf_op jit(solution)/shard_map/ppermute | solution.py:976
  106.1 10.5 %collective-permute-start.22 = (bf16[96,1536]{1,0:T(8,128)(2,1)S(1)}, bf16[96,1536]{1,0:T(8,128)(2,1)S(1)}, u32[]{:S(2)}, u32[]{:S(2)}) collective-permute-start(bf16[96,1536]{1,0:T(8,128)(2,1)S(1)} %get-tuple-element.132), channel_id=1, source_target_pairs={{0,8},{2,10},{8,16},{10,18},{16,24},{18,26},{24,28},{26,30},{28,20... | collective-permute-start | bytes 884744 | tf_op jit(solution)/shard_map/ppermute | solution.py:976
  113.8 25.7 %collective-permute-start.34 = (bf16[512,768]{1,0:T(8,128)(2,1)S(1)}, bf16[512,768]{1,0:T(8,128)(2,1)S(1)}, u32[]{:S(2)}, u32[]{:S(2)}) collective-permute-start(bf16[512,768]{1,0:T(8,128)(2,1)S(1)} %get-tuple-element.101), channel_id=1, source_target_pairs={{0,1},{1,0},{2,3},{3,2},{4,5},{5,4},{6,7},{7,6},{8,9},{9,8},{10,11... | collective-permute-start | bytes 2359304 | tf_op jit(solution)/shard_map/ppermute | solution.py:785
  114.6 9.6 %collective-permute-start.29 = (bf16[48,1536]{1,0:T(8,128)(2,1)S(1)}, bf16[48,1536]{1,0:T(8,128)(2,1)S(1)}, u32[]{:S(2)}, u32[]{:S(2)}) collective-permute-start(bf16[48,1536]{1,0:T(8,128)(2,1)S(1)} %get-tuple-element.102), channel_id=1, source_target_pairs={{8,0},{10,2},{16,8},{18,10},{24,16},{26,18},{28,24},{30,26},{20,28... | collective-permute-start | bytes 442376 | tf_op jit(solution)/shard_map/ppermute | solution.py:976
  115.0 9.2 %collective-permute-start.30 = (bf16[48,1536]{1,0:T(8,128)(2,1)S(1)}, bf16[48,1536]{1,0:T(8,128)(2,1)S(1)}, u32[]{:S(2)}, u32[]{:S(2)}) collective-permute-start(bf16[48,1536]{1,0:T(8,128)(2,1)S(1)} %get-tuple-element.103), channel_id=1, source_target_pairs={{0,8},{2,10},{8,16},{10,18},{16,24},{18,26},{24,28},{26,30},{28,20... | collective-permute-start | bytes 442376 | tf_op jit(solution)/shard_map/ppermute | solution.py:976
  125.5 11.9 %collective-permute-start.25 = (bf16[96,1536]{1,0:T(8,128)(2,1)S(1)}, bf16[96,1536]{1,0:T(8,128)(2,1)S(1)}, u32[]{:S(2)}, u32[]{:S(2)}) collective-permute-start(bf16[96,1536]{1,0:T(8,128)(2,1)S(1)} %fusion.2), channel_id=1, source_target_pairs={{0,8},{2,10},{8,16},{10,18},{16,24},{18,26},{24,28},{26,30},{28,20... | collective-permute-start | bytes 884744 | tf_op jit(solution)/shard_map/ppermute | solution.py:976
  127.2 11.9 %collective-permute-start.27 = (bf16[96,1536]{1,0:T(8,128)(2,1)S(1)}, bf16[96,1536]{1,0:T(8,128)(2,1)S(1)}, u32[]{:S(2)}, u32[]{:S(2)}) collective-permute-start(bf16[96,1536]{1,0:T(8,128)(2,1)S(1)} %fusion.2), channel_id=1, source_target_pairs={{8,0},{10,2},{16,8},{18,10},{24,16},{26,18},{28,24},{30,26},{20,28... | collective-permute-start | bytes 884744 | tf_op jit(solution)/shard_map/ppermute | solution.py:976
  137.4 10.8 %collective-permute-start.26 = (bf16[96,1536]{1,0:T(8,128)(2,1)S(1)}, bf16[96,1536]{1,0:T(8,128)(2,1)S(1)}, u32[]{:S(2)}, u32[]{:S(2)}) collective-permute-start(bf16[96,1536]{1,0:T(8,128)(2,1)S(1)} %collective-permute-done.25), channel_id=1, source_target_pairs={{0,8},{2,10},{8,16},{10,18},{16,24},{18,26},{24,28},{26,30},{28,20... | collective-permute-start | bytes 884744 | tf_op jit(solution)/shard_map/ppermute | solution.py:976
  139.1 10.9 %collective-permute-start.28 = (bf16[96,1536]{1,0:T(8,128)(2,1)S(1)}, bf16[96,1536]{1,0:T(8,128)(2,1)S(1)}, u32[]{:S(2)}, u32[]{:S(2)}) collective-permute-start(bf16[96,1536]{1,0:T(8,128)(2,1)S(1)} %collective-permute-done.27), channel_id=1, source_target_pairs={{8,0},{10,2},{16,8},{18,10},{24,16},{26,18},{28,24},{30,26},{20,28... | collective-permute-start | bytes 884744 | tf_op jit(solution)/shard_map/ppermute | solution.py:976
  148.3 9.9 %collective-permute-start.41 = (bf16[96,1536]{1,0:T(8,128)(2,1)S(1)}, bf16[96,1536]{1,0:T(8,128)(2,1)S(1)}, u32[]{:S(2)}, u32[]{:S(2)}) collective-permute-start(bf16[96,1536]{1,0:T(8,128)(2,1)S(1)} %collective-permute-done.26), channel_id=1, source_target_pairs={{0,8},{2,10},{8,16},{10,18},{16,24},{18,26},{24,28},{26,30},{28,20... | collective-permute-start | bytes 884744 | tf_op jit(solution)/shard_map/ppermute | solution.py:976
  150.0 9.9 %collective-permute-start.42 = (bf16[96,1536]{1,0:T(8,128)(2,1)S(1)}, bf16[96,1536]{1,0:T(8,128)(2,1)S(1)}, u32[]{:S(2)}, u32[]{:S(2)}) collective-permute-start(bf16[96,1536]{1,0:T(8,128)(2,1)S(1)} %collective-permute-done.28), channel_id=1, source_target_pairs={{8,0},{10,2},{16,8},{18,10},{24,16},{26,18},{28,24},{30,26},{20,28... | collective-permute-start | bytes 884744 | tf_op jit(solution)/shard_map/ppermute | solution.py:976
  150.7 12.4 %collective-permute-start.39 = (bf16[72,1536]{1,0:T(8,128)(2,1)S(1)}, bf16[72,1536]{1,0:T(8,128)(2,1)S(1)}, u32[]{:S(2)}, u32[]{:S(2)}) collective-permute-start(bf16[72,1536]{1,0:T(8,128)(2,1)S(1)} %collective-permute-done.36), channel_id=1, source_target_pairs={{8,0},{10,2},{16,8},{18,10},{24,16},{26,18},{28,24},{30,26},{20,28... | collective-permute-start | bytes 663560 | tf_op jit(solution)/shard_map/ppermute | solution.py:976
  152.6 10.6 %collective-permute-start.40 = (bf16[72,1536]{1,0:T(8,128)(2,1)S(1)}, bf16[72,1536]{1,0:T(8,128)(2,1)S(1)}, u32[]{:S(2)}, u32[]{:S(2)}) collective-permute-start(bf16[72,1536]{1,0:T(8,128)(2,1)S(1)} %collective-permute-done.37), channel_id=1, source_target_pairs={{0,8},{2,10},{8,16},{10,18},{16,24},{18,26},{24,28},{26,30},{28,20... | collective-permute-start | bytes 663560 | tf_op jit(solution)/shard_map/ppermute | solution.py:976
  158.2 11.6 %collective-permute-start.46 = (bf16[96,1536]{1,0:T(8,128)(2,1)S(1)}, bf16[96,1536]{1,0:T(8,128)(2,1)S(1)}, u32[]{:S(2)}, u32[]{:S(2)}) collective-permute-start(bf16[96,1536]{1,0:T(8,128)(2,1)S(1)} %collective-permute-done.41), channel_id=1, source_target_pairs={{0,8},{2,10},{8,16},{10,18},{16,24},{18,26},{24,28},{26,30},{28,20... | collective-permute-start | bytes 884744 | tf_op jit(solution)/shard_map/ppermute | solution.py:976
  (62 other events, 431.1 us)

commit v6 on v5

--- a/solution.py
+++ b/solution.py
@@ -106,7 +106,7 @@
         out[:chans, :quarter] = first[...]
         out[:chans, quarter:] = last[...]
         out[chans:, :] = jnp.zeros_like(out[chans:, :])
-        rest = g[...]
+        rest = g[...].reshape(1, chans)
         rows = []
         for _ in range(3):
             term = rest.astype(BF16).astype(F32)
@@ -123,7 +123,7 @@
         [
             pl.BlockSpec((chans, quarter), lambda i, p: (0, 0)),
             pl.BlockSpec((chans, quarter), lambda i, p: (0, 3)),
-            whole((1, chans)),
+            pl.BlockSpec((chans,), lambda i, p: (0,)),
         ],
         [(shape((chans + 16, 2 * quarter), BF16), whole((chans + 16, 2 * quarter)))],
         [frames_in, frames_in, gain],
@@ -242,7 +242,7 @@
     return turned[:, 0:1], turned[:, 1:2]
 
 
-STEP = 64
+STEP = 128
 
 
 def conv_forward(places, before, glu, after, taps):
@@ -463,7 +463,7 @@
 def pair_grads(places, chips, mine, theirs, normed, normed_theirs, scale):
     frames, half = mine[0].shape
     width = normed.shape[1]
-    step = 512
+    step = width // 2
 
     def body(p, mv, mg, tv, tg, n, nt, out, turned):
         @pl.when(pl.program_id(0) == 0)
@@ -1024,7 +1024,7 @@
     places = places.astype(jnp.int32)
 
     gain = norm_gain[None]
-    edges = pack_edges(places, frames_in, gain)
+    edges = pack_edges(places, frames_in, norm_gain)
     edges_theirs = other(edges)
     middle = frames_in[:, quarter : 3 * quarter]
     middle_theirs = other(middle)

time: 182 us -> 181 us (level)
    unnamed x75 -> x79, local copies, waits for them, and re-layouts: 9.52 us -> 10.7 us
  transfers between devices with their start and end apart: 49 -> 49, of which waited for: 21 -> 22; matrix products, arithmetic and copies ran while one was open for 2% -> 2% of each run, Pallas kernels for 31% -> 30%
where the time goes in v6:
time: 181 us
  Pallas kernels  62.6 us (35%)
  starting transfers between devices  55.6 us (31%)
  waiting for transfers between devices  45.7 us (25%)
  local copies, waits for them, and re-layouts  12.6 us (7%)
  other arithmetic  2.59 us (1%)
    pallas_call x17, Pallas kernels, call(): pl.pallas_call(body, out_shape=[s for s, _ in outs], grid_spec=pltpu.Pref...  62.6 us
    ppermute x28, starting transfers between devices, send(): lax.ppermute(x, 'seq', way)  34.5 us
    ppermute x28, waiting for transfers between devices, send(): lax.ppermute(x, 'seq', way)  23.3 us
    ppermute x8, waiting for transfers between devices, other(): return lax.ppermute(values, 'tp', [(0, 1), (1, 0)])  17.2 us
    ppermute x8, starting transfers between devices, other(): return lax.ppermute(values, 'tp', [(0, 1), (1, 0)])  11.1 us
    unnamed x79, local copies, waits for them, and re-layouts  10.7 us
    ppermute x2, starting transfers between devices, rims(): before = lax.ppermute(tail, 'seq', [(i, i + 1) for i in range(count - 1)])  5.09 us
  transfers between devices with their start and end apart: 49, of which 22 were waited for; matrix products, arithmetic and copies ran while one was open for 2% of the time, Pallas kernels for 30%

profile of v6, /device:TPU:0, one launch (start us, length us, event | category | flops | bytes accessed | tf_op | source)
XLA Modules:
  0.0 180.7 jit_solution(3408474558277277619)
XLA Ops:
  3.3 3.0 %collective-permute-start = (bf16[784,256]{1,0:T(8,128)(2,1)S(1)}, bf16[784,256]{1,0:T(8,128)(2,1)S(1)}, u32[]{:S(2)}, u32[]{:S(2)}) collective-permute-start(bf16[784,256]{1,0:T(8,128)(2,1)S(1)} %pack_edges.1.xm), channel_id=1, source_target_pairs={{0,1},{1,0},{2,3},{3,2},{4,5},{5,4},{6,7},{7,6},{8,9},{9,8},{10,11... | collective-permute-start | bytes 1204232 | tf_op jit(solution)/shard_map/ppermute | solution.py:785
  11.5 5.0 %collective-permute-done.xt.gt = bf16[784,256]{1,0:T(8,128)(2,1)S(1)} collective-permute-done((bf16[784,256]{1,0:T(8,128)(2,1)S(1)}, bf16[784,256]{1,0:T(8,128)(2,1)S(1)}, u32[]{:S(2)}, u32[]{:S(2)}) %collective-permute-start) | collective-permute-done | bytes 401440 | tf_op jit(solution)/shard_map/ppermute | solution.py:785
  17.4 4.0 %glu_edges.1 = (bf16[512,1536]{1,0:T(8,128)(2,1)}, f32[512,768]{1,0:T(8,128)S(1)}, f32[512,128]{1,0:T(8,128)S(1)}, bf16[512,768]{1,0:T(8,128)(2,1)S(1)}, f32[512...) custom-call(s32[4]{0:T(128)S(1)} %pad_add_fusion.p, bf16[784,256]{1,0:T(8,128)(2,1)S(1)} %copy-done.19, ...), custom_call_target="tpu_custom_call" | custom-call | flops 1000 | bytes 1000 | tf_op jit(solution)/shard_map/glu_edges/pallas_call | solution.py:30
  21.4 2.6 %collective-permute-done.3.xt = bf16[768,256]{1,0:T(8,128)(2,1)S(1)} collective-permute-done((bf16[768,256]{1,0:T(8,128)(2,1)S(1)}, bf16[768,256]{1,0:T(8,128)(2,1)S(1)}, u32[]{:S(2)}, u32[]{:S(2)}) %collective-permute-start.3) | collective-permute-done | bytes 393248 | tf_op jit(solution)/shard_map/ppermute | solution.py:785
  24.0 4.0 %glu_middle.1 = (bf16[512,1536]{1,0:T(8,128)(2,1)}, f32[512,768]{1,0:T(8,128)S(1)}, f32[512,128]{1,0:T(8,128)S(1)}, bf16[512,768]{1,0:T(8,128)(2,1)S(1)}, f32[51...) custom-call(s32[4]{0:T(128)S(1)} %pad_add_fusion.p, ...), custom_call_target="tpu_custom_call", output_to_operand_aliasing={{0}: (7, {}), {1}: (8, {}), {2}: (9, {}), {3}: (10, {}), {4... | custom-call | flops 1000 | bytes 1000 | tf_op jit(solution)/shard_map/glu_middle/pallas_call | solution.py:30
  33.4 2.8 %collective-permute-done.4.a = bf16[16,768]{1,0:T(8,128)(2,1)S(1)} collective-permute-done((bf16[16,768]{1,0:T(8,128)(2,1)S(1)}, bf16[16,768]{1,0:T(8,128)(2,1)S(1)}, u32[]{:S(2)}, u32[]{:S(2)}) %collective-permute-start.4) | collective-permute-done | bytes 24608 | tf_op jit(solution)/shard_map/ppermute | solution.py:939
  36.1 5.2 %conv_forward.1 = (f32[512,768]{1,0:T(8,128)S(1)}, f32[8,512]{1,0:T(8,128)S(1)}) custom-call(s32[4]{0:T(128)S(1)} %pad_add_fusion.p, bf16[16,768]{1,0:T(8,128)(2,1)S(1)} %collective-permute-done.2.b, bf16[512,768]{1,0:T(8,128)(2,1)S(1)} %get-tuple-element.77.g, bf16[16,768]{1,0:T(8,128)(2,1)S(1)} %collective-permute-done.4.a, f32[32,768]{1,0:T(8,128)S(1)} %bitcast.123), custom_call_target="tpu_custom_call" | custom-call | flops 1000 | bytes 1000 | tf_op jit(solution)/shard_map/conv_forward/pallas_call | solution.py:30
  43.0 5.4 %collective-permute-done.5.st = f32[8,512]{1,0:T(8,128)S(1)} collective-permute-done((f32[8,512]{1,0:T(8,128)S(1)}, f32[8,512]{1,0:T(8,128)S(1)}, u32[]{:S(2)}, u32[]{:S(2)}) %collective-permute-start.5) | collective-permute-done | bytes 16416 | tf_op jit(solution)/shard_map/ppermute | solution.py:785
  48.5 2.7 %act_step.1 = (f32[512,768]{1,0:T(8,128)S(1)}, f32[512,768]{1,0:T(8,128)S(1)}, f32[8,512]{1,0:T(8,128)S(1)}, f32[1,768]{1,0:T(1,128)S(1)}) custom-call(s32[4]{0:T(128)S(1)} %pad_add_fusion.p, f32[512,768]{1,0:T(8,128)S(1)} %get-tuple-element.78.x, f32[8,512]{1,0:T(8,128)S(1)} %get-tuple-element.79.sm, f32[8,512]{1,0:T(8,128)S(1)} %collective-permute-done.5.st, ...), custom_call_target="tpu_custom_call" | custom-call | flops 1000 | bytes 1000 | tf_op jit(solution)/shard_map/act_step/pallas_call | solution.py:30
  55.0 3.2 %d_conv_step.1 = (bf16[512,768]{1,0:T(8,128)(2,1)S(1)}, bf16[512,768]{1,0:T(8,128)(2,1)}, bf16[16,768]{1,0:T(8,128)(2,1)S(1)}, bf16[16,768]{1,0:T(8,128)(2,1)S(1)}) custom-call(s32[4]{0:T(128)S(1)} %pad_add_fusion.p, f32[512,768]{1,0:T(8,128)S(1)} %get-tuple-element.81.d, f32[512,768]{1,0:T(8,128)S(1)} %get-tuple-element.82.h, ...), custom_call_target="tpu_custom_call" | custom-call | flops 1000 | bytes 1000 | tf_op jit(solution)/shard_map/d_conv_step/pallas_call | solution.py:30
  59.5 3.0 %collective-permute-start.9 = (bf16[16,768]{1,0:T(8,128)(2,1)S(1)}, bf16[16,768]{1,0:T(8,128)(2,1)S(1)}, u32[]{:S(2)}, u32[]{:S(2)}) collective-permute-start(bf16[16,768]{1,0:T(8,128)(2,1)S(1)} %get-tuple-element.85), channel_id=1, source_target_pairs={{0,2},{2,4},{4,6},{6,8},{8,10},{10,12},{12,14},{14,16},{16,18},{18... | collective-permute-start | bytes 73736 | tf_op jit(solution)/shard_map/ppermute | solution.py:938
  63.4 3.7 %d_glu_other.1 = (bf16[512,384]{1,0:T(8,128)(2,1)}, bf16[512,384]{1,0:T(8,128)(2,1)}) custom-call(s32[4]{0:T(128)S(1)} %pad_add_fusion.p, bf16[16,768]{1,0:T(8,128)(2,1)S(1)} %collective-permute-done.9.b, bf16[512,768]{1,0:T(8,128)(2,1)S(1)} %get-tuple-element.104.d, bf16[16,768]{1,0:T(8,128)(2,1)S(1)} %collective-permute-done.10.a, ...), custom_call_target="tpu_custom_call" | custom-call | flops 1000 | bytes 1000 | tf_op jit(solution)/shard_map/d_glu_other/pallas_call | solution.py:30
  73.7 3.1 %d_glu_own.1 = (bf16[512,384]{1,0:T(8,128)(2,1)S(1)}, bf16[512,384]{1,0:T(8,128)(2,1)S(1)}) custom-call(s32[4]{0:T(128)S(1)} %pad_add_fusion.p, bf16[16,768]{1,0:T(8,128)(2,1)S(1)} %copy-done.31, bf16[512,768]{1,0:T(8,128)(2,1)S(1)} %copy-done.14, bf16[16,768]{1,0:T(8,128)(2,1)S(1)} %copy-done.29, f32[32,768]{1,0:T(8,128)S(1)} %bitcast.125, ...), custom_call_target="tpu_custom_call" | custom-call | flops 1000 | bytes 1000 | tf_op jit(solution)/shard_map/d_glu_own/pallas_call | solution.py:30
  76.9 5.6 %pair_grads.1 = bf16[8,2,48,1536]{3,2,1,0:T(8,128)(2,1)S(1)} custom-call(s32[4]{0:T(128)S(1)} %pad_add_fusion.p, bf16[512,384]{1,0:T(8,128)(2,1)S(1)} %get-tuple-element.100.mv.vo, bf16[512,384]{1,0:T(8,128)(2,1)S(1)} %get-tuple-element.93.mg.go, bf16[512,384]{1,0:T(8,128)(2,1)} %collective-permute-done.11.tv, bf16[512,384]{1,0:T(8,128)(2,1)} %collective-permute-done.12.tg, ...), custom_call_target="tpu_custom_call" | custom-call | flops 1000 | bytes 1000 | tf_op jit(solution)/shard_map/pair_grads/pallas_call | solution.py:30
  83.4 3.6 %collective-permute-start.16 = (bf16[96,1536]{1,0:T(8,128)(2,1)}, bf16[96,1536]{1,0:T(8,128)(2,1)}, u32[]{:S(2)}, u32[]{:S(2)}) collective-permute-start(bf16[96,1536]{1,0:T(8,128)(2,1)} %get-tuple-element.135), channel_id=1, source_target_pairs={{0,8},{2,10},{8,16},{10,18},{16,24},{18,26},{24,28},{26,30},{28,20... | collective-permute-start | bytes 884744 | tf_op jit(solution)/shard_map/ppermute | solution.py:976
  98.1 4.4 %out_grads.1 = bf16[384,1536]{1,0:T(8,128)(2,1)S(1)} custom-call(s32[4]{0:T(128)S(1)} %pad_add_fusion.p, bf16[768,512]{1,0:T(8,128)(2,1)S(1)} %copy-done.10, bf16[384,512]{1,0:T(8,128)(2,1)S(1)} %copy-done.27, bf16[512,768]{1,0:T(8,128)(2,1)} %get-tuple-element.96.a, bf16[512,768]{1,0:T(8,128)(2,1)} %collective-permute-done.8.b, ...), custom_call_target="tpu_custom_call" | custom-call | flops 1000 | bytes 1000 | tf_op jit(solution)/shard_map/out_grads/pallas_call | solution.py:30
  106.9 5.6 %d_normed_terms.1 = (bf16[512,768]{1,0:T(8,128)(2,1)S(1)}, bf16[512,768]{1,0:T(8,128)(2,1)S(1)}) custom-call(s32[4]{0:T(128)S(1)} %pad_add_fusion.p, bf16[512,384]{1,0:T(8,128)(2,1)S(1)} %get-tuple-element.100.mv.vo, bf16[512,384]{1,0:T(8,128)(2,1)} %get-tuple-element.90.vt, bf16[512,384]{1,0:T(8,128)(2,1)S(1)} %copy-done.21, ...), custom_call_target="tpu_custom_call" | custom-call | flops 1000 | bytes 1000 | tf_op jit(solution)/shard_map/d_normed_terms/pallas_call | solution.py:30
  117.7 5.3 %taps_grad.1 = f32[32,768]{1,0:T(8,128)S(1)} custom-call(s32[4]{0:T(128)S(1)} %pad_add_fusion.p, bf16[16,768]{1,0:T(8,128)(2,1)S(1)} %copy-done.33, bf16[512,768]{1,0:T(8,128)(2,1)S(1)} %copy-done.17, bf16[16,768]{1,0:T(8,128)(2,1)S(1)} %copy-done.35, bf16[512,768]{1,0:T(8,128)(2,1)S(1)} %copy-done.15), custom_call_target="tpu_custom_call" | custom-call | flops 1000 | bytes 1000 | tf_op jit(solution)/shard_map/taps_grad/pallas_call | solution.py:30
  133.6 2.6 %collective-permute-done.32 = bf16[48,1536]{1,0:T(8,128)(2,1)S(1)} collective-permute-done((bf16[48,1536]{1,0:T(8,128)(2,1)S(1)}, bf16[48,1536]{1,0:T(8,128)(2,1)S(1)}, u32[]{:S(2)}, u32[]{:S(2)}) %collective-permute-start.32) | collective-permute-done | bytes 147488 | tf_op jit(solution)/shard_map/ppermute | solution.py:976
  143.8 3.2 %input_step.1 = bf16[768,512]{1,0:T(8,128)(2,1)} custom-call(s32[4]{0:T(128)S(1)} %pad_add_fusion.p, bf16[512,768]{1,0:T(8,128)(2,1)S(1)} %get-tuple-element.109.tm, bf16[512,768]{1,0:T(8,128)(2,1)S(1)} %collective-permute-done.34.tr, f32[512,768]{1,0:T(8,128)S(1)} %copy-done.5, f32[1,768]{1,0:T(1,128)S(1)} %broadcast_in_dim.41.gm.g, ...), custom_call_target="tpu_custom_call" | custom-call | flops 1000 | bytes 1000 | tf_op jit(solution)/shard_map/input_step/pallas_call | solution.py:30
  152.3 4.5 %out_step.1 = bf16[768,512]{1,0:T(8,128)(2,1)} custom-call(s32[4]{0:T(128)S(1)} %pad_add_fusion.p, bf16[768,512]{1,0:T(8,128)(2,1)S(1)} %copy-done.8, bf16[768,1536]{1,0:T(8,128)(2,1)S(1)} %copy-done.12, bf16[512,768]{1,0:T(8,128)(2,1)} %get-tuple-element.96.a, bf16[512,768]{1,0:T(8,128)(2,1)} %collective-permute-done.8.b), custom_call_target="tpu_custom_call" | custom-call | flops 1000 | bytes 1000 | tf_op jit(solution)/shard_map/out_step/pallas_call | solution.py:30
  158.8 3.3 %collective-permute-done.39 = bf16[72,1536]{1,0:T(8,128)(2,1)S(1)} collective-permute-done((bf16[72,1536]{1,0:T(8,128)(2,1)S(1)}, bf16[72,1536]{1,0:T(8,128)(2,1)S(1)}, u32[]{:S(2)}, u32[]{:S(2)}) %collective-permute-start.39) | collective-permute-done | bytes 221216 | tf_op jit(solution)/shard_map/ppermute | solution.py:976
  164.1 4.0 %collective-permute-done.43 = bf16[72,1536]{1,0:T(8,128)(2,1)S(1)} collective-permute-done((bf16[72,1536]{1,0:T(8,128)(2,1)S(1)}, bf16[72,1536]{1,0:T(8,128)(2,1)S(1)}, u32[]{:S(2)}, u32[]{:S(2)}) %collective-permute-start.43) | collective-permute-done | bytes 221216 | tf_op jit(solution)/shard_map/ppermute | solution.py:976
  177.0 3.5 %join_halves.1 = (bf16[2,8,48,1536]{3,2,1,0:T(8,128)(2,1)}, bf16[2,8,48,1536]{3,2,1,0:T(8,128)(2,1)}, bf16[2,8,48,1536]{3,2,1,0:T(8,128)(2,1)}) custom-call(s32[4]{0:T(128)S(1)} %pad_add_fusion.p, bf16[8,2,48,1536]{3,2,1,0:T(8,128)(2,1)S(1)} %bitcast.116, bf16[8,2,48,1536]{3,2,1,0:T(8,128)(2,1)S(1)} %collective-permute-done.47.at, ...), custom_call_target="tpu_custom_call" | custom-call | flops 1000 | bytes 1000 | tf_op jit(solution)/shard_map/join_halves/pallas_call | solution.py:30
  (211 shorter events, 85.9 us)
Async XLA Ops:
  3.3 13.1 %collective-permute-start = (bf16[784,256]{1,0:T(8,128)(2,1)S(1)}, bf16[784,256]{1,0:T(8,128)(2,1)S(1)}, u32[]{:S(2)}, u32[]{:S(2)}) collective-permute-start(bf16[784,256]{1,0:T(8,128)(2,1)S(1)} %pack_edges.1.xm), channel_id=1, source_target_pairs={{0,1},{1,0},{2,3},{3,2},{4,5},{5,4},{6,7},{7,6},{8,9},{9,8},{10,11... | collective-permute-start | bytes 1204232 | tf_op jit(solution)/shard_map/ppermute | solution.py:785
  6.5 17.5 %collective-permute-start.3 = (bf16[768,256]{1,0:T(8,128)(2,1)S(1)}, bf16[768,256]{1,0:T(8,128)(2,1)S(1)}, u32[]{:S(2)}, u32[]{:S(2)}) collective-permute-start(bf16[768,256]{1,0:T(8,128)(2,1)S(1)} %slice.77.xm), channel_id=1, source_target_pairs={{0,1},{1,0},{2,3},{3,2},{4,5},{5,4},{6,7},{7,6},{8,9},{9,8},{10,11... | collective-permute-start | bytes 1179656 | tf_op jit(solution)/shard_map/ppermute | solution.py:785
  28.1 48.8 %collective-permute-start.13 = (bf16[512,1536]{1,0:T(8,128)(2,1)}, bf16[512,1536]{1,0:T(8,128)(2,1)}, u32[]{:S(2)}, u32[]{:S(2)}) collective-permute-start(bf16[512,1536]{1,0:T(8,128)(2,1)} %get-tuple-element.95.n), channel_id=1, source_target_pairs={{0,2},{2,0},{4,6},{6,4},{8,10},{10,8},{12,14},{14,12},{16,18},{18,... | collective-permute-start | bytes 4718600 | tf_op jit(solution)/shard_map/ppermute | solution.py:933
  28.2 20.3 %collective-permute-start.6 = (bf16[512,768]{1,0:T(8,128)(2,1)S(1)}, bf16[512,768]{1,0:T(8,128)(2,1)S(1)}, u32[]{:S(2)}, u32[]{:S(2)}) collective-permute-start(bf16[512,768]{1,0:T(8,128)(2,1)S(1)} %get-tuple-element.68), channel_id=1, source_target_pairs={{0,1},{1,0},{2,3},{3,2},{4,5},{5,4},{6,7},{7,6},{8,9},{9,8},{10,11... | collective-permute-start | bytes 2359304 | tf_op jit(solution)/shard_map/ppermute | solution.py:785
  67.1 9.7 %collective-permute-start.11 = (bf16[512,384]{1,0:T(8,128)(2,1)}, bf16[512,384]{1,0:T(8,128)(2,1)}, u32[]{:S(2)}, u32[]{:S(2)}) collective-permute-start(bf16[512,384]{1,0:T(8,128)(2,1)} %get-tuple-element.90.vt), channel_id=1, source_target_pairs={{0,2},{2,0},{4,6},{6,4},{8,10},{10,8},{12,14},{14,12},{16,18},{18,... | collective-permute-start | bytes 1179656 | tf_op jit(solution)/shard_map/ppermute | solution.py:933
  68.6 20.2 %collective-permute-start.8 = (bf16[512,768]{1,0:T(8,128)(2,1)}, bf16[512,768]{1,0:T(8,128)(2,1)}, u32[]{:S(2)}, u32[]{:S(2)}) collective-permute-start(bf16[512,768]{1,0:T(8,128)(2,1)} %get-tuple-element.96.a), channel_id=1, source_target_pairs={{0,1},{1,0},{2,3},{3,2},{4,5},{5,4},{6,7},{7,6},{8,9},{9,8},{10,11... | collective-permute-start | bytes 2359304 | tf_op jit(solution)/shard_map/ppermute | solution.py:785
  83.4 10.1 %collective-permute-start.16 = (bf16[96,1536]{1,0:T(8,128)(2,1)}, bf16[96,1536]{1,0:T(8,128)(2,1)}, u32[]{:S(2)}, u32[]{:S(2)}) collective-permute-start(bf16[96,1536]{1,0:T(8,128)(2,1)} %get-tuple-element.135), channel_id=1, source_target_pairs={{0,8},{2,10},{8,16},{10,18},{16,24},{18,26},{24,28},{26,30},{28,20... | collective-permute-start | bytes 884744 | tf_op jit(solution)/shard_map/ppermute | solution.py:976
  89.3 13.3 %collective-permute-start.17 = (bf16[96,1536]{1,0:T(8,128)(2,1)}, bf16[96,1536]{1,0:T(8,128)(2,1)S(1)}, u32[]{:S(2)}, u32[]{:S(2)}) collective-permute-start(bf16[96,1536]{1,0:T(8,128)(2,1)} %get-tuple-element.134), channel_id=1, source_target_pairs={{8,0},{10,2},{16,8},{18,10},{24,16},{26,18},{28,24},{30,26},{20,28... | collective-permute-start | bytes 884744 | tf_op jit(solution)/shard_map/ppermute | solution.py:976
  94.5 10.1 %collective-permute-start.18 = (bf16[96,1536]{1,0:T(8,128)(2,1)S(1)}, bf16[96,1536]{1,0:T(8,128)(2,1)S(1)}, u32[]{:S(2)}, u32[]{:S(2)}) collective-permute-start(bf16[96,1536]{1,0:T(8,128)(2,1)S(1)} %fusion.6), channel_id=1, source_target_pairs={{0,8},{2,10},{8,16},{10,18},{16,24},{18,26},{24,28},{26,30},{28,20... | collective-permute-start | bytes 884744 | tf_op jit(solution)/shard_map/ppermute | solution.py:976
  102.5 10.7 %collective-permute-start.20 = (bf16[48,1536]{1,0:T(8,128)(2,1)S(1)}, bf16[48,1536]{1,0:T(8,128)(2,1)S(1)}, u32[]{:S(2)}, u32[]{:S(2)}) collective-permute-start(bf16[48,1536]{1,0:T(8,128)(2,1)S(1)} %get-tuple-element.98), channel_id=1, source_target_pairs={{8,0},{10,2},{16,8},{18,10},{24,16},{26,18},{28,24},{30,26},{20,28... | collective-permute-start | bytes 442376 | tf_op jit(solution)/shard_map/ppermute | solution.py:976
  102.6 10.6 %collective-permute-start.21 = (bf16[48,1536]{1,0:T(8,128)(2,1)S(1)}, bf16[48,1536]{1,0:T(8,128)(2,1)S(1)}, u32[]{:S(2)}, u32[]{:S(2)}) collective-permute-start(bf16[48,1536]{1,0:T(8,128)(2,1)S(1)} %get-tuple-element.99), channel_id=1, source_target_pairs={{0,8},{2,10},{8,16},{10,18},{16,24},{18,26},{24,28},{26,30},{28,20... | collective-permute-start | bytes 442376 | tf_op jit(solution)/shard_map/ppermute | solution.py:976
  104.9 10.5 %collective-permute-start.22 = (bf16[96,1536]{1,0:T(8,128)(2,1)S(1)}, bf16[96,1536]{1,0:T(8,128)(2,1)S(1)}, u32[]{:S(2)}, u32[]{:S(2)}) collective-permute-start(bf16[96,1536]{1,0:T(8,128)(2,1)S(1)} %get-tuple-element.132), channel_id=1, source_target_pairs={{0,8},{2,10},{8,16},{10,18},{16,24},{18,26},{24,28},{26,30},{28,20... | collective-permute-start | bytes 884744 | tf_op jit(solution)/shard_map/ppermute | solution.py:976
  112.6 25.7 %collective-permute-start.34 = (bf16[512,768]{1,0:T(8,128)(2,1)S(1)}, bf16[512,768]{1,0:T(8,128)(2,1)S(1)}, u32[]{:S(2)}, u32[]{:S(2)}) collective-permute-start(bf16[512,768]{1,0:T(8,128)(2,1)S(1)} %get-tuple-element.101), channel_id=1, source_target_pairs={{0,1},{1,0},{2,3},{3,2},{4,5},{5,4},{6,7},{7,6},{8,9},{9,8},{10,11... | collective-permute-start | bytes 2359304 | tf_op jit(solution)/shard_map/ppermute | solution.py:785
  113.4 9.6 %collective-permute-start.29 = (bf16[48,1536]{1,0:T(8,128)(2,1)S(1)}, bf16[48,1536]{1,0:T(8,128)(2,1)S(1)}, u32[]{:S(2)}, u32[]{:S(2)}) collective-permute-start(bf16[48,1536]{1,0:T(8,128)(2,1)S(1)} %get-tuple-element.102), channel_id=1, source_target_pairs={{8,0},{10,2},{16,8},{18,10},{24,16},{26,18},{28,24},{30,26},{20,28... | collective-permute-start | bytes 442376 | tf_op jit(solution)/shard_map/ppermute | solution.py:976
  113.8 9.2 %collective-permute-start.30 = (bf16[48,1536]{1,0:T(8,128)(2,1)S(1)}, bf16[48,1536]{1,0:T(8,128)(2,1)S(1)}, u32[]{:S(2)}, u32[]{:S(2)}) collective-permute-start(bf16[48,1536]{1,0:T(8,128)(2,1)S(1)} %get-tuple-element.103), channel_id=1, source_target_pairs={{0,8},{2,10},{8,16},{10,18},{16,24},{18,26},{24,28},{26,30},{28,20... | collective-permute-start | bytes 442376 | tf_op jit(solution)/shard_map/ppermute | solution.py:976
  124.3 11.9 %collective-permute-start.25 = (bf16[96,1536]{1,0:T(8,128)(2,1)S(1)}, bf16[96,1536]{1,0:T(8,128)(2,1)S(1)}, u32[]{:S(2)}, u32[]{:S(2)}) collective-permute-start(bf16[96,1536]{1,0:T(8,128)(2,1)S(1)} %fusion.2), channel_id=1, source_target_pairs={{0,8},{2,10},{8,16},{10,18},{16,24},{18,26},{24,28},{26,30},{28,20... | collective-permute-start | bytes 884744 | tf_op jit(solution)/shard_map/ppermute | solution.py:976
  125.9 11.9 %collective-permute-start.27 = (bf16[96,1536]{1,0:T(8,128)(2,1)S(1)}, bf16[96,1536]{1,0:T(8,128)(2,1)S(1)}, u32[]{:S(2)}, u32[]{:S(2)}) collective-permute-start(bf16[96,1536]{1,0:T(8,128)(2,1)S(1)} %fusion.2), channel_id=1, source_target_pairs={{8,0},{10,2},{16,8},{18,10},{24,16},{26,18},{28,24},{30,26},{20,28... | collective-permute-start | bytes 884744 | tf_op jit(solution)/shard_map/ppermute | solution.py:976
  136.2 10.8 %collective-permute-start.26 = (bf16[96,1536]{1,0:T(8,128)(2,1)S(1)}, bf16[96,1536]{1,0:T(8,128)(2,1)S(1)}, u32[]{:S(2)}, u32[]{:S(2)}) collective-permute-start(bf16[96,1536]{1,0:T(8,128)(2,1)S(1)} %collective-permute-done.25), channel_id=1, source_target_pairs={{0,8},{2,10},{8,16},{10,18},{16,24},{18,26},{24,28},{26,30},{28,20... | collective-permute-start | bytes 884744 | tf_op jit(solution)/shard_map/ppermute | solution.py:976
  137.9 10.9 %collective-permute-start.28 = (bf16[96,1536]{1,0:T(8,128)(2,1)S(1)}, bf16[96,1536]{1,0:T(8,128)(2,1)S(1)}, u32[]{:S(2)}, u32[]{:S(2)}) collective-permute-start(bf16[96,1536]{1,0:T(8,128)(2,1)S(1)} %collective-permute-done.27), channel_id=1, source_target_pairs={{8,0},{10,2},{16,8},{18,10},{24,16},{26,18},{28,24},{30,26},{20,28... | collective-permute-start | bytes 884744 | tf_op jit(solution)/shard_map/ppermute | solution.py:976
  147.0 9.9 %collective-permute-start.41 = (bf16[96,1536]{1,0:T(8,128)(2,1)S(1)}, bf16[96,1536]{1,0:T(8,128)(2,1)S(1)}, u32[]{:S(2)}, u32[]{:S(2)}) collective-permute-start(bf16[96,1536]{1,0:T(8,128)(2,1)S(1)} %collective-permute-done.26), channel_id=1, source_target_pairs={{0,8},{2,10},{8,16},{10,18},{16,24},{18,26},{24,28},{26,30},{28,20... | collective-permute-start | bytes 884744 | tf_op jit(solution)/shard_map/ppermute | solution.py:976
  148.8 10.0 %collective-permute-start.42 = (bf16[96,1536]{1,0:T(8,128)(2,1)S(1)}, bf16[96,1536]{1,0:T(8,128)(2,1)S(1)}, u32[]{:S(2)}, u32[]{:S(2)}) collective-permute-start(bf16[96,1536]{1,0:T(8,128)(2,1)S(1)} %collective-permute-done.28), channel_id=1, source_target_pairs={{8,0},{10,2},{16,8},{18,10},{24,16},{26,18},{28,24},{30,26},{20,28... | collective-permute-start | bytes 884744 | tf_op jit(solution)/shard_map/ppermute | solution.py:976
  150.3 11.7 %collective-permute-start.39 = (bf16[72,1536]{1,0:T(8,128)(2,1)S(1)}, bf16[72,1536]{1,0:T(8,128)(2,1)S(1)}, u32[]{:S(2)}, u32[]{:S(2)}) collective-permute-start(bf16[72,1536]{1,0:T(8,128)(2,1)S(1)} %collective-permute-done.36), channel_id=1, source_target_pairs={{8,0},{10,2},{16,8},{18,10},{24,16},{26,18},{28,24},{30,26},{20,28... | collective-permute-start | bytes 663560 | tf_op jit(solution)/shard_map/ppermute | solution.py:976
  152.3 9.7 %collective-permute-start.40 = (bf16[72,1536]{1,0:T(8,128)(2,1)S(1)}, bf16[72,1536]{1,0:T(8,128)(2,1)S(1)}, u32[]{:S(2)}, u32[]{:S(2)}) collective-permute-start(bf16[72,1536]{1,0:T(8,128)(2,1)S(1)} %collective-permute-done.37), channel_id=1, source_target_pairs={{0,8},{2,10},{8,16},{10,18},{16,24},{18,26},{24,28},{26,30},{28,20... | collective-permute-start | bytes 663560 | tf_op jit(solution)/shard_map/ppermute | solution.py:976
  156.9 12.5 %collective-permute-start.46 = (bf16[96,1536]{1,0:T(8,128)(2,1)S(1)}, bf16[96,1536]{1,0:T(8,128)(2,1)S(1)}, u32[]{:S(2)}, u32[]{:S(2)}) collective-permute-start(bf16[96,1536]{1,0:T(8,128)(2,1)S(1)} %collective-permute-done.41), channel_id=1, source_target_pairs={{0,8},{2,10},{8,16},{10,18},{16,24},{18,26},{24,28},{26,30},{28,20... | collective-permute-start | bytes 884744 | tf_op jit(solution)/shard_map/ppermute | solution.py:976
  (64 other events, 429.6 us)

commit v7 on v6

--- a/solution.py
+++ b/solution.py
@@ -428,7 +428,7 @@
 
 def taps_grad(places, before, glu, after, d_conv, scale):
     frames, chans = glu.shape
-    part = 32
+    part = 128
 
     def body(p, b, g, a, d, out, wide, sums):
         fill_edges_first(wide, b, g, a)

time: 181 us -> 181 us (level)
  no operation moved by 1% of the time
where the time goes in v7:
time: 181 us
  Pallas kernels  62.2 us (34%)
  starting transfers between devices  55.6 us (31%)
  waiting for transfers between devices  46.1 us (25%)
  local copies, waits for them, and re-layouts  12.6 us (7%)
  other arithmetic  2.59 us (1%)
    pallas_call x17, Pallas kernels, call(): pl.pallas_call(body, out_shape=[s for s, _ in outs], grid_spec=pltpu.Pref...  62.2 us
    ppermute x28, starting transfers between devices, send(): lax.ppermute(x, 'seq', way)  34.5 us
    ppermute x28, waiting for transfers between devices, send(): lax.ppermute(x, 'seq', way)  23.7 us
    ppermute x8, waiting for transfers between devices, other(): return lax.ppermute(values, 'tp', [(0, 1), (1, 0)])  17.2 us
    ppermute x8, starting transfers between devices, other(): return lax.ppermute(values, 'tp', [(0, 1), (1, 0)])  11.1 us
    unnamed x79, local copies, waits for them, and re-layouts  10.7 us
    ppermute x2, starting transfers between devices, rims(): before = lax.ppermute(tail, 'seq', [(i, i + 1) for i in range(count - 1)])  5.09 us
  transfers between devices with their start and end apart: 49, of which 22 were waited for; matrix products, arithmetic and copies ran while one was open for 2% of the time, Pallas kernels for 30%

profile of v7, /device:TPU:0, one launch (start us, length us, event | category | flops | bytes accessed | tf_op | source)
XLA Modules:
  0.0 180.7 jit_solution(17314248135154622893)
XLA Ops:
  3.3 3.0 %collective-permute-start = (bf16[784,256]{1,0:T(8,128)(2,1)S(1)}, bf16[784,256]{1,0:T(8,128)(2,1)S(1)}, u32[]{:S(2)}, u32[]{:S(2)}) collective-permute-start(bf16[784,256]{1,0:T(8,128)(2,1)S(1)} %pack_edges.1.xm), channel_id=1, source_target_pairs={{0,1},{1,0},{2,3},{3,2},{4,5},{5,4},{6,7},{7,6},{8,9},{9,8},{10,11... | collective-permute-start | bytes 1204232 | tf_op jit(solution)/shard_map/ppermute | solution.py:785
  11.5 5.0 %collective-permute-done.xt.gt = bf16[784,256]{1,0:T(8,128)(2,1)S(1)} collective-permute-done((bf16[784,256]{1,0:T(8,128)(2,1)S(1)}, bf16[784,256]{1,0:T(8,128)(2,1)S(1)}, u32[]{:S(2)}, u32[]{:S(2)}) %collective-permute-start) | collective-permute-done | bytes 401440 | tf_op jit(solution)/shard_map/ppermute | solution.py:785
  17.4 4.0 %glu_edges.1 = (bf16[512,1536]{1,0:T(8,128)(2,1)}, f32[512,768]{1,0:T(8,128)S(1)}, f32[512,128]{1,0:T(8,128)S(1)}, bf16[512,768]{1,0:T(8,128)(2,1)S(1)}, f32[512...) custom-call(s32[4]{0:T(128)S(1)} %pad_add_fusion.p, bf16[784,256]{1,0:T(8,128)(2,1)S(1)} %copy-done.19, ...), custom_call_target="tpu_custom_call" | custom-call | flops 1000 | bytes 1000 | tf_op jit(solution)/shard_map/glu_edges/pallas_call | solution.py:30
  21.4 2.6 %collective-permute-done.3.xt = bf16[768,256]{1,0:T(8,128)(2,1)S(1)} collective-permute-done((bf16[768,256]{1,0:T(8,128)(2,1)S(1)}, bf16[768,256]{1,0:T(8,128)(2,1)S(1)}, u32[]{:S(2)}, u32[]{:S(2)}) %collective-permute-start.3) | collective-permute-done | bytes 393248 | tf_op jit(solution)/shard_map/ppermute | solution.py:785
  24.0 4.0 %glu_middle.1 = (bf16[512,1536]{1,0:T(8,128)(2,1)}, f32[512,768]{1,0:T(8,128)S(1)}, f32[512,128]{1,0:T(8,128)S(1)}, bf16[512,768]{1,0:T(8,128)(2,1)S(1)}, f32[51...) custom-call(s32[4]{0:T(128)S(1)} %pad_add_fusion.p, ...), custom_call_target="tpu_custom_call", output_to_operand_aliasing={{0}: (7, {}), {1}: (8, {}), {2}: (9, {}), {3}: (10, {}), {4... | custom-call | flops 1000 | bytes 1000 | tf_op jit(solution)/shard_map/glu_middle/pallas_call | solution.py:30
  33.4 2.8 %collective-permute-done.4.a = bf16[16,768]{1,0:T(8,128)(2,1)S(1)} collective-permute-done((bf16[16,768]{1,0:T(8,128)(2,1)S(1)}, bf16[16,768]{1,0:T(8,128)(2,1)S(1)}, u32[]{:S(2)}, u32[]{:S(2)}) %collective-permute-start.4) | collective-permute-done | bytes 24608 | tf_op jit(solution)/shard_map/ppermute | solution.py:939
  36.1 5.2 %conv_forward.1 = (f32[512,768]{1,0:T(8,128)S(1)}, f32[8,512]{1,0:T(8,128)S(1)}) custom-call(s32[4]{0:T(128)S(1)} %pad_add_fusion.p, bf16[16,768]{1,0:T(8,128)(2,1)S(1)} %collective-permute-done.2.b, bf16[512,768]{1,0:T(8,128)(2,1)S(1)} %get-tuple-element.77.g, bf16[16,768]{1,0:T(8,128)(2,1)S(1)} %collective-permute-done.4.a, f32[32,768]{1,0:T(8,128)S(1)} %bitcast.123), custom_call_target="tpu_custom_call" | custom-call | flops 1000 | bytes 1000 | tf_op jit(solution)/shard_map/conv_forward/pallas_call | solution.py:30
  43.0 5.4 %collective-permute-done.5.st = f32[8,512]{1,0:T(8,128)S(1)} collective-permute-done((f32[8,512]{1,0:T(8,128)S(1)}, f32[8,512]{1,0:T(8,128)S(1)}, u32[]{:S(2)}, u32[]{:S(2)}) %collective-permute-start.5) | collective-permute-done | bytes 16416 | tf_op jit(solution)/shard_map/ppermute | solution.py:785
  48.5 2.7 %act_step.1 = (f32[512,768]{1,0:T(8,128)S(1)}, f32[512,768]{1,0:T(8,128)S(1)}, f32[8,512]{1,0:T(8,128)S(1)}, f32[1,768]{1,0:T(1,128)S(1)}) custom-call(s32[4]{0:T(128)S(1)} %pad_add_fusion.p, f32[512,768]{1,0:T(8,128)S(1)} %get-tuple-element.78.x, f32[8,512]{1,0:T(8,128)S(1)} %get-tuple-element.79.sm, f32[8,512]{1,0:T(8,128)S(1)} %collective-permute-done.5.st, ...), custom_call_target="tpu_custom_call" | custom-call | flops 1000 | bytes 1000 | tf_op jit(solution)/shard_map/act_step/pallas_call | solution.py:30
  55.0 3.2 %d_conv_step.1 = (bf16[512,768]{1,0:T(8,128)(2,1)S(1)}, bf16[512,768]{1,0:T(8,128)(2,1)}, bf16[16,768]{1,0:T(8,128)(2,1)S(1)}, bf16[16,768]{1,0:T(8,128)(2,1)S(1)}) custom-call(s32[4]{0:T(128)S(1)} %pad_add_fusion.p, f32[512,768]{1,0:T(8,128)S(1)} %get-tuple-element.81.d, f32[512,768]{1,0:T(8,128)S(1)} %get-tuple-element.82.h, ...), custom_call_target="tpu_custom_call" | custom-call | flops 1000 | bytes 1000 | tf_op jit(solution)/shard_map/d_conv_step/pallas_call | solution.py:30
  59.5 3.0 %collective-permute-start.9 = (bf16[16,768]{1,0:T(8,128)(2,1)S(1)}, bf16[16,768]{1,0:T(8,128)(2,1)S(1)}, u32[]{:S(2)}, u32[]{:S(2)}) collective-permute-start(bf16[16,768]{1,0:T(8,128)(2,1)S(1)} %get-tuple-element.85), channel_id=1, source_target_pairs={{0,2},{2,4},{4,6},{6,8},{8,10},{10,12},{12,14},{14,16},{16,18},{18... | collective-permute-start | bytes 73736 | tf_op jit(solution)/shard_map/ppermute | solution.py:938
  63.4 3.7 %d_glu_other.1 = (bf16[512,384]{1,0:T(8,128)(2,1)}, bf16[512,384]{1,0:T(8,128)(2,1)}) custom-call(s32[4]{0:T(128)S(1)} %pad_add_fusion.p, bf16[16,768]{1,0:T(8,128)(2,1)S(1)} %collective-permute-done.9.b, bf16[512,768]{1,0:T(8,128)(2,1)S(1)} %get-tuple-element.104.d, bf16[16,768]{1,0:T(8,128)(2,1)S(1)} %collective-permute-done.10.a, ...), custom_call_target="tpu_custom_call" | custom-call | flops 1000 | bytes 1000 | tf_op jit(solution)/shard_map/d_glu_other/pallas_call | solution.py:30
  73.7 3.1 %d_glu_own.1 = (bf16[512,384]{1,0:T(8,128)(2,1)S(1)}, bf16[512,384]{1,0:T(8,128)(2,1)S(1)}) custom-call(s32[4]{0:T(128)S(1)} %pad_add_fusion.p, bf16[16,768]{1,0:T(8,128)(2,1)S(1)} %copy-done.31, bf16[512,768]{1,0:T(8,128)(2,1)S(1)} %copy-done.14, bf16[16,768]{1,0:T(8,128)(2,1)S(1)} %copy-done.29, f32[32,768]{1,0:T(8,128)S(1)} %bitcast.125, ...), custom_call_target="tpu_custom_call" | custom-call | flops 1000 | bytes 1000 | tf_op jit(solution)/shard_map/d_glu_own/pallas_call | solution.py:30
  76.9 5.6 %pair_grads.1 = bf16[8,2,48,1536]{3,2,1,0:T(8,128)(2,1)S(1)} custom-call(s32[4]{0:T(128)S(1)} %pad_add_fusion.p, bf16[512,384]{1,0:T(8,128)(2,1)S(1)} %get-tuple-element.100.mv.vo, bf16[512,384]{1,0:T(8,128)(2,1)S(1)} %get-tuple-element.93.mg.go, bf16[512,384]{1,0:T(8,128)(2,1)} %collective-permute-done.11.tv, bf16[512,384]{1,0:T(8,128)(2,1)} %collective-permute-done.12.tg, ...), custom_call_target="tpu_custom_call" | custom-call | flops 1000 | bytes 1000 | tf_op jit(solution)/shard_map/pair_grads/pallas_call | solution.py:30
  83.4 3.6 %collective-permute-start.16 = (bf16[96,1536]{1,0:T(8,128)(2,1)}, bf16[96,1536]{1,0:T(8,128)(2,1)}, u32[]{:S(2)}, u32[]{:S(2)}) collective-permute-start(bf16[96,1536]{1,0:T(8,128)(2,1)} %get-tuple-element.135), channel_id=1, source_target_pairs={{0,8},{2,10},{8,16},{10,18},{16,24},{18,26},{24,28},{26,30},{28,20... | collective-permute-start | bytes 884744 | tf_op jit(solution)/shard_map/ppermute | solution.py:976
  98.1 4.4 %out_grads.1 = bf16[384,1536]{1,0:T(8,128)(2,1)S(1)} custom-call(s32[4]{0:T(128)S(1)} %pad_add_fusion.p, bf16[768,512]{1,0:T(8,128)(2,1)S(1)} %copy-done.10, bf16[384,512]{1,0:T(8,128)(2,1)S(1)} %copy-done.27, bf16[512,768]{1,0:T(8,128)(2,1)} %get-tuple-element.96.a, bf16[512,768]{1,0:T(8,128)(2,1)} %collective-permute-done.8.b, ...), custom_call_target="tpu_custom_call" | custom-call | flops 1000 | bytes 1000 | tf_op jit(solution)/shard_map/out_grads/pallas_call | solution.py:30
  106.9 5.6 %d_normed_terms.1 = (bf16[512,768]{1,0:T(8,128)(2,1)S(1)}, bf16[512,768]{1,0:T(8,128)(2,1)S(1)}) custom-call(s32[4]{0:T(128)S(1)} %pad_add_fusion.p, bf16[512,384]{1,0:T(8,128)(2,1)S(1)} %get-tuple-element.100.mv.vo, bf16[512,384]{1,0:T(8,128)(2,1)} %get-tuple-element.90.vt, bf16[512,384]{1,0:T(8,128)(2,1)S(1)} %copy-done.21, ...), custom_call_target="tpu_custom_call" | custom-call | flops 1000 | bytes 1000 | tf_op jit(solution)/shard_map/d_normed_terms/pallas_call | solution.py:30
  117.7 4.9 %taps_grad.1 = f32[32,768]{1,0:T(8,128)S(1)} custom-call(s32[4]{0:T(128)S(1)} %pad_add_fusion.p, bf16[16,768]{1,0:T(8,128)(2,1)S(1)} %copy-done.33, bf16[512,768]{1,0:T(8,128)(2,1)S(1)} %copy-done.17, bf16[16,768]{1,0:T(8,128)(2,1)S(1)} %copy-done.35, bf16[512,768]{1,0:T(8,128)(2,1)S(1)} %copy-done.15), custom_call_target="tpu_custom_call" | custom-call | flops 1000 | bytes 1000 | tf_op jit(solution)/shard_map/taps_grad/pallas_call | solution.py:30
  133.6 2.6 %collective-permute-done.32 = bf16[48,1536]{1,0:T(8,128)(2,1)S(1)} collective-permute-done((bf16[48,1536]{1,0:T(8,128)(2,1)S(1)}, bf16[48,1536]{1,0:T(8,128)(2,1)S(1)}, u32[]{:S(2)}, u32[]{:S(2)}) %collective-permute-start.32) | collective-permute-done | bytes 147488 | tf_op jit(solution)/shard_map/ppermute | solution.py:976
  143.8 3.2 %input_step.1 = bf16[768,512]{1,0:T(8,128)(2,1)} custom-call(s32[4]{0:T(128)S(1)} %pad_add_fusion.p, bf16[512,768]{1,0:T(8,128)(2,1)S(1)} %get-tuple-element.109.tm, bf16[512,768]{1,0:T(8,128)(2,1)S(1)} %collective-permute-done.34.tr, f32[512,768]{1,0:T(8,128)S(1)} %copy-done.5, f32[1,768]{1,0:T(1,128)S(1)} %broadcast_in_dim.41.gm.g, ...), custom_call_target="tpu_custom_call" | custom-call | flops 1000 | bytes 1000 | tf_op jit(solution)/shard_map/input_step/pallas_call | solution.py:30
  152.3 4.5 %out_step.1 = bf16[768,512]{1,0:T(8,128)(2,1)} custom-call(s32[4]{0:T(128)S(1)} %pad_add_fusion.p, bf16[768,512]{1,0:T(8,128)(2,1)S(1)} %copy-done.8, bf16[768,1536]{1,0:T(8,128)(2,1)S(1)} %copy-done.12, bf16[512,768]{1,0:T(8,128)(2,1)} %get-tuple-element.96.a, bf16[512,768]{1,0:T(8,128)(2,1)} %collective-permute-done.8.b), custom_call_target="tpu_custom_call" | custom-call | flops 1000 | bytes 1000 | tf_op jit(solution)/shard_map/out_step/pallas_call | solution.py:30
  158.8 3.3 %collective-permute-done.39 = bf16[72,1536]{1,0:T(8,128)(2,1)S(1)} collective-permute-done((bf16[72,1536]{1,0:T(8,128)(2,1)S(1)}, bf16[72,1536]{1,0:T(8,128)(2,1)S(1)}, u32[]{:S(2)}, u32[]{:S(2)}) %collective-permute-start.39) | collective-permute-done | bytes 221216 | tf_op jit(solution)/shard_map/ppermute | solution.py:976
  164.1 4.0 %collective-permute-done.43 = bf16[72,1536]{1,0:T(8,128)(2,1)S(1)} collective-permute-done((bf16[72,1536]{1,0:T(8,128)(2,1)S(1)}, bf16[72,1536]{1,0:T(8,128)(2,1)S(1)}, u32[]{:S(2)}, u32[]{:S(2)}) %collective-permute-start.43) | collective-permute-done | bytes 221216 | tf_op jit(solution)/shard_map/ppermute | solution.py:976
  177.0 3.5 %join_halves.1 = (bf16[2,8,48,1536]{3,2,1,0:T(8,128)(2,1)}, bf16[2,8,48,1536]{3,2,1,0:T(8,128)(2,1)}, bf16[2,8,48,1536]{3,2,1,0:T(8,128)(2,1)}) custom-call(s32[4]{0:T(128)S(1)} %pad_add_fusion.p, bf16[8,2,48,1536]{3,2,1,0:T(8,128)(2,1)S(1)} %bitcast.116, bf16[8,2,48,1536]{3,2,1,0:T(8,128)(2,1)S(1)} %collective-permute-done.47.at, ...), custom_call_target="tpu_custom_call" | custom-call | flops 1000 | bytes 1000 | tf_op jit(solution)/shard_map/join_halves/pallas_call | solution.py:30
  (211 shorter events, 86.3 us)
Async XLA Ops:
  3.3 13.1 %collective-permute-start = (bf16[784,256]{1,0:T(8,128)(2,1)S(1)}, bf16[784,256]{1,0:T(8,128)(2,1)S(1)}, u32[]{:S(2)}, u32[]{:S(2)}) collective-permute-start(bf16[784,256]{1,0:T(8,128)(2,1)S(1)} %pack_edges.1.xm), channel_id=1, source_target_pairs={{0,1},{1,0},{2,3},{3,2},{4,5},{5,4},{6,7},{7,6},{8,9},{9,8},{10,11... | collective-permute-start | bytes 1204232 | tf_op jit(solution)/shard_map/ppermute | solution.py:785
  6.5 17.5 %collective-permute-start.3 = (bf16[768,256]{1,0:T(8,128)(2,1)S(1)}, bf16[768,256]{1,0:T(8,128)(2,1)S(1)}, u32[]{:S(2)}, u32[]{:S(2)}) collective-permute-start(bf16[768,256]{1,0:T(8,128)(2,1)S(1)} %slice.77.xm), channel_id=1, source_target_pairs={{0,1},{1,0},{2,3},{3,2},{4,5},{5,4},{6,7},{7,6},{8,9},{9,8},{10,11... | collective-permute-start | bytes 1179656 | tf_op jit(solution)/shard_map/ppermute | solution.py:785
  28.1 48.8 %collective-permute-start.13 = (bf16[512,1536]{1,0:T(8,128)(2,1)}, bf16[512,1536]{1,0:T(8,128)(2,1)}, u32[]{:S(2)}, u32[]{:S(2)}) collective-permute-start(bf16[512,1536]{1,0:T(8,128)(2,1)} %get-tuple-element.95.n), channel_id=1, source_target_pairs={{0,2},{2,0},{4,6},{6,4},{8,10},{10,8},{12,14},{14,12},{16,18},{18,... | collective-permute-start | bytes 4718600 | tf_op jit(solution)/shard_map/ppermute | solution.py:933
  28.2 20.3 %collective-permute-start.6 = (bf16[512,768]{1,0:T(8,128)(2,1)S(1)}, bf16[512,768]{1,0:T(8,128)(2,1)S(1)}, u32[]{:S(2)}, u32[]{:S(2)}) collective-permute-start(bf16[512,768]{1,0:T(8,128)(2,1)S(1)} %get-tuple-element.68), channel_id=1, source_target_pairs={{0,1},{1,0},{2,3},{3,2},{4,5},{5,4},{6,7},{7,6},{8,9},{9,8},{10,11... | collective-permute-start | bytes 2359304 | tf_op jit(solution)/shard_map/ppermute | solution.py:785
  67.1 9.7 %collective-permute-start.11 = (bf16[512,384]{1,0:T(8,128)(2,1)}, bf16[512,384]{1,0:T(8,128)(2,1)}, u32[]{:S(2)}, u32[]{:S(2)}) collective-permute-start(bf16[512,384]{1,0:T(8,128)(2,1)} %get-tuple-element.90.vt), channel_id=1, source_target_pairs={{0,2},{2,0},{4,6},{6,4},{8,10},{10,8},{12,14},{14,12},{16,18},{18,... | collective-permute-start | bytes 1179656 | tf_op jit(solution)/shard_map/ppermute | solution.py:933
  68.6 20.2 %collective-permute-start.8 = (bf16[512,768]{1,0:T(8,128)(2,1)}, bf16[512,768]{1,0:T(8,128)(2,1)}, u32[]{:S(2)}, u32[]{:S(2)}) collective-permute-start(bf16[512,768]{1,0:T(8,128)(2,1)} %get-tuple-element.96.a), channel_id=1, source_target_pairs={{0,1},{1,0},{2,3},{3,2},{4,5},{5,4},{6,7},{7,6},{8,9},{9,8},{10,11... | collective-permute-start | bytes 2359304 | tf_op jit(solution)/shard_map/ppermute | solution.py:785
  83.4 10.1 %collective-permute-start.16 = (bf16[96,1536]{1,0:T(8,128)(2,1)}, bf16[96,1536]{1,0:T(8,128)(2,1)}, u32[]{:S(2)}, u32[]{:S(2)}) collective-permute-start(bf16[96,1536]{1,0:T(8,128)(2,1)} %get-tuple-element.135), channel_id=1, source_target_pairs={{0,8},{2,10},{8,16},{10,18},{16,24},{18,26},{24,28},{26,30},{28,20... | collective-permute-start | bytes 884744 | tf_op jit(solution)/shard_map/ppermute | solution.py:976
  89.3 13.3 %collective-permute-start.17 = (bf16[96,1536]{1,0:T(8,128)(2,1)}, bf16[96,1536]{1,0:T(8,128)(2,1)S(1)}, u32[]{:S(2)}, u32[]{:S(2)}) collective-permute-start(bf16[96,1536]{1,0:T(8,128)(2,1)} %get-tuple-element.134), channel_id=1, source_target_pairs={{8,0},{10,2},{16,8},{18,10},{24,16},{26,18},{28,24},{30,26},{20,28... | collective-permute-start | bytes 884744 | tf_op jit(solution)/shard_map/ppermute | solution.py:976
  94.5 10.1 %collective-permute-start.18 = (bf16[96,1536]{1,0:T(8,128)(2,1)S(1)}, bf16[96,1536]{1,0:T(8,128)(2,1)S(1)}, u32[]{:S(2)}, u32[]{:S(2)}) collective-permute-start(bf16[96,1536]{1,0:T(8,128)(2,1)S(1)} %fusion.6), channel_id=1, source_target_pairs={{0,8},{2,10},{8,16},{10,18},{16,24},{18,26},{24,28},{26,30},{28,20... | collective-permute-start | bytes 884744 | tf_op jit(solution)/shard_map/ppermute | solution.py:976
  102.5 10.7 %collective-permute-start.20 = (bf16[48,1536]{1,0:T(8,128)(2,1)S(1)}, bf16[48,1536]{1,0:T(8,128)(2,1)S(1)}, u32[]{:S(2)}, u32[]{:S(2)}) collective-permute-start(bf16[48,1536]{1,0:T(8,128)(2,1)S(1)} %get-tuple-element.98), channel_id=1, source_target_pairs={{8,0},{10,2},{16,8},{18,10},{24,16},{26,18},{28,24},{30,26},{20,28... | collective-permute-start | bytes 442376 | tf_op jit(solution)/shard_map/ppermute | solution.py:976
  102.6 10.6 %collective-permute-start.21 = (bf16[48,1536]{1,0:T(8,128)(2,1)S(1)}, bf16[48,1536]{1,0:T(8,128)(2,1)S(1)}, u32[]{:S(2)}, u32[]{:S(2)}) collective-permute-start(bf16[48,1536]{1,0:T(8,128)(2,1)S(1)} %get-tuple-element.99), channel_id=1, source_target_pairs={{0,8},{2,10},{8,16},{10,18},{16,24},{18,26},{24,28},{26,30},{28,20... | collective-permute-start | bytes 442376 | tf_op jit(solution)/shard_map/ppermute | solution.py:976
  104.9 10.5 %collective-permute-start.22 = (bf16[96,1536]{1,0:T(8,128)(2,1)S(1)}, bf16[96,1536]{1,0:T(8,128)(2,1)S(1)}, u32[]{:S(2)}, u32[]{:S(2)}) collective-permute-start(bf16[96,1536]{1,0:T(8,128)(2,1)S(1)} %get-tuple-element.132), channel_id=1, source_target_pairs={{0,8},{2,10},{8,16},{10,18},{16,24},{18,26},{24,28},{26,30},{28,20... | collective-permute-start | bytes 884744 | tf_op jit(solution)/shard_map/ppermute | solution.py:976
  112.6 25.7 %collective-permute-start.34 = (bf16[512,768]{1,0:T(8,128)(2,1)S(1)}, bf16[512,768]{1,0:T(8,128)(2,1)S(1)}, u32[]{:S(2)}, u32[]{:S(2)}) collective-permute-start(bf16[512,768]{1,0:T(8,128)(2,1)S(1)} %get-tuple-element.101), channel_id=1, source_target_pairs={{0,1},{1,0},{2,3},{3,2},{4,5},{5,4},{6,7},{7,6},{8,9},{9,8},{10,11... | collective-permute-start | bytes 2359304 | tf_op jit(solution)/shard_map/ppermute | solution.py:785
  113.4 9.2 %collective-permute-start.29 = (bf16[48,1536]{1,0:T(8,128)(2,1)S(1)}, bf16[48,1536]{1,0:T(8,128)(2,1)S(1)}, u32[]{:S(2)}, u32[]{:S(2)}) collective-permute-start(bf16[48,1536]{1,0:T(8,128)(2,1)S(1)} %get-tuple-element.102), channel_id=1, source_target_pairs={{8,0},{10,2},{16,8},{18,10},{24,16},{26,18},{28,24},{30,26},{20,28... | collective-permute-start | bytes 442376 | tf_op jit(solution)/shard_map/ppermute | solution.py:976
  113.8 8.8 %collective-permute-start.30 = (bf16[48,1536]{1,0:T(8,128)(2,1)S(1)}, bf16[48,1536]{1,0:T(8,128)(2,1)S(1)}, u32[]{:S(2)}, u32[]{:S(2)}) collective-permute-start(bf16[48,1536]{1,0:T(8,128)(2,1)S(1)} %get-tuple-element.103), channel_id=1, source_target_pairs={{0,8},{2,10},{8,16},{10,18},{16,24},{18,26},{24,28},{26,30},{28,20... | collective-permute-start | bytes 442376 | tf_op jit(solution)/shard_map/ppermute | solution.py:976
  124.3 11.9 %collective-permute-start.25 = (bf16[96,1536]{1,0:T(8,128)(2,1)S(1)}, bf16[96,1536]{1,0:T(8,128)(2,1)S(1)}, u32[]{:S(2)}, u32[]{:S(2)}) collective-permute-start(bf16[96,1536]{1,0:T(8,128)(2,1)S(1)} %fusion.2), channel_id=1, source_target_pairs={{0,8},{2,10},{8,16},{10,18},{16,24},{18,26},{24,28},{26,30},{28,20... | collective-permute-start | bytes 884744 | tf_op jit(solution)/shard_map/ppermute | solution.py:976
  125.9 11.9 %collective-permute-start.27 = (bf16[96,1536]{1,0:T(8,128)(2,1)S(1)}, bf16[96,1536]{1,0:T(8,128)(2,1)S(1)}, u32[]{:S(2)}, u32[]{:S(2)}) collective-permute-start(bf16[96,1536]{1,0:T(8,128)(2,1)S(1)} %fusion.2), channel_id=1, source_target_pairs={{8,0},{10,2},{16,8},{18,10},{24,16},{26,18},{28,24},{30,26},{20,28... | collective-permute-start | bytes 884744 | tf_op jit(solution)/shard_map/ppermute | solution.py:976
  136.2 10.8 %collective-permute-start.26 = (bf16[96,1536]{1,0:T(8,128)(2,1)S(1)}, bf16[96,1536]{1,0:T(8,128)(2,1)S(1)}, u32[]{:S(2)}, u32[]{:S(2)}) collective-permute-start(bf16[96,1536]{1,0:T(8,128)(2,1)S(1)} %collective-permute-done.25), channel_id=1, source_target_pairs={{0,8},{2,10},{8,16},{10,18},{16,24},{18,26},{24,28},{26,30},{28,20... | collective-permute-start | bytes 884744 | tf_op jit(solution)/shard_map/ppermute | solution.py:976
  137.9 10.9 %collective-permute-start.28 = (bf16[96,1536]{1,0:T(8,128)(2,1)S(1)}, bf16[96,1536]{1,0:T(8,128)(2,1)S(1)}, u32[]{:S(2)}, u32[]{:S(2)}) collective-permute-start(bf16[96,1536]{1,0:T(8,128)(2,1)S(1)} %collective-permute-done.27), channel_id=1, source_target_pairs={{8,0},{10,2},{16,8},{18,10},{24,16},{26,18},{28,24},{30,26},{20,28... | collective-permute-start | bytes 884744 | tf_op jit(solution)/shard_map/ppermute | solution.py:976
  147.0 9.9 %collective-permute-start.41 = (bf16[96,1536]{1,0:T(8,128)(2,1)S(1)}, bf16[96,1536]{1,0:T(8,128)(2,1)S(1)}, u32[]{:S(2)}, u32[]{:S(2)}) collective-permute-start(bf16[96,1536]{1,0:T(8,128)(2,1)S(1)} %collective-permute-done.26), channel_id=1, source_target_pairs={{0,8},{2,10},{8,16},{10,18},{16,24},{18,26},{24,28},{26,30},{28,20... | collective-permute-start | bytes 884744 | tf_op jit(solution)/shard_map/ppermute | solution.py:976
  148.8 10.0 %collective-permute-start.42 = (bf16[96,1536]{1,0:T(8,128)(2,1)S(1)}, bf16[96,1536]{1,0:T(8,128)(2,1)S(1)}, u32[]{:S(2)}, u32[]{:S(2)}) collective-permute-start(bf16[96,1536]{1,0:T(8,128)(2,1)S(1)} %collective-permute-done.28), channel_id=1, source_target_pairs={{8,0},{10,2},{16,8},{18,10},{24,16},{26,18},{28,24},{30,26},{20,28... | collective-permute-start | bytes 884744 | tf_op jit(solution)/shard_map/ppermute | solution.py:976
  150.3 11.7 %collective-permute-start.39 = (bf16[72,1536]{1,0:T(8,128)(2,1)S(1)}, bf16[72,1536]{1,0:T(8,128)(2,1)S(1)}, u32[]{:S(2)}, u32[]{:S(2)}) collective-permute-start(bf16[72,1536]{1,0:T(8,128)(2,1)S(1)} %collective-permute-done.36), channel_id=1, source_target_pairs={{8,0},{10,2},{16,8},{18,10},{24,16},{26,18},{28,24},{30,26},{20,28... | collective-permute-start | bytes 663560 | tf_op jit(solution)/shard_map/ppermute | solution.py:976
  152.3 9.7 %collective-permute-start.40 = (bf16[72,1536]{1,0:T(8,128)(2,1)S(1)}, bf16[72,1536]{1,0:T(8,128)(2,1)S(1)}, u32[]{:S(2)}, u32[]{:S(2)}) collective-permute-start(bf16[72,1536]{1,0:T(8,128)(2,1)S(1)} %collective-permute-done.37), channel_id=1, source_target_pairs={{0,8},{2,10},{8,16},{10,18},{16,24},{18,26},{24,28},{26,30},{28,20... | collective-permute-start | bytes 663560 | tf_op jit(solution)/shard_map/ppermute | solution.py:976
  156.9 12.5 %collective-permute-start.46 = (bf16[96,1536]{1,0:T(8,128)(2,1)S(1)}, bf16[96,1536]{1,0:T(8,128)(2,1)S(1)}, u32[]{:S(2)}, u32[]{:S(2)}) collective-permute-start(bf16[96,1536]{1,0:T(8,128)(2,1)S(1)} %collective-permute-done.41), channel_id=1, source_target_pairs={{0,8},{2,10},{8,16},{10,18},{16,24},{18,26},{24,28},{26,30},{28,20... | collective-permute-start | bytes 884744 | tf_op jit(solution)/shard_map/ppermute | solution.py:976
  (64 other events, 429.6 us)
